TPU v7x, 512 devices: a whole 4x8x8 slice. The times are simulated.
512 devices in a mesh: tm: 64 (over z, y_hi, core), space: 8 (over y_lo, x).
Axes of the slice: x: 4, y: 8 (y_hi: 4, y_lo: 2; y = y_hi * 2 + y_lo), z: 8, core: 2. Of those that a mesh axis runs over, the one named last changes fastest.
Arguments:
- fine_nodes: float32 [64, 3, 3, 64, 16, 128], P('tm', None, None, 'space'), may hold values from -4 to 4
- regions: int32 [64, 16, 128], P('space'), may hold values from 0 to 2
- activity: float32 [64, 16, 128], P('space'), may hold values from 0.3 to 3
- dirichlet: int32 [64, 16, 128], P('space'), may hold values 0 or 1
Outputs:
- next_nodes: float32 [64, 3, 3, 64, 16, 128], P('tm', None, None, 'space')
All inputs are finite; a program needn't handle non-finite values. No bound on the sum of `dirichlet` on one device may be relied on, other than what follows from the above.
Results may differ from a plain program's by a relative error of at most 0.0003.
Values sent between devices are 32-bit elements; how exact they have to be, the bound alone decides.
No kernel may reach another device: no remote copies, remote signals or barrier semaphores. Data moves between devices by JAX's collectives and lax.ppermute only.
A program may use at most 64 MiB of HBM per device.

v0:
```python
import jax
import jax.numpy as jnp
from jax import lax
from jax.sharding import PartitionSpec as P

time_step = 0.05
KAPPA_TABLE = ((1.0, 0.6, 1.4), (0.8, 1.2, 0.5), (0.7, 0.9, 1.1))
RELAX_RATES = (0.5, 1.0, 0.3)
SOURCE_SIGNS = (-1.0, -0.5, 0.25)


def extended(block, sides, width):
    for axis, dim in sides:
        count = lax.axis_size(axis)
        forward = [(i, i + 1) for i in range(count - 1)]
        backward = [(target, source) for source, target in forward]
        low = lax.ppermute(
            lax.slice_in_dim(block, block.shape[dim] - width, None, axis=dim), axis, forward
        )
        high = lax.ppermute(lax.slice_in_dim(block, 0, width, axis=dim), axis, backward)
        block = jnp.concatenate([low, block, high], axis=dim)
    return block


def from_behind(block, axis, distance):
    devices = range(lax.axis_size(axis))
    route = [(i - distance, i) for i in devices if i - distance in devices]
    return lax.ppermute(block, axis, route)


def cell_tables(regions, activity, dirichlet):
    kappa_table = jnp.asarray(KAPPA_TABLE, dtype=jnp.float32)
    conduct = jnp.zeros((3,) + regions.shape, jnp.float32)
    for r in range(3):
        in_region = (regions == r).astype(jnp.float32)
        conduct = conduct + kappa_table[:, r][:, None, None, None] * in_region[None]
    film_act = (regions == 0).astype(jnp.float32) * activity
    mobile = 1.0 - dirichlet.astype(jnp.float32)
    return (conduct, film_act, mobile)


def reaction(u, film_act):
    oxygen = u[..., 0, :, :, :]
    overpot = u[..., 1, :, :, :] - 0.5 * u[..., 2, :, :, :]
    forward = jnp.exp(0.5 * overpot)
    backward = jnp.exp(-0.5 * overpot)
    current = film_act * oxygen * (forward - backward)
    return (current, forward, backward, oxygen)


def sources(u, film_act):
    current = reaction(u, film_act)[0]
    return jnp.stack([SOURCE_SIGNS[k] * current for k in range(3)], axis=-4)


def explicit(u, padded, conduct, film_act, mobile):
    along_x = padded[..., 2:, :, :] + padded[..., :-2, :, :]
    widths_y = [(0, 0)] * (u.ndim - 2) + [(1, 1), (0, 0)]
    pad_y = jnp.pad(u, widths_y)
    along_y = pad_y[..., 2:, :] + pad_y[..., :-2, :]
    widths_z = [(0, 0)] * (u.ndim - 1) + [(1, 1)]
    pad_z = jnp.pad(u, widths_z)
    along_z = pad_z[..., 2:] + pad_z[..., :-2]
    laplace = along_x + along_y + along_z - 6.0 * u
    return mobile * (conduct * laplace + sources(u, film_act))


def restrict(v):
    shape = v.shape
    blocks = v.reshape(shape[:-3] + (shape[-3] // 2, 2, shape[-2] // 2, 2, shape[-1]))
    return 0.25 * jnp.sum(blocks, axis=(-4, -2))


def prolong(v):
    return jnp.repeat(jnp.repeat(v, 2, axis=-3), 2, axis=-2)


def matvec(matrix, v):
    return jnp.sum(matrix * v[None], axis=1)


def slice_work(node_vals, old_padded, padder, conduct, film_act, mobile):
    rates = jnp.asarray(RELAX_RATES, dtype=jnp.float32)[:, None, None, None]
    relax = rates * mobile[None]
    half_step = 0.5 * time_step
    old_expl = explicit(node_vals, old_padded, conduct, film_act, mobile)
    old_force = old_expl - relax * node_vals
    new_zero = node_vals[0]
    quad_one = time_step * (
        5.0 / 24.0 * old_force[0] + 1.0 / 3.0 * old_force[1] - 1.0 / 24.0 * old_force[2]
    )
    new_one = (new_zero + half_step * relax * node_vals[1] + quad_one) / (1.0 + half_step * relax)
    expl_one = explicit(new_one, padder(new_one), conduct, film_act, mobile)
    quad_two = time_step * (
        -1.0 / 24.0 * old_force[0] + 1.0 / 3.0 * old_force[1] + 5.0 / 24.0 * old_force[2]
    )
    new_two = (
        new_one + half_step * (expl_one - old_expl[1]) + half_step * relax * node_vals[2] + quad_two
    ) / (1.0 + half_step * relax)
    expl_two = explicit(new_two, padder(new_two), conduct, film_act, mobile)
    force_one = expl_one - relax * new_one
    force_two = expl_two - relax * new_two
    integral = time_step * (old_force[0] / 6.0 + 2.0 / 3.0 * force_one + force_two / 6.0)
    coarse_zero = restrict(new_zero)
    coarse_one = restrict(new_two)
    cfilm = restrict(film_act)
    cmobile = restrict(mobile)
    crelax = rates * cmobile[None]
    tend_zero = cmobile * sources(coarse_zero, cfilm) - crelax * coarse_zero
    tend_one = cmobile * sources(coarse_one, cfilm) - crelax * coarse_one
    fas_term = restrict(integral) - 0.5 * time_step * (tend_zero + tend_one)
    current, forward, backward, oxygen = reaction(coarse_zero, cfilm)
    derivs = jnp.stack(
        [
            cfilm * (forward - backward),
            cfilm * oxygen * 0.5 * (forward + backward),
            cfilm * oxygen * -0.25 * (forward + backward),
        ],
        axis=0,
    )
    jacobian = jnp.stack([SOURCE_SIGNS[k] * derivs for k in range(3)], axis=0)
    divisor = 1.0 + time_step * crelax
    identity = jnp.eye(3, dtype=jnp.float32)[:, :, None, None, None]
    matrix = (identity + time_step * cmobile * jacobian) / divisor[:, None]
    jac_start = matvec(jacobian, coarse_zero)
    offset = (
        -time_step * cmobile * jac_start
        + time_step * crelax * coarse_one
        + 0.5 * time_step * (tend_zero + tend_one)
        + fas_term
    ) / divisor
    return (jnp.stack([new_zero, new_one, new_two]), coarse_zero, coarse_one, matrix, offset)


def correct(new_vals, coarse_start, coarse_end, coarse_zero, coarse_one):
    delta_zero = coarse_start - coarse_zero
    delta_one = coarse_end - coarse_one
    return jnp.stack(
        [
            new_vals[0] + prolong(delta_zero),
            new_vals[1] + prolong(0.5 * (delta_zero + delta_one)),
            new_vals[2] + prolong(delta_one),
        ]
    )


def face_pad(u):
    return extended(u, (("space", 1),), 1)


def on_device(fine_nodes, regions, activity, dirichlet):
    node_vals = fine_nodes[0]
    conduct, film_act, mobile = cell_tables(regions, activity, dirichlet)
    old_padded = extended(node_vals, (("space", 2),), 1)
    new_vals, coarse_zero, coarse_one, matrix, offset = slice_work(
        node_vals, old_padded, face_pad, conduct, film_act, mobile
    )
    leading = lax.axis_index("tm") == 0

    def relay_round(count, value):
        arrived = from_behind(matvec(matrix, value) + offset, "tm", 1)
        return jnp.where(leading, coarse_zero, arrived)

    coarse_start = lax.fori_loop(0, lax.axis_size("tm") - 1, relay_round, coarse_zero)
    coarse_end = matvec(matrix, coarse_start) + offset
    corrected = correct(new_vals, coarse_start, coarse_end, coarse_zero, coarse_one)
    arrived_end = from_behind(corrected[2], "tm", 1)
    head_node = jnp.where(leading, corrected[0], arrived_end)
    return jnp.stack([head_node, corrected[1], corrected[2]])[None]


def solution(mesh):
    in_specs = (
        P("tm", None, None, "space", None, None),
        P("space", None, None),
        P("space", None, None),
        P("space", None, None),
    )
    out_specs = P("tm", None, None, "space", None, None)
    return jax.shard_map(
        on_device, mesh=mesh, in_specs=in_specs, out_specs=out_specs, check_vma=False
    )
```

profile of v0, /device:TPU:264, one launch (start us, length us, event | category | flops | bytes accessed | tf_op | source)
XLA Modules:
  0.0 659.5 jit_solution(8104112484084561987)
XLA Ops:
  35.0 612.1 %while.10 = (s32[]{:T(128)}, f32[3,4,8,128]{3,2,1,0:T(8,128)S(1)}, pred[]{:T(512)}, f32[3,3,4,8,128]{4,3,2,1,0:T(8,128)S(1)}, f32[3,4,8,128]{3,2,1,0:T(8,128)S(1)}, /*index=5*/f32[3,4,8,128]{3,2,1,0:T(8,128)S(1)}, s32[]{:T(128)}) while((s32[]{:T(128)}, f32[3,4,8,128]{3,2,1,0:T(8,128)S(1)}, pred[]{:T(512)}, f32[3,3,4,8,128]{4,3,2,1,0:T(8,128)S(1)}, ...), condition=%wide.region_8.9_spmd, body=%wide.region_6.8_spmd.sunk | while | flops 86018 | bytes 737398 | solution.py:164
  37.0 8.2 %collective-permute-done = f32[3,4,8,128]{3,2,1,0:T(8,128)S(1)} collective-permute-done((f32[3,4,8,128]{3,2,1,0:T(8,128)S(1)}, f32[3,4,8,128]{3,2,1,0:T(8,128)S(1)}, u32[]{:S(2)}, u32[]{:S(2)}) %collective-permute-start) | collective-permute-done | bytes 49184 | tf_op jit(solution)/shard_map/while/body/eval_jaxpr/ppermute | solution.py:28
  47.2 8.1 %collective-permute-done = f32[3,4,8,128]{3,2,1,0:T(8,128)S(1)} collective-permute-done((f32[3,4,8,128]{3,2,1,0:T(8,128)S(1)}, f32[3,4,8,128]{3,2,1,0:T(8,128)S(1)}, u32[]{:S(2)}, u32[]{:S(2)}) %collective-permute-start) | collective-permute-done | bytes 49184 | tf_op jit(solution)/shard_map/while/body/eval_jaxpr/ppermute | solution.py:28
  57.4 7.7 %collective-permute-done = f32[3,4,8,128]{3,2,1,0:T(8,128)S(1)} collective-permute-done((f32[3,4,8,128]{3,2,1,0:T(8,128)S(1)}, f32[3,4,8,128]{3,2,1,0:T(8,128)S(1)}, u32[]{:S(2)}, u32[]{:S(2)}) %collective-permute-start) | collective-permute-done | bytes 49184 | tf_op jit(solution)/shard_map/while/body/eval_jaxpr/ppermute | solution.py:28
  67.1 7.7 %collective-permute-done = f32[3,4,8,128]{3,2,1,0:T(8,128)S(1)} collective-permute-done((f32[3,4,8,128]{3,2,1,0:T(8,128)S(1)}, f32[3,4,8,128]{3,2,1,0:T(8,128)S(1)}, u32[]{:S(2)}, u32[]{:S(2)}) %collective-permute-start) | collective-permute-done | bytes 49184 | tf_op jit(solution)/shard_map/while/body/eval_jaxpr/ppermute | solution.py:28
  76.8 7.7 %collective-permute-done = f32[3,4,8,128]{3,2,1,0:T(8,128)S(1)} collective-permute-done((f32[3,4,8,128]{3,2,1,0:T(8,128)S(1)}, f32[3,4,8,128]{3,2,1,0:T(8,128)S(1)}, u32[]{:S(2)}, u32[]{:S(2)}) %collective-permute-start) | collective-permute-done | bytes 49184 | tf_op jit(solution)/shard_map/while/body/eval_jaxpr/ppermute | solution.py:28
  86.5 7.8 %collective-permute-done = f32[3,4,8,128]{3,2,1,0:T(8,128)S(1)} collective-permute-done((f32[3,4,8,128]{3,2,1,0:T(8,128)S(1)}, f32[3,4,8,128]{3,2,1,0:T(8,128)S(1)}, u32[]{:S(2)}, u32[]{:S(2)}) %collective-permute-start) | collective-permute-done | bytes 49184 | tf_op jit(solution)/shard_map/while/body/eval_jaxpr/ppermute | solution.py:28
  96.3 7.7 %collective-permute-done = f32[3,4,8,128]{3,2,1,0:T(8,128)S(1)} collective-permute-done((f32[3,4,8,128]{3,2,1,0:T(8,128)S(1)}, f32[3,4,8,128]{3,2,1,0:T(8,128)S(1)}, u32[]{:S(2)}, u32[]{:S(2)}) %collective-permute-start) | collective-permute-done | bytes 49184 | tf_op jit(solution)/shard_map/while/body/eval_jaxpr/ppermute | solution.py:28
  106.0 7.7 %collective-permute-done = f32[3,4,8,128]{3,2,1,0:T(8,128)S(1)} collective-permute-done((f32[3,4,8,128]{3,2,1,0:T(8,128)S(1)}, f32[3,4,8,128]{3,2,1,0:T(8,128)S(1)}, u32[]{:S(2)}, u32[]{:S(2)}) %collective-permute-start) | collective-permute-done | bytes 49184 | tf_op jit(solution)/shard_map/while/body/eval_jaxpr/ppermute | solution.py:28
  115.7 7.7 %collective-permute-done = f32[3,4,8,128]{3,2,1,0:T(8,128)S(1)} collective-permute-done((f32[3,4,8,128]{3,2,1,0:T(8,128)S(1)}, f32[3,4,8,128]{3,2,1,0:T(8,128)S(1)}, u32[]{:S(2)}, u32[]{:S(2)}) %collective-permute-start) | collective-permute-done | bytes 49184 | tf_op jit(solution)/shard_map/while/body/eval_jaxpr/ppermute | solution.py:28
  125.4 7.7 %collective-permute-done = f32[3,4,8,128]{3,2,1,0:T(8,128)S(1)} collective-permute-done((f32[3,4,8,128]{3,2,1,0:T(8,128)S(1)}, f32[3,4,8,128]{3,2,1,0:T(8,128)S(1)}, u32[]{:S(2)}, u32[]{:S(2)}) %collective-permute-start) | collective-permute-done | bytes 49184 | tf_op jit(solution)/shard_map/while/body/eval_jaxpr/ppermute | solution.py:28
  135.1 7.7 %collective-permute-done = f32[3,4,8,128]{3,2,1,0:T(8,128)S(1)} collective-permute-done((f32[3,4,8,128]{3,2,1,0:T(8,128)S(1)}, f32[3,4,8,128]{3,2,1,0:T(8,128)S(1)}, u32[]{:S(2)}, u32[]{:S(2)}) %collective-permute-start) | collective-permute-done | bytes 49184 | tf_op jit(solution)/shard_map/while/body/eval_jaxpr/ppermute | solution.py:28
  164.2 7.7 %collective-permute-done = f32[3,4,8,128]{3,2,1,0:T(8,128)S(1)} collective-permute-done((f32[3,4,8,128]{3,2,1,0:T(8,128)S(1)}, f32[3,4,8,128]{3,2,1,0:T(8,128)S(1)}, u32[]{:S(2)}, u32[]{:S(2)}) %collective-permute-start) | collective-permute-done | bytes 49184 | tf_op jit(solution)/shard_map/while/body/eval_jaxpr/ppermute | solution.py:28
  173.9 7.7 %collective-permute-done = f32[3,4,8,128]{3,2,1,0:T(8,128)S(1)} collective-permute-done((f32[3,4,8,128]{3,2,1,0:T(8,128)S(1)}, f32[3,4,8,128]{3,2,1,0:T(8,128)S(1)}, u32[]{:S(2)}, u32[]{:S(2)}) %collective-permute-start) | collective-permute-done | bytes 49184 | tf_op jit(solution)/shard_map/while/body/eval_jaxpr/ppermute | solution.py:28
  183.6 7.7 %collective-permute-done = f32[3,4,8,128]{3,2,1,0:T(8,128)S(1)} collective-permute-done((f32[3,4,8,128]{3,2,1,0:T(8,128)S(1)}, f32[3,4,8,128]{3,2,1,0:T(8,128)S(1)}, u32[]{:S(2)}, u32[]{:S(2)}) %collective-permute-start) | collective-permute-done | bytes 49184 | tf_op jit(solution)/shard_map/while/body/eval_jaxpr/ppermute | solution.py:28
  193.3 7.7 %collective-permute-done = f32[3,4,8,128]{3,2,1,0:T(8,128)S(1)} collective-permute-done((f32[3,4,8,128]{3,2,1,0:T(8,128)S(1)}, f32[3,4,8,128]{3,2,1,0:T(8,128)S(1)}, u32[]{:S(2)}, u32[]{:S(2)}) %collective-permute-start) | collective-permute-done | bytes 49184 | tf_op jit(solution)/shard_map/while/body/eval_jaxpr/ppermute | solution.py:28
  203.0 7.7 %collective-permute-done = f32[3,4,8,128]{3,2,1,0:T(8,128)S(1)} collective-permute-done((f32[3,4,8,128]{3,2,1,0:T(8,128)S(1)}, f32[3,4,8,128]{3,2,1,0:T(8,128)S(1)}, u32[]{:S(2)}, u32[]{:S(2)}) %collective-permute-start) | collective-permute-done | bytes 49184 | tf_op jit(solution)/shard_map/while/body/eval_jaxpr/ppermute | solution.py:28
  212.7 7.7 %collective-permute-done = f32[3,4,8,128]{3,2,1,0:T(8,128)S(1)} collective-permute-done((f32[3,4,8,128]{3,2,1,0:T(8,128)S(1)}, f32[3,4,8,128]{3,2,1,0:T(8,128)S(1)}, u32[]{:S(2)}, u32[]{:S(2)}) %collective-permute-start) | collective-permute-done | bytes 49184 | tf_op jit(solution)/shard_map/while/body/eval_jaxpr/ppermute | solution.py:28
  222.4 7.7 %collective-permute-done = f32[3,4,8,128]{3,2,1,0:T(8,128)S(1)} collective-permute-done((f32[3,4,8,128]{3,2,1,0:T(8,128)S(1)}, f32[3,4,8,128]{3,2,1,0:T(8,128)S(1)}, u32[]{:S(2)}, u32[]{:S(2)}) %collective-permute-start) | collective-permute-done | bytes 49184 | tf_op jit(solution)/shard_map/while/body/eval_jaxpr/ppermute | solution.py:28
  261.2 7.7 %collective-permute-done = f32[3,4,8,128]{3,2,1,0:T(8,128)S(1)} collective-permute-done((f32[3,4,8,128]{3,2,1,0:T(8,128)S(1)}, f32[3,4,8,128]{3,2,1,0:T(8,128)S(1)}, u32[]{:S(2)}, u32[]{:S(2)}) %collective-permute-start) | collective-permute-done | bytes 49184 | tf_op jit(solution)/shard_map/while/body/eval_jaxpr/ppermute | solution.py:28
  270.9 7.7 %collective-permute-done = f32[3,4,8,128]{3,2,1,0:T(8,128)S(1)} collective-permute-done((f32[3,4,8,128]{3,2,1,0:T(8,128)S(1)}, f32[3,4,8,128]{3,2,1,0:T(8,128)S(1)}, u32[]{:S(2)}, u32[]{:S(2)}) %collective-permute-start) | collective-permute-done | bytes 49184 | tf_op jit(solution)/shard_map/while/body/eval_jaxpr/ppermute | solution.py:28
  280.6 7.7 %collective-permute-done = f32[3,4,8,128]{3,2,1,0:T(8,128)S(1)} collective-permute-done((f32[3,4,8,128]{3,2,1,0:T(8,128)S(1)}, f32[3,4,8,128]{3,2,1,0:T(8,128)S(1)}, u32[]{:S(2)}, u32[]{:S(2)}) %collective-permute-start) | collective-permute-done | bytes 49184 | tf_op jit(solution)/shard_map/while/body/eval_jaxpr/ppermute | solution.py:28
  290.3 7.7 %collective-permute-done = f32[3,4,8,128]{3,2,1,0:T(8,128)S(1)} collective-permute-done((f32[3,4,8,128]{3,2,1,0:T(8,128)S(1)}, f32[3,4,8,128]{3,2,1,0:T(8,128)S(1)}, u32[]{:S(2)}, u32[]{:S(2)}) %collective-permute-start) | collective-permute-done | bytes 49184 | tf_op jit(solution)/shard_map/while/body/eval_jaxpr/ppermute | solution.py:28
  300.0 7.7 %collective-permute-done = f32[3,4,8,128]{3,2,1,0:T(8,128)S(1)} collective-permute-done((f32[3,4,8,128]{3,2,1,0:T(8,128)S(1)}, f32[3,4,8,128]{3,2,1,0:T(8,128)S(1)}, u32[]{:S(2)}, u32[]{:S(2)}) %collective-permute-start) | collective-permute-done | bytes 49184 | tf_op jit(solution)/shard_map/while/body/eval_jaxpr/ppermute | solution.py:28
  309.7 7.7 %collective-permute-done = f32[3,4,8,128]{3,2,1,0:T(8,128)S(1)} collective-permute-done((f32[3,4,8,128]{3,2,1,0:T(8,128)S(1)}, f32[3,4,8,128]{3,2,1,0:T(8,128)S(1)}, u32[]{:S(2)}, u32[]{:S(2)}) %collective-permute-start) | collective-permute-done | bytes 49184 | tf_op jit(solution)/shard_map/while/body/eval_jaxpr/ppermute | solution.py:28
  348.5 7.7 %collective-permute-done = f32[3,4,8,128]{3,2,1,0:T(8,128)S(1)} collective-permute-done((f32[3,4,8,128]{3,2,1,0:T(8,128)S(1)}, f32[3,4,8,128]{3,2,1,0:T(8,128)S(1)}, u32[]{:S(2)}, u32[]{:S(2)}) %collective-permute-start) | collective-permute-done | bytes 49184 | tf_op jit(solution)/shard_map/while/body/eval_jaxpr/ppermute | solution.py:28
  358.2 7.7 %collective-permute-done = f32[3,4,8,128]{3,2,1,0:T(8,128)S(1)} collective-permute-done((f32[3,4,8,128]{3,2,1,0:T(8,128)S(1)}, f32[3,4,8,128]{3,2,1,0:T(8,128)S(1)}, u32[]{:S(2)}, u32[]{:S(2)}) %collective-permute-start) | collective-permute-done | bytes 49184 | tf_op jit(solution)/shard_map/while/body/eval_jaxpr/ppermute | solution.py:28
  367.9 7.7 %collective-permute-done = f32[3,4,8,128]{3,2,1,0:T(8,128)S(1)} collective-permute-done((f32[3,4,8,128]{3,2,1,0:T(8,128)S(1)}, f32[3,4,8,128]{3,2,1,0:T(8,128)S(1)}, u32[]{:S(2)}, u32[]{:S(2)}) %collective-permute-start) | collective-permute-done | bytes 49184 | tf_op jit(solution)/shard_map/while/body/eval_jaxpr/ppermute | solution.py:28
  377.5 7.7 %collective-permute-done = f32[3,4,8,128]{3,2,1,0:T(8,128)S(1)} collective-permute-done((f32[3,4,8,128]{3,2,1,0:T(8,128)S(1)}, f32[3,4,8,128]{3,2,1,0:T(8,128)S(1)}, u32[]{:S(2)}, u32[]{:S(2)}) %collective-permute-start) | collective-permute-done | bytes 49184 | tf_op jit(solution)/shard_map/while/body/eval_jaxpr/ppermute | solution.py:28
  387.2 7.7 %collective-permute-done = f32[3,4,8,128]{3,2,1,0:T(8,128)S(1)} collective-permute-done((f32[3,4,8,128]{3,2,1,0:T(8,128)S(1)}, f32[3,4,8,128]{3,2,1,0:T(8,128)S(1)}, u32[]{:S(2)}, u32[]{:S(2)}) %collective-permute-start) | collective-permute-done | bytes 49184 | tf_op jit(solution)/shard_map/while/body/eval_jaxpr/ppermute | solution.py:28
  396.9 7.7 %collective-permute-done = f32[3,4,8,128]{3,2,1,0:T(8,128)S(1)} collective-permute-done((f32[3,4,8,128]{3,2,1,0:T(8,128)S(1)}, f32[3,4,8,128]{3,2,1,0:T(8,128)S(1)}, u32[]{:S(2)}, u32[]{:S(2)}) %collective-permute-start) | collective-permute-done | bytes 49184 | tf_op jit(solution)/shard_map/while/body/eval_jaxpr/ppermute | solution.py:28
  406.6 7.7 %collective-permute-done = f32[3,4,8,128]{3,2,1,0:T(8,128)S(1)} collective-permute-done((f32[3,4,8,128]{3,2,1,0:T(8,128)S(1)}, f32[3,4,8,128]{3,2,1,0:T(8,128)S(1)}, u32[]{:S(2)}, u32[]{:S(2)}) %collective-permute-start) | collective-permute-done | bytes 49184 | tf_op jit(solution)/shard_map/while/body/eval_jaxpr/ppermute | solution.py:28
  445.4 7.7 %collective-permute-done = f32[3,4,8,128]{3,2,1,0:T(8,128)S(1)} collective-permute-done((f32[3,4,8,128]{3,2,1,0:T(8,128)S(1)}, f32[3,4,8,128]{3,2,1,0:T(8,128)S(1)}, u32[]{:S(2)}, u32[]{:S(2)}) %collective-permute-start) | collective-permute-done | bytes 49184 | tf_op jit(solution)/shard_map/while/body/eval_jaxpr/ppermute | solution.py:28
  455.1 7.7 %collective-permute-done = f32[3,4,8,128]{3,2,1,0:T(8,128)S(1)} collective-permute-done((f32[3,4,8,128]{3,2,1,0:T(8,128)S(1)}, f32[3,4,8,128]{3,2,1,0:T(8,128)S(1)}, u32[]{:S(2)}, u32[]{:S(2)}) %collective-permute-start) | collective-permute-done | bytes 49184 | tf_op jit(solution)/shard_map/while/body/eval_jaxpr/ppermute | solution.py:28
  464.8 7.7 %collective-permute-done = f32[3,4,8,128]{3,2,1,0:T(8,128)S(1)} collective-permute-done((f32[3,4,8,128]{3,2,1,0:T(8,128)S(1)}, f32[3,4,8,128]{3,2,1,0:T(8,128)S(1)}, u32[]{:S(2)}, u32[]{:S(2)}) %collective-permute-start) | collective-permute-done | bytes 49184 | tf_op jit(solution)/shard_map/while/body/eval_jaxpr/ppermute | solution.py:28
  474.5 7.7 %collective-permute-done = f32[3,4,8,128]{3,2,1,0:T(8,128)S(1)} collective-permute-done((f32[3,4,8,128]{3,2,1,0:T(8,128)S(1)}, f32[3,4,8,128]{3,2,1,0:T(8,128)S(1)}, u32[]{:S(2)}, u32[]{:S(2)}) %collective-permute-start) | collective-permute-done | bytes 49184 | tf_op jit(solution)/shard_map/while/body/eval_jaxpr/ppermute | solution.py:28
  484.2 7.7 %collective-permute-done = f32[3,4,8,128]{3,2,1,0:T(8,128)S(1)} collective-permute-done((f32[3,4,8,128]{3,2,1,0:T(8,128)S(1)}, f32[3,4,8,128]{3,2,1,0:T(8,128)S(1)}, u32[]{:S(2)}, u32[]{:S(2)}) %collective-permute-start) | collective-permute-done | bytes 49184 | tf_op jit(solution)/shard_map/while/body/eval_jaxpr/ppermute | solution.py:28
  493.9 7.7 %collective-permute-done = f32[3,4,8,128]{3,2,1,0:T(8,128)S(1)} collective-permute-done((f32[3,4,8,128]{3,2,1,0:T(8,128)S(1)}, f32[3,4,8,128]{3,2,1,0:T(8,128)S(1)}, u32[]{:S(2)}, u32[]{:S(2)}) %collective-permute-start) | collective-permute-done | bytes 49184 | tf_op jit(solution)/shard_map/while/body/eval_jaxpr/ppermute | solution.py:28
  532.7 7.7 %collective-permute-done = f32[3,4,8,128]{3,2,1,0:T(8,128)S(1)} collective-permute-done((f32[3,4,8,128]{3,2,1,0:T(8,128)S(1)}, f32[3,4,8,128]{3,2,1,0:T(8,128)S(1)}, u32[]{:S(2)}, u32[]{:S(2)}) %collective-permute-start) | collective-permute-done | bytes 49184 | tf_op jit(solution)/shard_map/while/body/eval_jaxpr/ppermute | solution.py:28
  542.4 7.7 %collective-permute-done = f32[3,4,8,128]{3,2,1,0:T(8,128)S(1)} collective-permute-done((f32[3,4,8,128]{3,2,1,0:T(8,128)S(1)}, f32[3,4,8,128]{3,2,1,0:T(8,128)S(1)}, u32[]{:S(2)}, u32[]{:S(2)}) %collective-permute-start) | collective-permute-done | bytes 49184 | tf_op jit(solution)/shard_map/while/body/eval_jaxpr/ppermute | solution.py:28
  552.1 7.7 %collective-permute-done = f32[3,4,8,128]{3,2,1,0:T(8,128)S(1)} collective-permute-done((f32[3,4,8,128]{3,2,1,0:T(8,128)S(1)}, f32[3,4,8,128]{3,2,1,0:T(8,128)S(1)}, u32[]{:S(2)}, u32[]{:S(2)}) %collective-permute-start) | collective-permute-done | bytes 49184 | tf_op jit(solution)/shard_map/while/body/eval_jaxpr/ppermute | solution.py:28
  561.8 7.7 %collective-permute-done = f32[3,4,8,128]{3,2,1,0:T(8,128)S(1)} collective-permute-done((f32[3,4,8,128]{3,2,1,0:T(8,128)S(1)}, f32[3,4,8,128]{3,2,1,0:T(8,128)S(1)}, u32[]{:S(2)}, u32[]{:S(2)}) %collective-permute-start) | collective-permute-done | bytes 49184 | tf_op jit(solution)/shard_map/while/body/eval_jaxpr/ppermute | solution.py:28
  571.5 7.7 %collective-permute-done = f32[3,4,8,128]{3,2,1,0:T(8,128)S(1)} collective-permute-done((f32[3,4,8,128]{3,2,1,0:T(8,128)S(1)}, f32[3,4,8,128]{3,2,1,0:T(8,128)S(1)}, u32[]{:S(2)}, u32[]{:S(2)}) %collective-permute-start) | collective-permute-done | bytes 49184 | tf_op jit(solution)/shard_map/while/body/eval_jaxpr/ppermute | solution.py:28
  581.2 7.7 %collective-permute-done = f32[3,4,8,128]{3,2,1,0:T(8,128)S(1)} collective-permute-done((f32[3,4,8,128]{3,2,1,0:T(8,128)S(1)}, f32[3,4,8,128]{3,2,1,0:T(8,128)S(1)}, u32[]{:S(2)}, u32[]{:S(2)}) %collective-permute-start) | collective-permute-done | bytes 49184 | tf_op jit(solution)/shard_map/while/body/eval_jaxpr/ppermute | solution.py:28
  590.9 7.7 %collective-permute-done = f32[3,4,8,128]{3,2,1,0:T(8,128)S(1)} collective-permute-done((f32[3,4,8,128]{3,2,1,0:T(8,128)S(1)}, f32[3,4,8,128]{3,2,1,0:T(8,128)S(1)}, u32[]{:S(2)}, u32[]{:S(2)}) %collective-permute-start) | collective-permute-done | bytes 49184 | tf_op jit(solution)/shard_map/while/body/eval_jaxpr/ppermute | solution.py:28
  629.7 7.7 %collective-permute-done = f32[3,4,8,128]{3,2,1,0:T(8,128)S(1)} collective-permute-done((f32[3,4,8,128]{3,2,1,0:T(8,128)S(1)}, f32[3,4,8,128]{3,2,1,0:T(8,128)S(1)}, u32[]{:S(2)}, u32[]{:S(2)}) %collective-permute-start) | collective-permute-done | bytes 49184 | tf_op jit(solution)/shard_map/while/body/eval_jaxpr/ppermute | solution.py:28
  639.4 7.8 %collective-permute-done = f32[3,4,8,128]{3,2,1,0:T(8,128)S(1)} collective-permute-done((f32[3,4,8,128]{3,2,1,0:T(8,128)S(1)}, f32[3,4,8,128]{3,2,1,0:T(8,128)S(1)}, u32[]{:S(2)}, u32[]{:S(2)}) %collective-permute-start) | collective-permute-done | bytes 49184 | tf_op jit(solution)/shard_map/while/body/eval_jaxpr/ppermute | solution.py:28
  649.5 9.0 %collective-permute-done.7 = f32[3,8,16,128]{3,2,1,0:T(8,128)S(1)} collective-permute-done((f32[3,8,16,128]{3,2,1,0:T(8,128)S(1)}, f32[3,8,16,128]{3,2,1,0:T(8,128)S(1)}, u32[]{:S(2)}, u32[]{:S(2)}) %collective-permute-start.7) | collective-permute-done | bytes 196640 | tf_op jit(solution)/shard_map/ppermute | solution.py:28
  (345 shorter events, 292.0 us)
Async XLA Ops:
  35.1 10.2 %collective-permute-start = (f32[3,4,8,128]{3,2,1,0:T(8,128)S(1)}, f32[3,4,8,128]{3,2,1,0:T(8,128)S(1)}, u32[]{:S(2)}, u32[]{:S(2)}) collective-permute-start(f32[3,4,8,128]{3,2,1,0:T(8,128)S(1)} %add.501), channel_id=1, source_target_pairs={{0,8},{8,16},{16,24},{24,32},{32,40},{40,48},{48,56},{56,64},{64,7... | collective-permute-start | bytes 147464 | tf_op jit(solution)/shard_map/while/body/eval_jaxpr/ppermute | solution.py:28
  45.3 10.1 %collective-permute-start = (f32[3,4,8,128]{3,2,1,0:T(8,128)S(1)}, f32[3,4,8,128]{3,2,1,0:T(8,128)S(1)}, u32[]{:S(2)}, u32[]{:S(2)}) collective-permute-start(f32[3,4,8,128]{3,2,1,0:T(8,128)S(1)} %add.501), channel_id=1, source_target_pairs={{0,8},{8,16},{16,24},{24,32},{32,40},{40,48},{48,56},{56,64},{64,7... | collective-permute-start | bytes 147464 | tf_op jit(solution)/shard_map/while/body/eval_jaxpr/ppermute | solution.py:28
  55.4 9.7 %collective-permute-start = (f32[3,4,8,128]{3,2,1,0:T(8,128)S(1)}, f32[3,4,8,128]{3,2,1,0:T(8,128)S(1)}, u32[]{:S(2)}, u32[]{:S(2)}) collective-permute-start(f32[3,4,8,128]{3,2,1,0:T(8,128)S(1)} %add.501), channel_id=1, source_target_pairs={{0,8},{8,16},{16,24},{24,32},{32,40},{40,48},{48,56},{56,64},{64,7... | collective-permute-start | bytes 147464 | tf_op jit(solution)/shard_map/while/body/eval_jaxpr/ppermute | solution.py:28
  65.2 9.6 %collective-permute-start = (f32[3,4,8,128]{3,2,1,0:T(8,128)S(1)}, f32[3,4,8,128]{3,2,1,0:T(8,128)S(1)}, u32[]{:S(2)}, u32[]{:S(2)}) collective-permute-start(f32[3,4,8,128]{3,2,1,0:T(8,128)S(1)} %add.501), channel_id=1, source_target_pairs={{0,8},{8,16},{16,24},{24,32},{32,40},{40,48},{48,56},{56,64},{64,7... | collective-permute-start | bytes 147464 | tf_op jit(solution)/shard_map/while/body/eval_jaxpr/ppermute | solution.py:28
  74.9 9.6 %collective-permute-start = (f32[3,4,8,128]{3,2,1,0:T(8,128)S(1)}, f32[3,4,8,128]{3,2,1,0:T(8,128)S(1)}, u32[]{:S(2)}, u32[]{:S(2)}) collective-permute-start(f32[3,4,8,128]{3,2,1,0:T(8,128)S(1)} %add.501), channel_id=1, source_target_pairs={{0,8},{8,16},{16,24},{24,32},{32,40},{40,48},{48,56},{56,64},{64,7... | collective-permute-start | bytes 147464 | tf_op jit(solution)/shard_map/while/body/eval_jaxpr/ppermute | solution.py:28
  84.6 9.7 %collective-permute-start = (f32[3,4,8,128]{3,2,1,0:T(8,128)S(1)}, f32[3,4,8,128]{3,2,1,0:T(8,128)S(1)}, u32[]{:S(2)}, u32[]{:S(2)}) collective-permute-start(f32[3,4,8,128]{3,2,1,0:T(8,128)S(1)} %add.501), channel_id=1, source_target_pairs={{0,8},{8,16},{16,24},{24,32},{32,40},{40,48},{48,56},{56,64},{64,7... | collective-permute-start | bytes 147464 | tf_op jit(solution)/shard_map/while/body/eval_jaxpr/ppermute | solution.py:28
  94.4 9.6 %collective-permute-start = (f32[3,4,8,128]{3,2,1,0:T(8,128)S(1)}, f32[3,4,8,128]{3,2,1,0:T(8,128)S(1)}, u32[]{:S(2)}, u32[]{:S(2)}) collective-permute-start(f32[3,4,8,128]{3,2,1,0:T(8,128)S(1)} %add.501), channel_id=1, source_target_pairs={{0,8},{8,16},{16,24},{24,32},{32,40},{40,48},{48,56},{56,64},{64,7... | collective-permute-start | bytes 147464 | tf_op jit(solution)/shard_map/while/body/eval_jaxpr/ppermute | solution.py:28
  104.1 9.6 %collective-permute-start = (f32[3,4,8,128]{3,2,1,0:T(8,128)S(1)}, f32[3,4,8,128]{3,2,1,0:T(8,128)S(1)}, u32[]{:S(2)}, u32[]{:S(2)}) collective-permute-start(f32[3,4,8,128]{3,2,1,0:T(8,128)S(1)} %add.501), channel_id=1, source_target_pairs={{0,8},{8,16},{16,24},{24,32},{32,40},{40,48},{48,56},{56,64},{64,7... | collective-permute-start | bytes 147464 | tf_op jit(solution)/shard_map/while/body/eval_jaxpr/ppermute | solution.py:28
  113.8 9.6 %collective-permute-start = (f32[3,4,8,128]{3,2,1,0:T(8,128)S(1)}, f32[3,4,8,128]{3,2,1,0:T(8,128)S(1)}, u32[]{:S(2)}, u32[]{:S(2)}) collective-permute-start(f32[3,4,8,128]{3,2,1,0:T(8,128)S(1)} %add.501), channel_id=1, source_target_pairs={{0,8},{8,16},{16,24},{24,32},{32,40},{40,48},{48,56},{56,64},{64,7... | collective-permute-start | bytes 147464 | tf_op jit(solution)/shard_map/while/body/eval_jaxpr/ppermute | solution.py:28
  123.5 9.6 %collective-permute-start = (f32[3,4,8,128]{3,2,1,0:T(8,128)S(1)}, f32[3,4,8,128]{3,2,1,0:T(8,128)S(1)}, u32[]{:S(2)}, u32[]{:S(2)}) collective-permute-start(f32[3,4,8,128]{3,2,1,0:T(8,128)S(1)} %add.501), channel_id=1, source_target_pairs={{0,8},{8,16},{16,24},{24,32},{32,40},{40,48},{48,56},{56,64},{64,7... | collective-permute-start | bytes 147464 | tf_op jit(solution)/shard_map/while/body/eval_jaxpr/ppermute | solution.py:28
  133.2 9.6 %collective-permute-start = (f32[3,4,8,128]{3,2,1,0:T(8,128)S(1)}, f32[3,4,8,128]{3,2,1,0:T(8,128)S(1)}, u32[]{:S(2)}, u32[]{:S(2)}) collective-permute-start(f32[3,4,8,128]{3,2,1,0:T(8,128)S(1)} %add.501), channel_id=1, source_target_pairs={{0,8},{8,16},{16,24},{24,32},{32,40},{40,48},{48,56},{56,64},{64,7... | collective-permute-start | bytes 147464 | tf_op jit(solution)/shard_map/while/body/eval_jaxpr/ppermute | solution.py:28
  162.3 9.6 %collective-permute-start = (f32[3,4,8,128]{3,2,1,0:T(8,128)S(1)}, f32[3,4,8,128]{3,2,1,0:T(8,128)S(1)}, u32[]{:S(2)}, u32[]{:S(2)}) collective-permute-start(f32[3,4,8,128]{3,2,1,0:T(8,128)S(1)} %add.501), channel_id=1, source_target_pairs={{0,8},{8,16},{16,24},{24,32},{32,40},{40,48},{48,56},{56,64},{64,7... | collective-permute-start | bytes 147464 | tf_op jit(solution)/shard_map/while/body/eval_jaxpr/ppermute | solution.py:28
  172.0 9.6 %collective-permute-start = (f32[3,4,8,128]{3,2,1,0:T(8,128)S(1)}, f32[3,4,8,128]{3,2,1,0:T(8,128)S(1)}, u32[]{:S(2)}, u32[]{:S(2)}) collective-permute-start(f32[3,4,8,128]{3,2,1,0:T(8,128)S(1)} %add.501), channel_id=1, source_target_pairs={{0,8},{8,16},{16,24},{24,32},{32,40},{40,48},{48,56},{56,64},{64,7... | collective-permute-start | bytes 147464 | tf_op jit(solution)/shard_map/while/body/eval_jaxpr/ppermute | solution.py:28
  181.7 9.6 %collective-permute-start = (f32[3,4,8,128]{3,2,1,0:T(8,128)S(1)}, f32[3,4,8,128]{3,2,1,0:T(8,128)S(1)}, u32[]{:S(2)}, u32[]{:S(2)}) collective-permute-start(f32[3,4,8,128]{3,2,1,0:T(8,128)S(1)} %add.501), channel_id=1, source_target_pairs={{0,8},{8,16},{16,24},{24,32},{32,40},{40,48},{48,56},{56,64},{64,7... | collective-permute-start | bytes 147464 | tf_op jit(solution)/shard_map/while/body/eval_jaxpr/ppermute | solution.py:28
  191.4 9.6 %collective-permute-start = (f32[3,4,8,128]{3,2,1,0:T(8,128)S(1)}, f32[3,4,8,128]{3,2,1,0:T(8,128)S(1)}, u32[]{:S(2)}, u32[]{:S(2)}) collective-permute-start(f32[3,4,8,128]{3,2,1,0:T(8,128)S(1)} %add.501), channel_id=1, source_target_pairs={{0,8},{8,16},{16,24},{24,32},{32,40},{40,48},{48,56},{56,64},{64,7... | collective-permute-start | bytes 147464 | tf_op jit(solution)/shard_map/while/body/eval_jaxpr/ppermute | solution.py:28
  201.1 9.6 %collective-permute-start = (f32[3,4,8,128]{3,2,1,0:T(8,128)S(1)}, f32[3,4,8,128]{3,2,1,0:T(8,128)S(1)}, u32[]{:S(2)}, u32[]{:S(2)}) collective-permute-start(f32[3,4,8,128]{3,2,1,0:T(8,128)S(1)} %add.501), channel_id=1, source_target_pairs={{0,8},{8,16},{16,24},{24,32},{32,40},{40,48},{48,56},{56,64},{64,7... | collective-permute-start | bytes 147464 | tf_op jit(solution)/shard_map/while/body/eval_jaxpr/ppermute | solution.py:28
  210.8 9.6 %collective-permute-start = (f32[3,4,8,128]{3,2,1,0:T(8,128)S(1)}, f32[3,4,8,128]{3,2,1,0:T(8,128)S(1)}, u32[]{:S(2)}, u32[]{:S(2)}) collective-permute-start(f32[3,4,8,128]{3,2,1,0:T(8,128)S(1)} %add.501), channel_id=1, source_target_pairs={{0,8},{8,16},{16,24},{24,32},{32,40},{40,48},{48,56},{56,64},{64,7... | collective-permute-start | bytes 147464 | tf_op jit(solution)/shard_map/while/body/eval_jaxpr/ppermute | solution.py:28
  220.5 9.6 %collective-permute-start = (f32[3,4,8,128]{3,2,1,0:T(8,128)S(1)}, f32[3,4,8,128]{3,2,1,0:T(8,128)S(1)}, u32[]{:S(2)}, u32[]{:S(2)}) collective-permute-start(f32[3,4,8,128]{3,2,1,0:T(8,128)S(1)} %add.501), channel_id=1, source_target_pairs={{0,8},{8,16},{16,24},{24,32},{32,40},{40,48},{48,56},{56,64},{64,7... | collective-permute-start | bytes 147464 | tf_op jit(solution)/shard_map/while/body/eval_jaxpr/ppermute | solution.py:28
  259.3 9.6 %collective-permute-start = (f32[3,4,8,128]{3,2,1,0:T(8,128)S(1)}, f32[3,4,8,128]{3,2,1,0:T(8,128)S(1)}, u32[]{:S(2)}, u32[]{:S(2)}) collective-permute-start(f32[3,4,8,128]{3,2,1,0:T(8,128)S(1)} %add.501), channel_id=1, source_target_pairs={{0,8},{8,16},{16,24},{24,32},{32,40},{40,48},{48,56},{56,64},{64,7... | collective-permute-start | bytes 147464 | tf_op jit(solution)/shard_map/while/body/eval_jaxpr/ppermute | solution.py:28
  269.0 9.6 %collective-permute-start = (f32[3,4,8,128]{3,2,1,0:T(8,128)S(1)}, f32[3,4,8,128]{3,2,1,0:T(8,128)S(1)}, u32[]{:S(2)}, u32[]{:S(2)}) collective-permute-start(f32[3,4,8,128]{3,2,1,0:T(8,128)S(1)} %add.501), channel_id=1, source_target_pairs={{0,8},{8,16},{16,24},{24,32},{32,40},{40,48},{48,56},{56,64},{64,7... | collective-permute-start | bytes 147464 | tf_op jit(solution)/shard_map/while/body/eval_jaxpr/ppermute | solution.py:28
  278.7 9.6 %collective-permute-start = (f32[3,4,8,128]{3,2,1,0:T(8,128)S(1)}, f32[3,4,8,128]{3,2,1,0:T(8,128)S(1)}, u32[]{:S(2)}, u32[]{:S(2)}) collective-permute-start(f32[3,4,8,128]{3,2,1,0:T(8,128)S(1)} %add.501), channel_id=1, source_target_pairs={{0,8},{8,16},{16,24},{24,32},{32,40},{40,48},{48,56},{56,64},{64,7... | collective-permute-start | bytes 147464 | tf_op jit(solution)/shard_map/while/body/eval_jaxpr/ppermute | solution.py:28
  288.3 9.6 %collective-permute-start = (f32[3,4,8,128]{3,2,1,0:T(8,128)S(1)}, f32[3,4,8,128]{3,2,1,0:T(8,128)S(1)}, u32[]{:S(2)}, u32[]{:S(2)}) collective-permute-start(f32[3,4,8,128]{3,2,1,0:T(8,128)S(1)} %add.501), channel_id=1, source_target_pairs={{0,8},{8,16},{16,24},{24,32},{32,40},{40,48},{48,56},{56,64},{64,7... | collective-permute-start | bytes 147464 | tf_op jit(solution)/shard_map/while/body/eval_jaxpr/ppermute | solution.py:28
  298.0 9.6 %collective-permute-start = (f32[3,4,8,128]{3,2,1,0:T(8,128)S(1)}, f32[3,4,8,128]{3,2,1,0:T(8,128)S(1)}, u32[]{:S(2)}, u32[]{:S(2)}) collective-permute-start(f32[3,4,8,128]{3,2,1,0:T(8,128)S(1)} %add.501), channel_id=1, source_target_pairs={{0,8},{8,16},{16,24},{24,32},{32,40},{40,48},{48,56},{56,64},{64,7... | collective-permute-start | bytes 147464 | tf_op jit(solution)/shard_map/while/body/eval_jaxpr/ppermute | solution.py:28
  307.7 9.6 %collective-permute-start = (f32[3,4,8,128]{3,2,1,0:T(8,128)S(1)}, f32[3,4,8,128]{3,2,1,0:T(8,128)S(1)}, u32[]{:S(2)}, u32[]{:S(2)}) collective-permute-start(f32[3,4,8,128]{3,2,1,0:T(8,128)S(1)} %add.501), channel_id=1, source_target_pairs={{0,8},{8,16},{16,24},{24,32},{32,40},{40,48},{48,56},{56,64},{64,7... | collective-permute-start | bytes 147464 | tf_op jit(solution)/shard_map/while/body/eval_jaxpr/ppermute | solution.py:28
  317.4 9.6 %collective-permute-start = (f32[3,4,8,128]{3,2,1,0:T(8,128)S(1)}, f32[3,4,8,128]{3,2,1,0:T(8,128)S(1)}, u32[]{:S(2)}, u32[]{:S(2)}) collective-permute-start(f32[3,4,8,128]{3,2,1,0:T(8,128)S(1)} %add.501), channel_id=1, source_target_pairs={{0,8},{8,16},{16,24},{24,32},{32,40},{40,48},{48,56},{56,64},{64,7... | collective-permute-start | bytes 147464 | tf_op jit(solution)/shard_map/while/body/eval_jaxpr/ppermute | solution.py:28
  346.5 9.6 %collective-permute-start = (f32[3,4,8,128]{3,2,1,0:T(8,128)S(1)}, f32[3,4,8,128]{3,2,1,0:T(8,128)S(1)}, u32[]{:S(2)}, u32[]{:S(2)}) collective-permute-start(f32[3,4,8,128]{3,2,1,0:T(8,128)S(1)} %add.501), channel_id=1, source_target_pairs={{0,8},{8,16},{16,24},{24,32},{32,40},{40,48},{48,56},{56,64},{64,7... | collective-permute-start | bytes 147464 | tf_op jit(solution)/shard_map/while/body/eval_jaxpr/ppermute | solution.py:28
  356.2 9.6 %collective-permute-start = (f32[3,4,8,128]{3,2,1,0:T(8,128)S(1)}, f32[3,4,8,128]{3,2,1,0:T(8,128)S(1)}, u32[]{:S(2)}, u32[]{:S(2)}) collective-permute-start(f32[3,4,8,128]{3,2,1,0:T(8,128)S(1)} %add.501), channel_id=1, source_target_pairs={{0,8},{8,16},{16,24},{24,32},{32,40},{40,48},{48,56},{56,64},{64,7... | collective-permute-start | bytes 147464 | tf_op jit(solution)/shard_map/while/body/eval_jaxpr/ppermute | solution.py:28
  365.9 9.6 %collective-permute-start = (f32[3,4,8,128]{3,2,1,0:T(8,128)S(1)}, f32[3,4,8,128]{3,2,1,0:T(8,128)S(1)}, u32[]{:S(2)}, u32[]{:S(2)}) collective-permute-start(f32[3,4,8,128]{3,2,1,0:T(8,128)S(1)} %add.501), channel_id=1, source_target_pairs={{0,8},{8,16},{16,24},{24,32},{32,40},{40,48},{48,56},{56,64},{64,7... | collective-permute-start | bytes 147464 | tf_op jit(solution)/shard_map/while/body/eval_jaxpr/ppermute | solution.py:28
  375.6 9.6 %collective-permute-start = (f32[3,4,8,128]{3,2,1,0:T(8,128)S(1)}, f32[3,4,8,128]{3,2,1,0:T(8,128)S(1)}, u32[]{:S(2)}, u32[]{:S(2)}) collective-permute-start(f32[3,4,8,128]{3,2,1,0:T(8,128)S(1)} %add.501), channel_id=1, source_target_pairs={{0,8},{8,16},{16,24},{24,32},{32,40},{40,48},{48,56},{56,64},{64,7... | collective-permute-start | bytes 147464 | tf_op jit(solution)/shard_map/while/body/eval_jaxpr/ppermute | solution.py:28
  385.3 9.6 %collective-permute-start = (f32[3,4,8,128]{3,2,1,0:T(8,128)S(1)}, f32[3,4,8,128]{3,2,1,0:T(8,128)S(1)}, u32[]{:S(2)}, u32[]{:S(2)}) collective-permute-start(f32[3,4,8,128]{3,2,1,0:T(8,128)S(1)} %add.501), channel_id=1, source_target_pairs={{0,8},{8,16},{16,24},{24,32},{32,40},{40,48},{48,56},{56,64},{64,7... | collective-permute-start | bytes 147464 | tf_op jit(solution)/shard_map/while/body/eval_jaxpr/ppermute | solution.py:28
  395.0 9.6 %collective-permute-start = (f32[3,4,8,128]{3,2,1,0:T(8,128)S(1)}, f32[3,4,8,128]{3,2,1,0:T(8,128)S(1)}, u32[]{:S(2)}, u32[]{:S(2)}) collective-permute-start(f32[3,4,8,128]{3,2,1,0:T(8,128)S(1)} %add.501), channel_id=1, source_target_pairs={{0,8},{8,16},{16,24},{24,32},{32,40},{40,48},{48,56},{56,64},{64,7... | collective-permute-start | bytes 147464 | tf_op jit(solution)/shard_map/while/body/eval_jaxpr/ppermute | solution.py:28
  404.7 9.6 %collective-permute-start = (f32[3,4,8,128]{3,2,1,0:T(8,128)S(1)}, f32[3,4,8,128]{3,2,1,0:T(8,128)S(1)}, u32[]{:S(2)}, u32[]{:S(2)}) collective-permute-start(f32[3,4,8,128]{3,2,1,0:T(8,128)S(1)} %add.501), channel_id=1, source_target_pairs={{0,8},{8,16},{16,24},{24,32},{32,40},{40,48},{48,56},{56,64},{64,7... | collective-permute-start | bytes 147464 | tf_op jit(solution)/shard_map/while/body/eval_jaxpr/ppermute | solution.py:28
  443.5 9.6 %collective-permute-start = (f32[3,4,8,128]{3,2,1,0:T(8,128)S(1)}, f32[3,4,8,128]{3,2,1,0:T(8,128)S(1)}, u32[]{:S(2)}, u32[]{:S(2)}) collective-permute-start(f32[3,4,8,128]{3,2,1,0:T(8,128)S(1)} %add.501), channel_id=1, source_target_pairs={{0,8},{8,16},{16,24},{24,32},{32,40},{40,48},{48,56},{56,64},{64,7... | collective-permute-start | bytes 147464 | tf_op jit(solution)/shard_map/while/body/eval_jaxpr/ppermute | solution.py:28
  453.2 9.6 %collective-permute-start = (f32[3,4,8,128]{3,2,1,0:T(8,128)S(1)}, f32[3,4,8,128]{3,2,1,0:T(8,128)S(1)}, u32[]{:S(2)}, u32[]{:S(2)}) collective-permute-start(f32[3,4,8,128]{3,2,1,0:T(8,128)S(1)} %add.501), channel_id=1, source_target_pairs={{0,8},{8,16},{16,24},{24,32},{32,40},{40,48},{48,56},{56,64},{64,7... | collective-permute-start | bytes 147464 | tf_op jit(solution)/shard_map/while/body/eval_jaxpr/ppermute | solution.py:28
  462.9 9.6 %collective-permute-start = (f32[3,4,8,128]{3,2,1,0:T(8,128)S(1)}, f32[3,4,8,128]{3,2,1,0:T(8,128)S(1)}, u32[]{:S(2)}, u32[]{:S(2)}) collective-permute-start(f32[3,4,8,128]{3,2,1,0:T(8,128)S(1)} %add.501), channel_id=1, source_target_pairs={{0,8},{8,16},{16,24},{24,32},{32,40},{40,48},{48,56},{56,64},{64,7... | collective-permute-start | bytes 147464 | tf_op jit(solution)/shard_map/while/body/eval_jaxpr/ppermute | solution.py:28
  472.6 9.6 %collective-permute-start = (f32[3,4,8,128]{3,2,1,0:T(8,128)S(1)}, f32[3,4,8,128]{3,2,1,0:T(8,128)S(1)}, u32[]{:S(2)}, u32[]{:S(2)}) collective-permute-start(f32[3,4,8,128]{3,2,1,0:T(8,128)S(1)} %add.501), channel_id=1, source_target_pairs={{0,8},{8,16},{16,24},{24,32},{32,40},{40,48},{48,56},{56,64},{64,7... | collective-permute-start | bytes 147464 | tf_op jit(solution)/shard_map/while/body/eval_jaxpr/ppermute | solution.py:28
  482.3 9.6 %collective-permute-start = (f32[3,4,8,128]{3,2,1,0:T(8,128)S(1)}, f32[3,4,8,128]{3,2,1,0:T(8,128)S(1)}, u32[]{:S(2)}, u32[]{:S(2)}) collective-permute-start(f32[3,4,8,128]{3,2,1,0:T(8,128)S(1)} %add.501), channel_id=1, source_target_pairs={{0,8},{8,16},{16,24},{24,32},{32,40},{40,48},{48,56},{56,64},{64,7... | collective-permute-start | bytes 147464 | tf_op jit(solution)/shard_map/while/body/eval_jaxpr/ppermute | solution.py:28
  492.0 9.6 %collective-permute-start = (f32[3,4,8,128]{3,2,1,0:T(8,128)S(1)}, f32[3,4,8,128]{3,2,1,0:T(8,128)S(1)}, u32[]{:S(2)}, u32[]{:S(2)}) collective-permute-start(f32[3,4,8,128]{3,2,1,0:T(8,128)S(1)} %add.501), channel_id=1, source_target_pairs={{0,8},{8,16},{16,24},{24,32},{32,40},{40,48},{48,56},{56,64},{64,7... | collective-permute-start | bytes 147464 | tf_op jit(solution)/shard_map/while/body/eval_jaxpr/ppermute | solution.py:28
  501.7 9.6 %collective-permute-start = (f32[3,4,8,128]{3,2,1,0:T(8,128)S(1)}, f32[3,4,8,128]{3,2,1,0:T(8,128)S(1)}, u32[]{:S(2)}, u32[]{:S(2)}) collective-permute-start(f32[3,4,8,128]{3,2,1,0:T(8,128)S(1)} %add.501), channel_id=1, source_target_pairs={{0,8},{8,16},{16,24},{24,32},{32,40},{40,48},{48,56},{56,64},{64,7... | collective-permute-start | bytes 147464 | tf_op jit(solution)/shard_map/while/body/eval_jaxpr/ppermute | solution.py:28
  530.8 9.6 %collective-permute-start = (f32[3,4,8,128]{3,2,1,0:T(8,128)S(1)}, f32[3,4,8,128]{3,2,1,0:T(8,128)S(1)}, u32[]{:S(2)}, u32[]{:S(2)}) collective-permute-start(f32[3,4,8,128]{3,2,1,0:T(8,128)S(1)} %add.501), channel_id=1, source_target_pairs={{0,8},{8,16},{16,24},{24,32},{32,40},{40,48},{48,56},{56,64},{64,7... | collective-permute-start | bytes 147464 | tf_op jit(solution)/shard_map/while/body/eval_jaxpr/ppermute | solution.py:28
  540.5 9.6 %collective-permute-start = (f32[3,4,8,128]{3,2,1,0:T(8,128)S(1)}, f32[3,4,8,128]{3,2,1,0:T(8,128)S(1)}, u32[]{:S(2)}, u32[]{:S(2)}) collective-permute-start(f32[3,4,8,128]{3,2,1,0:T(8,128)S(1)} %add.501), channel_id=1, source_target_pairs={{0,8},{8,16},{16,24},{24,32},{32,40},{40,48},{48,56},{56,64},{64,7... | collective-permute-start | bytes 147464 | tf_op jit(solution)/shard_map/while/body/eval_jaxpr/ppermute | solution.py:28
  550.2 9.6 %collective-permute-start = (f32[3,4,8,128]{3,2,1,0:T(8,128)S(1)}, f32[3,4,8,128]{3,2,1,0:T(8,128)S(1)}, u32[]{:S(2)}, u32[]{:S(2)}) collective-permute-start(f32[3,4,8,128]{3,2,1,0:T(8,128)S(1)} %add.501), channel_id=1, source_target_pairs={{0,8},{8,16},{16,24},{24,32},{32,40},{40,48},{48,56},{56,64},{64,7... | collective-permute-start | bytes 147464 | tf_op jit(solution)/shard_map/while/body/eval_jaxpr/ppermute | solution.py:28
  559.9 9.6 %collective-permute-start = (f32[3,4,8,128]{3,2,1,0:T(8,128)S(1)}, f32[3,4,8,128]{3,2,1,0:T(8,128)S(1)}, u32[]{:S(2)}, u32[]{:S(2)}) collective-permute-start(f32[3,4,8,128]{3,2,1,0:T(8,128)S(1)} %add.501), channel_id=1, source_target_pairs={{0,8},{8,16},{16,24},{24,32},{32,40},{40,48},{48,56},{56,64},{64,7... | collective-permute-start | bytes 147464 | tf_op jit(solution)/shard_map/while/body/eval_jaxpr/ppermute | solution.py:28
  569.6 9.6 %collective-permute-start = (f32[3,4,8,128]{3,2,1,0:T(8,128)S(1)}, f32[3,4,8,128]{3,2,1,0:T(8,128)S(1)}, u32[]{:S(2)}, u32[]{:S(2)}) collective-permute-start(f32[3,4,8,128]{3,2,1,0:T(8,128)S(1)} %add.501), channel_id=1, source_target_pairs={{0,8},{8,16},{16,24},{24,32},{32,40},{40,48},{48,56},{56,64},{64,7... | collective-permute-start | bytes 147464 | tf_op jit(solution)/shard_map/while/body/eval_jaxpr/ppermute | solution.py:28
  579.3 9.6 %collective-permute-start = (f32[3,4,8,128]{3,2,1,0:T(8,128)S(1)}, f32[3,4,8,128]{3,2,1,0:T(8,128)S(1)}, u32[]{:S(2)}, u32[]{:S(2)}) collective-permute-start(f32[3,4,8,128]{3,2,1,0:T(8,128)S(1)} %add.501), channel_id=1, source_target_pairs={{0,8},{8,16},{16,24},{24,32},{32,40},{40,48},{48,56},{56,64},{64,7... | collective-permute-start | bytes 147464 | tf_op jit(solution)/shard_map/while/body/eval_jaxpr/ppermute | solution.py:28
  589.0 9.6 %collective-permute-start = (f32[3,4,8,128]{3,2,1,0:T(8,128)S(1)}, f32[3,4,8,128]{3,2,1,0:T(8,128)S(1)}, u32[]{:S(2)}, u32[]{:S(2)}) collective-permute-start(f32[3,4,8,128]{3,2,1,0:T(8,128)S(1)} %add.501), channel_id=1, source_target_pairs={{0,8},{8,16},{16,24},{24,32},{32,40},{40,48},{48,56},{56,64},{64,7... | collective-permute-start | bytes 147464 | tf_op jit(solution)/shard_map/while/body/eval_jaxpr/ppermute | solution.py:28
  637.4 9.7 %collective-permute-start = (f32[3,4,8,128]{3,2,1,0:T(8,128)S(1)}, f32[3,4,8,128]{3,2,1,0:T(8,128)S(1)}, u32[]{:S(2)}, u32[]{:S(2)}) collective-permute-start(f32[3,4,8,128]{3,2,1,0:T(8,128)S(1)} %add.501), channel_id=1, source_target_pairs={{0,8},{8,16},{16,24},{24,32},{32,40},{40,48},{48,56},{56,64},{64,7... | collective-permute-start | bytes 147464 | tf_op jit(solution)/shard_map/while/body/eval_jaxpr/ppermute | solution.py:28
  647.3 11.2 %collective-permute-start.7 = (f32[3,8,16,128]{3,2,1,0:T(8,128)S(1)}, f32[3,8,16,128]{3,2,1,0:T(8,128)S(1)}, u32[]{:S(2)}, u32[]{:S(2)}) collective-permute-start(f32[3,8,16,128]{3,2,1,0:T(8,128)S(1)} %add.240), channel_id=1, source_target_pairs={{0,8},{8,16},{16,24},{24,32},{32,40},{40,48},{48,56},{56,64},{64,7... | collective-permute-start | bytes 589832 | tf_op jit(solution)/shard_map/ppermute | solution.py:28
  (30 other events, 235.7 us)
where the time goes:
time: 665 us; the launch traced here: 660 us
  waiting for transfers between devices  507 us (76%)
  starting transfers between devices  141 us (21%)
    ppermute x64, waiting for transfers between devices, from_behind(): return lax.ppermute(block, axis, route)  495 us
    ppermute x64, starting transfers between devices, from_behind(): return lax.ppermute(block, axis, route)  123 us
  transfers between devices with their start and end apart: 70, of which 67 were waited for; matrix products, arithmetic and copies ran while one was open for 0% of the time, Pallas kernels for 0%

commit v1 on v0

v1 whole, which is shorter than its diff:
```python
import jax
import jax.numpy as jnp
from jax import lax
from jax.experimental import pallas as pl
from jax.experimental.pallas import tpu as pltpu
from jax.sharding import PartitionSpec as P

DT = 0.05
H = 0.5 * DT
KAPPA = ((1.0, 0.6, 1.4), (0.8, 1.2, 0.5), (0.7, 0.9, 1.1))
RATES = (0.5, 1.0, 0.3)
SIGNS = (-1.0, -0.5, 0.25)
Q1 = (DT * 5.0 / 24.0, DT / 3.0, -DT / 24.0)
Q2 = (-DT / 24.0, DT / 3.0, DT * 5.0 / 24.0)
Q3 = (DT / 6.0, DT * 2.0 / 3.0, DT / 6.0)
ROWS = 16
LANES = 128
EDGE = 18


def combine(weights, states):
    total = weights[0] * states[0]
    for w, s in zip(weights[1:], states[1:]):
        total = total + w * s
    return total


def shifted(v):
    rows = v.shape[0]
    y = lax.rem(lax.broadcasted_iota(jnp.int32, v.shape, 0), ROWS)
    z = lax.broadcasted_iota(jnp.int32, v.shape, 1)
    up = jnp.where(y == 0, 0.0, pltpu.roll(v, 1, 0))
    down = jnp.where(y == ROWS - 1, 0.0, pltpu.roll(v, rows - 1, 0))
    left = jnp.where(z == 0, 0.0, pltpu.roll(v, 1, 1))
    right = jnp.where(z == LANES - 1, 0.0, pltpu.roll(v, LANES - 1, 1))
    return (up + down) + (left + right)


def laplace(v):
    mid = v[ROWS:-ROWS]
    return v[: -2 * ROWS] + v[2 * ROWS :] + shifted(mid) - 6.0 * mid


def reaction(o, p, q):
    over = 0.5 * (p - 0.5 * q)
    return jnp.exp(over), jnp.exp(-over)


def current(state, film):
    fwd, bwd = reaction(*state)
    return film * state[0] * (fwd - bwd)


def conduct(region, k):
    return jnp.where(region == 0.0, KAPPA[k][0], jnp.where(region == 1.0, KAPPA[k][1], KAPPA[k][2]))


def inverse(mobile, k):
    return 1.0 - mobile * (H * RATES[k] / (1.0 + H * RATES[k]))


def first_new(old, lap, region, film, mobile):
    flow = combine(Q1, [current(old[m], film) for m in range(3)])
    news = []
    for k in range(3):
        w1 = combine(Q1, [old[m][k] for m in range(3)])
        inner = conduct(region, k) * lap[k] + SIGNS[k] * flow + RATES[k] * (H * old[1][k] - w1)
        news.append((old[0][k] + mobile * inner) * inverse(mobile, k))
    return news


def w2_of(old, k):
    return combine((Q2[0], Q2[1] - H, Q2[2]), [old[m][k] for m in range(3)])


def planes(lo, hi):
    return pl.ds(lo * ROWS, (hi - lo) * ROWS)


def edge_kernel(u, regions, activity, dirichlet, low_out, high_out):
    def tables(at):
        region = regions[at].astype(jnp.float32)
        film = jnp.where(region == 0.0, activity[at], 0.0)
        return region, film, 1.0 - dirichlet[at].astype(jnp.float32)

    for out, edge, inner, three in ((low_out, 0, 1, 0), (high_out, 7, 6, 5)):
        at = planes(inner, inner + 1)
        old = [[u[m * 3 + k, at] for k in range(3)] for m in range(3)]
        wide = planes(three, three + 3)
        lap = []
        for k in range(3):
            w1 = combine(Q1, [u[m * 3 + k, wide] for m in range(3)])
            out[9 + k] = w1[ROWS : 2 * ROWS]
            lap.append(laplace(w1))
        news = first_new(old, lap, *tables(at))
        for k in range(3):
            out[12 + k] = H * news[k] + w2_of(old, k)
        end = planes(edge, edge + 1)
        for i in range(9):
            out[i] = u[i, end]
        for i, table in enumerate(tables(end)):
            out[15 + i] = table


def main_kernel(u, regions, activity, dirichlet, low, high, new1_out, new2_out, payload, local, scratch):
    def wrap(inside, i):
        return jnp.concatenate([low[i], inside, high[i]], axis=0)

    region = wrap(regions[...].astype(jnp.float32), 15)
    film = wrap(jnp.where(regions[...] == 0, activity[...], 0.0), 16)
    mobile = wrap(1.0 - dirichlet[...].astype(jnp.float32), 17)
    old = [[wrap(u[m * 3 + k], m * 3 + k) for k in range(3)] for m in range(3)]
    lap1 = []
    for k in range(3):
        w1 = combine(Q1, [old[m][k] for m in range(3)])
        lap1.append(laplace(jnp.concatenate([low[9 + k], w1, high[9 + k]], axis=0)))
    new1 = first_new(old, lap1, region, film, mobile)
    flows = [current(old[m], film) for m in range(3)]
    flow2 = combine((Q2[0], Q2[1] - H, Q2[2]), flows) + H * current(new1, film)
    new2 = []
    for k in range(3):
        v2 = H * new1[k] + w2_of(old, k)
        lap2 = laplace(jnp.concatenate([low[12 + k], v2, high[12 + k]], axis=0))
        decay = H * old[2][k] - combine(Q2, [old[m][k] for m in range(3)])
        inner = conduct(region, k) * lap2 + SIGNS[k] * flow2 + RATES[k] * decay
        new2.append((new1[k] + mobile * inner) * inverse(mobile, k))
    mid = slice(ROWS, -ROWS)
    flow3 = combine(Q3, [flows[0][mid], current([v[mid] for v in new1], film[mid]), current([v[mid] for v in new2], film[mid])])

    def restrict(i, v):
        pairs = v.reshape(4, 2, ROWS, LANES)
        scratch[i] = (pairs[:, 0] + pairs[:, 1]).reshape(4 * ROWS, LANES)
        return 0.25 * (scratch[i, pl.ds(0, 32, stride=2)] + scratch[i, pl.ds(1, 32, stride=2)])

    region, mobile_mid, film_mid = region[mid], mobile[mid], film[mid]
    integral, zero, one = [], [], []
    for k in range(3):
        v3 = combine(Q3, [old[0][k], new1[k], new2[k]])
        force = mobile_mid * (conduct(region, k) * laplace(v3) + SIGNS[k] * flow3 - RATES[k] * v3[mid])
        integral.append(restrict(k, force))
        new1_out[k] = new1[k][mid]
        new2_out[k] = new2[k][mid]
        zero.append(restrict(3 + k, old[0][k][mid]))
        one.append(restrict(6 + k, new2[k][mid]))
    cfilm = restrict(9, film_mid)
    cmobile = restrict(10, mobile_mid)
    fwd, bwd = reaction(*zero)
    scale = (DT * cmobile) * cfilm
    a = scale * (fwd - bwd)
    b = scale * zero[0] * 0.5 * (fwd + bwd)
    slope = a * zero[0] + b * (zero[1] - 0.5 * zero[2])
    flow_c = (cfilm * zero[0] * (fwd - bwd)) + current(one, cfilm)
    is_first = lax.axis_index("tm") == 0
    local[3] = a
    local[4] = b
    local[5] = cmobile
    sent = []
    for k in range(3):
        tend = H * cmobile * (SIGNS[k] * flow_c - RATES[k] * (zero[k] + one[k]))
        fas = integral[k] - tend
        term = (DT * RATES[k]) * cmobile * one[k] - SIGNS[k] * slope + tend + fas
        local[k] = term
        local[6 + k] = zero[k]
        local[9 + k] = one[k]
        sent.append(jnp.where(is_first, term + zero[k] + SIGNS[k] * slope, term))
    sent += [jnp.where(is_first, 0.0, a), jnp.where(is_first, 0.0, b), jnp.zeros_like(a)]
    lane = lax.broadcasted_iota(jnp.int32, (32, LANES), 1)
    half = lane < 64
    for m in range(3):
        x, y = sent[2 * m], sent[2 * m + 1]
        payload[pl.ds(m, 32, stride=8)] = jnp.where(half, x, pltpu.roll(y, 64, 1))
        payload[pl.ds(4 + m, 32, stride=8)] = jnp.where(half, pltpu.roll(x, 64, 1), y)
    payload[pl.ds(3, 32, stride=8)] = jnp.zeros_like(a)
    payload[pl.ds(7, 32, stride=8)] = jnp.zeros_like(a)


def scan_kernel(arrived, local, out, rolled, states):
    me = lax.axis_index("tm")
    row = local[5, pl.ds(me // 2, 1)]
    cmobile = jnp.where(lax.rem(me, 2) == 0, row, pltpu.roll(row, 64, 1))
    keep = [1.0 / (1.0 + (DT * RATES[k]) * cmobile) for k in range(3)]
    rolled[...] = pltpu.roll(arrived[...], 64, 1)
    v = [jnp.zeros((1, LANES), jnp.float32) for _ in range(3)]
    for n in range(64):
        for k in range(3):
            states[k, pl.ds(n, 1)] = v[k]
        term = [arrived[pl.ds(4 * n, 1)], rolled[pl.ds(4 * n, 1)], arrived[pl.ds(4 * n + 1, 1)]]
        a, b = rolled[pl.ds(4 * n + 1, 1)], arrived[pl.ds(4 * n + 2, 1)]
        t = a * v[0] + b * (v[1] - 0.5 * v[2])
        v = [keep[k] * (v[k] + term[k] + SIGNS[k] * t) for k in range(3)]
    half = lax.broadcasted_iota(jnp.int32, (64, LANES), 1) < 64
    out[pl.ds(0, 64, stride=2)] = jnp.where(half, states[0], pltpu.roll(states[1], 64, 1))
    out[pl.ds(1, 64, stride=2)] = states[2]


def finish_kernel(u, new1, new2, behind, local, starts, out, scratch):
    is_first = lax.axis_index("tm") == 0
    half = lax.broadcasted_iota(jnp.int32, (32, LANES), 1) < 64
    rows = [starts[pl.ds(i, 32, stride=4)] for i in range(4)]
    start = [
        jnp.where(half, rows[0], pltpu.roll(rows[2], 64, 1)),
        jnp.where(half, pltpu.roll(rows[0], 64, 1), rows[2]),
        jnp.where(half, rows[1], pltpu.roll(rows[3], 64, 1)),
    ]
    start = [jnp.where(is_first, local[6 + k], start[k]) for k in range(3)]
    t = local[3] * start[0] + local[4] * (start[1] - 0.5 * start[2])

    def prolong(i, v):
        scratch[i, pl.ds(0, 32, stride=2)] = v
        scratch[i, pl.ds(1, 32, stride=2)] = v
        wide = scratch[i].reshape(4, 1, ROWS, LANES)
        return jnp.broadcast_to(wide, (4, 2, ROWS, LANES)).reshape(8 * ROWS, LANES)

    for k in range(3):
        end = (start[k] + local[k] + SIGNS[k] * t) / (1.0 + (DT * RATES[k]) * local[5])
        delta_zero = start[k] - local[6 + k]
        delta_one = end - local[9 + k]
        head = jnp.where(is_first, u[k], behind[k])
        pairs = head.reshape(4, 2, ROWS, LANES)
        scratch[9 + k] = (pairs[:, 0] + pairs[:, 1]).reshape(4 * ROWS, LANES)
        coarse = 0.25 * (scratch[9 + k, pl.ds(0, 32, stride=2)] + scratch[9 + k, pl.ds(1, 32, stride=2)])
        out[k] = head + prolong(3 * k, start[k] - coarse)
        out[3 + k] = new1[k] + prolong(3 * k + 1, 0.5 * (delta_zero + delta_one))
        out[6 + k] = new2[k] + prolong(3 * k + 2, delta_one)


def call(kernel, outs, scratch, *args):
    return pl.pallas_call(
        kernel,
        out_shape=[jax.ShapeDtypeStruct(s, jnp.float32) for s in outs],
        in_specs=[pl.BlockSpec(memory_space=pltpu.VMEM)] * len(args),
        out_specs=[pl.BlockSpec(memory_space=pltpu.VMEM)] * len(outs),
        scratch_shapes=[pltpu.VMEM(s, jnp.float32) for s in scratch],
        compiler_params=pltpu.CompilerParams(vmem_limit_bytes=32 * 1024 * 1024),
    )(*args)


def on_device(fine_nodes, regions, activity, dirichlet):
    u = fine_nodes.reshape(9, 128, LANES)
    tables = [v.reshape(128, LANES) for v in (regions, activity, dirichlet)]
    edge = (EDGE, ROWS, LANES)
    to_low, to_high = call(edge_kernel, [edge, edge], [], u, *tables)
    count = lax.axis_size("space")
    low = lax.ppermute(to_high, "space", [(i, i + 1) for i in range(count - 1)])
    high = lax.ppermute(to_low, "space", [(i + 1, i) for i in range(count - 1)])
    brick = (3, 128, LANES)
    new1, new2, payload, local = call(
        main_kernel, [brick, brick, (256, LANES), (12, 32, LANES)], [(11, 64, LANES)], u, *tables, low, high
    )
    slices = lax.axis_size("tm")
    behind = lax.ppermute(new2, "tm", [(i, i + 1) for i in range(slices - 1)])
    arrived = lax.all_to_all(payload, "tm", 0, 0, tiled=True)
    (starts,) = call(scan_kernel, [(128, LANES)], [(256, LANES), (3, 64, LANES)], arrived, local)
    starts = lax.all_to_all(starts, "tm", 0, 0, tiled=True)
    (out,) = call(finish_kernel, [(9, 128, LANES)], [(12, 64, LANES)], u, new1, new2, behind, local, starts)
    return out.reshape(fine_nodes.shape)


def solution(mesh):
    whole = P("tm", None, None, "space", None, None)
    part = P("space", None, None)
    return jax.shard_map(
        on_device, mesh=mesh, in_specs=(whole, part, part, part), out_specs=whole, check_vma=False
    )
```

time: 665 us -> 68.1 us (0.10)
  the two profiles are of different devices: /device:TPU:264 before, /device:TPU:7 now
where the time goes in v1:
time: 68.1 us; the launch traced here: 67.6 us
  starting transfers between devices  32.5 us (48%)
  waiting for transfers between devices  27.2 us (40%)
  Pallas kernels  4.23 us (6%)
  local copies, waits for them, and re-layouts  3.58 us (5%)
    all_to_all x1, starting transfers between devices, on_device(): arrived = lax.all_to_all(payload, 'tm', 0, 0, tiled=True)  17.2 us
    all_to_all x1, waiting for transfers between devices, on_device(): starts = lax.all_to_all(starts, 'tm', 0, 0, tiled=True)  12.2 us
    all_to_all x1, waiting for transfers between devices, on_device(): arrived = lax.all_to_all(payload, 'tm', 0, 0, tiled=True)  8.78 us
    all_to_all x1, starting transfers between devices, on_device(): starts = lax.all_to_all(starts, 'tm', 0, 0, tiled=True)  5.58 us
    ppermute x1, waiting for transfers between devices, on_device(): high = lax.ppermute(to_low, 'space', [(i + 1, i) for i in range(count - 1)])  4.92 us
    ppermute x1, starting transfers between devices, on_device(): behind = lax.ppermute(new2, 'tm', [(i, i + 1) for i in range(slices - 1)])  4.44 us
    pallas_call x4, Pallas kernels, call(): pl.pallas_call(kernel, out_shape=[jax.ShapeDtypeStruct(s, jnp.float32) fo...  4.23 us
    unnamed x10, local copies, waits for them, and re-layouts  3.58 us
  transfers between devices with their start and end apart: 5, of which 4 were waited for; matrix products, arithmetic and copies ran while one was open for 0% of the time, Pallas kernels for 2%

profile of v1, /device:TPU:7, one launch (start us, length us, event | category | flops | bytes accessed | tf_op | source)
XLA Modules:
  0.0 67.6 jit_solution(14564601502661225238)
XLA Ops:
  0.0 0.0 copy-start
  0.0 1.1 %copy-done = f32[1,3,3,8,16,128]{5,4,3,2,1,0:T(8,128)S(1)} copy-done((f32[1,3,3,8,16,128]{5,4,3,2,1,0:T(8,128)S(1)}, f32[1,3,3,8,16,128]{5,4,3,2,1,0:T(8,128)}, u32[]{:S(2)}) %copy-start) | copy-done | bytes 589848
  1.1 0.0 copy-start.2
  1.1 0.8 %copy-done.2 = s32[8,16,128]{2,1,0:T(8,128)S(1)} copy-done((s32[8,16,128]{2,1,0:T(8,128)S(1)}, s32[8,16,128]{2,1,0:T(8,128)}, u32[]{:S(2)}) %copy-start.2) | copy-done | bytes 65560
  1.9 0.0 copy-start.3
  1.9 0.8 %copy-done.3 = f32[8,16,128]{2,1,0:T(8,128)S(1)} copy-done((f32[8,16,128]{2,1,0:T(8,128)S(1)}, f32[8,16,128]{2,1,0:T(8,128)}, u32[]{:S(2)}) %copy-start.3) | copy-done | bytes 65560
  2.7 0.0 copy-start.4
  2.7 0.8 %copy-done.4 = s32[8,16,128]{2,1,0:T(8,128)S(1)} copy-done((s32[8,16,128]{2,1,0:T(8,128)S(1)}, s32[8,16,128]{2,1,0:T(8,128)}, u32[]{:S(2)}) %copy-start.4) | copy-done | bytes 65560
  3.6 0.1 shard_map.46
  3.7 3.1 %collective-permute-start = (f32[18,16,128]{2,1,0:T(8,128)S(1)}, f32[18,16,128]{2,1,0:T(8,128)S(1)}, u32[]{:S(2)}, u32[]{:S(2)}) collective-permute-start(f32[18,16,128]{2,1,0:T(8,128)S(1)} %get-tuple-element.11), channel_id=1, source_target_pairs={{0,1},{1,2},{2,3},{3,4},{4,5},{5,6},{6,7},{8,9},{9,10},{10,11},{11... | collective-permute-start | bytes 442376 | tf_op jit(solution)/shard_map/ppermute | solution.py:244
  6.8 2.2 %collective-permute-start.1 = (f32[18,16,128]{2,1,0:T(8,128)S(1)}, f32[18,16,128]{2,1,0:T(8,128)S(1)}, u32[]{:S(2)}, u32[]{:S(2)}) collective-permute-start(f32[18,16,128]{2,1,0:T(8,128)S(1)} %get-tuple-element.12), channel_id=1, source_target_pairs={{1,0},{2,1},{3,2},{4,3},{5,4},{6,5},{7,6},{9,8},{10,9},{11,10},{12... | collective-permute-start | bytes 442376 | tf_op jit(solution)/shard_map/ppermute | solution.py:245
  9.0 1.3 %collective-permute-done.low = f32[18,16,128]{2,1,0:T(8,128)S(1)} collective-permute-done((f32[18,16,128]{2,1,0:T(8,128)S(1)}, f32[18,16,128]{2,1,0:T(8,128)S(1)}, u32[]{:S(2)}, u32[]{:S(2)}) %collective-permute-start) | collective-permute-done | bytes 147488 | tf_op jit(solution)/shard_map/ppermute | solution.py:244
  10.3 4.9 %collective-permute-done.1.high = f32[18,16,128]{2,1,0:T(8,128)S(1)} collective-permute-done((f32[18,16,128]{2,1,0:T(8,128)S(1)}, f32[18,16,128]{2,1,0:T(8,128)S(1)}, u32[]{:S(2)}, u32[]{:S(2)}) %collective-permute-start.1) | collective-permute-done | bytes 147488 | tf_op jit(solution)/shard_map/ppermute | solution.py:245
  15.2 1.9 %shard_map.47 = (f32[3,128,128]{2,1,0:T(8,128)S(1)}, f32[3,128,128]{2,1,0:T(8,128)S(1)}, f32[256,128]{1,0:T(8,128)}, f32[12,32,128]{2,1,0:T(8,128)S(1)}) custom-call(f32[9,128,128]{2,1,0:T(8,128)S(1)} %bitcast.10, s32[128,128]{1,0:T(8,128)S(1)} %bitcast.14, f32[128,128]{1,0:T(8,128)S(1)} %bitcast.16, s32[128,128]{1,0:T(8,128)S(1)} %bitcast.18, ...), custom_call_target="tpu_custom_call" | custom-call | tf_op jit(solution)/shard_map/pallas_call | solution.py:228
  17.1 0.0 copy-start.1
  17.1 17.2 %all-to-all-start = ((f32[64,4,128]{2,1,0:T(4,128)}), f32[64,4,128]{2,1,0:T(4,128)S(1)}, u32[]{:S(2)}, u32[]{:S(2)}) async-start(f32[64,4,128]{2,1,0:T(4,128)} %bitcast.4), calls=%async_computation | async-start | bytes 262144 | tf_op jit(solution)/shard_map/all_to_all | solution.py:252
  34.3 4.4 %collective-permute-start.2 = (f32[3,128,128]{2,1,0:T(8,128)S(1)}, f32[3,128,128]{2,1,0:T(8,128)S(1)}, u32[]{:S(2)}, u32[]{:S(2)}) collective-permute-start(f32[3,128,128]{2,1,0:T(8,128)S(1)} %get-tuple-element.14.new2), channel_id=1, source_target_pairs={{0,8},{8,16},{16,24},{24,32},{32,40},{40,48},{48,56},{56,64},{64,7... | collective-permute-start | bytes 589832 | tf_op jit(solution)/shard_map/ppermute | solution.py:251
  38.8 8.8 %all-to-all-done = f32[64,4,128]{2,1,0:T(4,128)S(1)} async-done(((f32[64,4,128]{2,1,0:T(4,128)}), f32[64,4,128]{2,1,0:T(4,128)S(1)}, u32[]{:S(2)}, u32[]{:S(2)}) %all-to-all-start) | async-done | bytes 131104 | tf_op jit(solution)/shard_map/all_to_all | solution.py:252
  47.6 1.3 %shard_map.48 = f32[128,128]{1,0:T(8,128)} custom-call(f32[256,128]{1,0:T(8,128)S(1)} %bitcast.12, f32[12,32,128]{2,1,0:T(8,128)S(1)} %get-tuple-element.15.local), custom_call_target="tpu_custom_call" | custom-call | tf_op jit(solution)/shard_map/pallas_call | solution.py:228
  48.8 5.6 %all-to-all-start.1 = ((f32[64,2,128]{2,1,0:T(2,128)}), f32[64,2,128]{2,1,0:T(2,128)S(1)}, u32[]{:S(2)}, u32[]{:S(2)}) async-start(f32[64,2,128]{2,1,0:T(2,128)} %bitcast.6), calls=%async_computation.1 | async-start | bytes 131072 | tf_op jit(solution)/shard_map/all_to_all | solution.py:254
  54.4 0.0 collective-permute-done.2.behind
  54.4 12.2 %all-to-all-done.1 = f32[64,2,128]{2,1,0:T(2,128)S(1)} async-done(((f32[64,2,128]{2,1,0:T(2,128)}), f32[64,2,128]{2,1,0:T(2,128)S(1)}, u32[]{:S(2)}, u32[]{:S(2)}) %all-to-all-start.1) | async-done | bytes 65568 | tf_op jit(solution)/shard_map/all_to_all | solution.py:254
  66.6 0.0 copy-done.1
  66.6 1.0 %shard_map.49 = f32[9,128,128]{2,1,0:T(8,128)} custom-call(f32[9,128,128]{2,1,0:T(8,128)S(1)} %bitcast.11, f32[3,128,128]{2,1,0:T(8,128)S(1)} %get-tuple-element.13.new1, f32[3,128,128]{2,1,0:T(8,128)S(1)} %get-tuple-element.14.new2, f32[3,128,128]{2,1,0:T(8,128)S(1)} %collective-permute-done.2.behind, f32[12,32,128]{2,1,0:T(8,128)S(1)} %get-tuple-element.15.local, ...), custom_call_target="tpu_custom_call" | custom-call | tf_op jit(solution)/shard_map/pallas_call | solution.py:228
Async XLA Ops:
  0.0 1.1 %copy-start = (f32[1,3,3,8,16,128]{5,4,3,2,1,0:T(8,128)S(1)}, f32[1,3,3,8,16,128]{5,4,3,2,1,0:T(8,128)}, u32[]{:S(2)}) copy-start(f32[1,3,3,8,16,128]{5,4,3,2,1,0:T(8,128)} %param.4) | copy-start | bytes 1769476
  1.1 0.8 %copy-start.2 = (s32[8,16,128]{2,1,0:T(8,128)S(1)}, s32[8,16,128]{2,1,0:T(8,128)}, u32[]{:S(2)}) copy-start(s32[8,16,128]{2,1,0:T(8,128)} %param.5) | copy-start | bytes 196612
  1.9 0.8 %copy-start.3 = (f32[8,16,128]{2,1,0:T(8,128)S(1)}, f32[8,16,128]{2,1,0:T(8,128)}, u32[]{:S(2)}) copy-start(f32[8,16,128]{2,1,0:T(8,128)} %param.6) | copy-start | bytes 196612
  2.7 0.8 %copy-start.4 = (s32[8,16,128]{2,1,0:T(8,128)S(1)}, s32[8,16,128]{2,1,0:T(8,128)}, u32[]{:S(2)}) copy-start(s32[8,16,128]{2,1,0:T(8,128)} %param.7) | copy-start | bytes 196612
  3.7 6.6 %collective-permute-start = (f32[18,16,128]{2,1,0:T(8,128)S(1)}, f32[18,16,128]{2,1,0:T(8,128)S(1)}, u32[]{:S(2)}, u32[]{:S(2)}) collective-permute-start(f32[18,16,128]{2,1,0:T(8,128)S(1)} %get-tuple-element.11), channel_id=1, source_target_pairs={{0,1},{1,2},{2,3},{3,4},{4,5},{5,6},{6,7},{8,9},{9,10},{10,11},{11... | collective-permute-start | bytes 442376 | tf_op jit(solution)/shard_map/ppermute | solution.py:244
  6.8 8.4 %collective-permute-start.1 = (f32[18,16,128]{2,1,0:T(8,128)S(1)}, f32[18,16,128]{2,1,0:T(8,128)S(1)}, u32[]{:S(2)}, u32[]{:S(2)}) collective-permute-start(f32[18,16,128]{2,1,0:T(8,128)S(1)} %get-tuple-element.12), channel_id=1, source_target_pairs={{1,0},{2,1},{3,2},{4,3},{5,4},{6,5},{7,6},{9,8},{10,9},{11,10},{12... | collective-permute-start | bytes 442376 | tf_op jit(solution)/shard_map/ppermute | solution.py:245
  17.1 49.5 %copy-start.1 = (f32[1,3,3,8,16,128]{5,4,3,2,1,0:T(8,128)S(1)}, f32[1,3,3,8,16,128]{5,4,3,2,1,0:T(8,128)}, u32[]{:S(2)}) copy-start(f32[1,3,3,8,16,128]{5,4,3,2,1,0:T(8,128)} %param.4) | copy-start | bytes 1769476
  17.1 30.5 %all-to-all-start = ((f32[64,4,128]{2,1,0:T(4,128)}), f32[64,4,128]{2,1,0:T(4,128)S(1)}, u32[]{:S(2)}, u32[]{:S(2)}) async-start(f32[64,4,128]{2,1,0:T(4,128)} %bitcast.4), calls=%async_computation | async-start | bytes 262144 | tf_op jit(solution)/shard_map/all_to_all | solution.py:252
  34.3 20.1 %collective-permute-start.2 = (f32[3,128,128]{2,1,0:T(8,128)S(1)}, f32[3,128,128]{2,1,0:T(8,128)S(1)}, u32[]{:S(2)}, u32[]{:S(2)}) collective-permute-start(f32[3,128,128]{2,1,0:T(8,128)S(1)} %get-tuple-element.14.new2), channel_id=1, source_target_pairs={{0,8},{8,16},{16,24},{24,32},{32,40},{40,48},{48,56},{56,64},{64,7... | collective-permute-start | bytes 589832 | tf_op jit(solution)/shard_map/ppermute | solution.py:251
  48.8 17.8 %all-to-all-start.1 = ((f32[64,2,128]{2,1,0:T(2,128)}), f32[64,2,128]{2,1,0:T(2,128)S(1)}, u32[]{:S(2)}, u32[]{:S(2)}) async-start(f32[64,2,128]{2,1,0:T(2,128)} %bitcast.6), calls=%async_computation.1 | async-start | bytes 131072 | tf_op jit(solution)/shard_map/all_to_all | solution.py:254

commit v2 on v1

--- a/solution.py
+++ b/solution.py
@@ -77,79 +77,158 @@
     return pl.ds(lo * ROWS, (hi - lo) * ROWS)
 
 
-def edge_kernel(u, regions, activity, dirichlet, low_out, high_out):
-    def tables(at):
-        region = regions[at].astype(jnp.float32)
-        film = jnp.where(region == 0.0, activity[at], 0.0)
-        return region, film, 1.0 - dirichlet[at].astype(jnp.float32)
-
-    for out, edge, inner, three in ((low_out, 0, 1, 0), (high_out, 7, 6, 5)):
-        at = planes(inner, inner + 1)
-        old = [[u[m * 3 + k, at] for k in range(3)] for m in range(3)]
-        wide = planes(three, three + 3)
+def copy_all(pairs, sems):
+    copies = [pltpu.make_async_copy(src, dst, sems.at[i]) for i, (src, dst) in enumerate(pairs)]
+    for copy in copies:
+        copy.start()
+    for copy in copies:
+        copy.wait()
+
+
+def edge_kernel(u_far, regions_far, activity_far, dirichlet_far, low_out, high_out, u, ints, activity, sems):
+    pairs = []
+    for side, three, two in ((0, 0, 0), (1, 5, 6)):
+        wide, at = planes(three, three + 3), planes(two, two + 2)
+        pairs.append((u_far.at[:, wide], u.at[side]))
+        pairs.append((regions_far.at[at], ints.at[side, 0]))
+        pairs.append((dirichlet_far.at[at], ints.at[side, 1]))
+        pairs.append((activity_far.at[at], activity.at[side]))
+    copy_all(pairs, sems)
+
+    def tables(side, plane):
+        at = planes(plane, plane + 1)
+        region = ints[side, 0, at].astype(jnp.float32)
+        film = jnp.where(region == 0.0, activity[side, at], 0.0)
+        return region, film, 1.0 - ints[side, 1, at].astype(jnp.float32)
+
+    mid = planes(1, 2)
+    for side, out, edge in ((0, low_out, 0), (1, high_out, 2)):
+        old = [[u[side, m * 3 + k, mid] for k in range(3)] for m in range(3)]
         lap = []
         for k in range(3):
-            w1 = combine(Q1, [u[m * 3 + k, wide] for m in range(3)])
+            w1 = combine(Q1, [u[side, m * 3 + k] for m in range(3)])
             out[9 + k] = w1[ROWS : 2 * ROWS]
             lap.append(laplace(w1))
-        news = first_new(old, lap, *tables(at))
+        news = first_new(old, lap, *tables(side, 1 - side))
         for k in range(3):
             out[12 + k] = H * news[k] + w2_of(old, k)
         end = planes(edge, edge + 1)
         for i in range(9):
-            out[i] = u[i, end]
-        for i, table in enumerate(tables(end)):
+            out[i] = u[side, i, end]
+        for i, table in enumerate(tables(side, side)):
             out[15 + i] = table
 
 
-def main_kernel(u, regions, activity, dirichlet, low, high, new1_out, new2_out, payload, local, scratch):
-    def wrap(inside, i):
-        return jnp.concatenate([low[i], inside, high[i]], axis=0)
-
-    region = wrap(regions[...].astype(jnp.float32), 15)
-    film = wrap(jnp.where(regions[...] == 0, activity[...], 0.0), 16)
-    mobile = wrap(1.0 - dirichlet[...].astype(jnp.float32), 17)
-    old = [[wrap(u[m * 3 + k], m * 3 + k) for k in range(3)] for m in range(3)]
+def restrict(scratch, i, v):
+    pairs = v.reshape(4, 2, ROWS, LANES)
+    scratch[i] = (pairs[:, 0] + pairs[:, 1]).reshape(4 * ROWS, LANES)
+    return 0.25 * (scratch[i, pl.ds(0, 32, stride=2)] + scratch[i, pl.ds(1, 32, stride=2)])
+
+
+def inner_kernel(u, regions, activity, dirichlet, fine, coarse, scratch):
+    region = regions[...].astype(jnp.float32)
+    film = jnp.where(regions[...] == 0, activity[...], 0.0)
+    mobile = 1.0 - dirichlet[...].astype(jnp.float32)
+    old = [[u[m * 3 + k] for k in range(3)] for m in range(3)]
+    zeros = jnp.zeros((ROWS, LANES), jnp.float32)
     lap1 = []
     for k in range(3):
         w1 = combine(Q1, [old[m][k] for m in range(3)])
-        lap1.append(laplace(jnp.concatenate([low[9 + k], w1, high[9 + k]], axis=0)))
+        fine[9 + k] = w1
+        lap1.append(laplace(jnp.concatenate([zeros, w1, zeros], axis=0)))
     new1 = first_new(old, lap1, region, film, mobile)
     flows = [current(old[m], film) for m in range(3)]
-    flow2 = combine((Q2[0], Q2[1] - H, Q2[2]), flows) + H * current(new1, film)
-    new2 = []
-    for k in range(3):
-        v2 = H * new1[k] + w2_of(old, k)
-        lap2 = laplace(jnp.concatenate([low[12 + k], v2, high[12 + k]], axis=0))
+    flow2 = combine((Q2[0], Q2[1] - H, Q2[2]), flows)
+    fine[12] = flows[0]
+    for k in range(3):
+        fine[k] = new1[k]
+        fine[3 + k] = w2_of(old, k)
         decay = H * old[2][k] - combine(Q2, [old[m][k] for m in range(3)])
-        inner = conduct(region, k) * lap2 + SIGNS[k] * flow2 + RATES[k] * decay
-        new2.append((new1[k] + mobile * inner) * inverse(mobile, k))
-    mid = slice(ROWS, -ROWS)
-    flow3 = combine(Q3, [flows[0][mid], current([v[mid] for v in new1], film[mid]), current([v[mid] for v in new2], film[mid])])
-
-    def restrict(i, v):
-        pairs = v.reshape(4, 2, ROWS, LANES)
-        scratch[i] = (pairs[:, 0] + pairs[:, 1]).reshape(4 * ROWS, LANES)
-        return 0.25 * (scratch[i, pl.ds(0, 32, stride=2)] + scratch[i, pl.ds(1, 32, stride=2)])
-
-    region, mobile_mid, film_mid = region[mid], mobile[mid], film[mid]
-    integral, zero, one = [], [], []
-    for k in range(3):
-        v3 = combine(Q3, [old[0][k], new1[k], new2[k]])
-        force = mobile_mid * (conduct(region, k) * laplace(v3) + SIGNS[k] * flow3 - RATES[k] * v3[mid])
-        integral.append(restrict(k, force))
-        new1_out[k] = new1[k][mid]
-        new2_out[k] = new2[k][mid]
-        zero.append(restrict(3 + k, old[0][k][mid]))
-        one.append(restrict(6 + k, new2[k][mid]))
-    cfilm = restrict(9, film_mid)
-    cmobile = restrict(10, mobile_mid)
+        fine[6 + k] = SIGNS[k] * flow2 + RATES[k] * decay
+    zero = [restrict(scratch, k, old[0][k]) for k in range(3)]
+    cfilm = restrict(scratch, 3, film)
+    cmobile = restrict(scratch, 4, mobile)
     fwd, bwd = reaction(*zero)
     scale = (DT * cmobile) * cfilm
-    a = scale * (fwd - bwd)
-    b = scale * zero[0] * 0.5 * (fwd + bwd)
+    coarse[0] = scale * (fwd - bwd)
+    coarse[1] = scale * zero[0] * 0.5 * (fwd + bwd)
+    coarse[2] = cmobile
+    coarse[3] = cfilm
+    coarse[4] = cfilm * zero[0] * (fwd - bwd)
+    for k in range(3):
+        coarse[5 + k] = zero[k]
+
+
+def outer_new1(near, side):
+    old = [[side[m * 3 + k] for k in range(3)] for m in range(3)]
+    lap = []
+    for k in range(3):
+        w1 = combine(Q1, [old[m][k] for m in range(3)])
+        lap.append(side[9 + k] + near[k] + shifted(w1) - 6.0 * w1)
+    return first_new(old, lap, side[15], side[16], side[17])
+
+
+def outer_rest(side):
+    old = [[side[m * 3 + k] for k in range(3)] for m in range(3)]
+    flow2 = combine((Q2[0], Q2[1] - H, Q2[2]), [current(old[m], side[16]) for m in range(3)])
+    rest = []
+    for k in range(3):
+        decay = H * old[2][k] - combine(Q2, [old[m][k] for m in range(3)])
+        rest.append(SIGNS[k] * flow2 + RATES[k] * decay)
+    return rest, [w2_of(old, k) for k in range(3)]
+
+
+def main_kernel(u, regions, activity, dirichlet, fine, coarse, low, high, new1_out, new2_out, payload, local, scratch):
+    def wrap(first, inside, last):
+        return jnp.concatenate([first, inside, last], axis=0)
+
+    own_region = regions[...].astype(jnp.float32)
+    own_mobile = 1.0 - dirichlet[...].astype(jnp.float32)
+    own_film = jnp.where(regions[...] == 0, activity[...], 0.0)
+    region = wrap(low[15], own_region, high[15])
+    film = wrap(low[16], own_film, high[16])
+    mobile = wrap(low[17], own_mobile, high[17])
+    first, last, between = slice(0, ROWS), slice(7 * ROWS, 8 * ROWS), slice(ROWS, 7 * ROWS)
+    below = outer_new1([fine[9 + k, planes(0, 1)] for k in range(3)], low)
+    above = outer_new1([fine[9 + k, planes(7, 8)] for k in range(3)], high)
+    low_rest, low_w2 = outer_rest(low)
+    high_rest, high_w2 = outer_rest(high)
+    new1, own1 = [], []
+    for k in range(3):
+        v = fine[k]
+        ends = []
+        for at, side in ((first, low), (last, high)):
+            factor = own_mobile[at] * inverse(own_mobile[at], k) * conduct(own_region[at], k)
+            ends.append(v[at] + factor * combine(Q1, [side[m * 3 + k] for m in range(3)]))
+        v = jnp.concatenate([ends[0], v[between], ends[1]], axis=0)
+        own1.append(v)
+        new1_out[k] = v
+        new1.append(wrap(below[k], v, above[k]))
+    flow1 = H * current(new1, film)
+    new2, own2 = [], []
+    for k in range(3):
+        w2 = wrap(low_w2[k], fine[3 + k], high_w2[k])
+        v2 = H * new1[k] + w2
+        lap2 = laplace(jnp.concatenate([low[12 + k], v2, high[12 + k]], axis=0))
+        rest = wrap(low_rest[k], fine[6 + k], high_rest[k])
+        inner = conduct(region, k) * lap2 + SIGNS[k] * flow1 + rest
+        v = (new1[k] + mobile * inner) * inverse(mobile, k)
+        new2.append(v)
+        own2.append(v[ROWS:-ROWS])
+        new2_out[k] = own2[k]
+    flow3 = Q3[0] * fine[12] + (Q3[1] / H) * flow1[ROWS:-ROWS] + Q3[2] * current(own2, own_film)
+    integral, one = [], []
+    for k in range(3):
+        ends = [combine(Q3, [side[k], new1[k][at], new2[k][at]]) for side, at in ((low, slice(0, ROWS)), (high, slice(9 * ROWS, 10 * ROWS)))]
+        v3 = combine(Q3, [u[k], own1[k], own2[k]])
+        lap3 = laplace(wrap(ends[0], v3, ends[1]))
+        force = own_mobile * (conduct(own_region, k) * lap3 + SIGNS[k] * flow3 - RATES[k] * v3)
+        integral.append(restrict(scratch, k, force))
+        one.append(restrict(scratch, 3 + k, own2[k]))
+    a, b, cmobile, cfilm = (coarse[i] for i in range(4))
+    zero = [coarse[5 + k] for k in range(3)]
     slope = a * zero[0] + b * (zero[1] - 0.5 * zero[2])
-    flow_c = (cfilm * zero[0] * (fwd - bwd)) + current(one, cfilm)
+    flow_c = coarse[4] + current(one, cfilm)
     is_first = lax.axis_index("tm") == 0
     local[3] = a
     local[4] = b
@@ -193,7 +272,7 @@
     out[pl.ds(1, 64, stride=2)] = states[2]
 
 
-def finish_kernel(u, new1, new2, behind, local, starts, out, scratch):
+def finish_kernel(u, new1, new2, behind, local, starts, far, out, scratch, sems):
     is_first = lax.axis_index("tm") == 0
     half = lax.broadcasted_iota(jnp.int32, (32, LANES), 1) < 64
     rows = [starts[pl.ds(i, 32, stride=4)] for i in range(4)]
@@ -211,6 +290,7 @@
         wide = scratch[i].reshape(4, 1, ROWS, LANES)
         return jnp.broadcast_to(wide, (4, 2, ROWS, LANES)).reshape(8 * ROWS, LANES)
 
+    copies = []
     for k in range(3):
         end = (start[k] + local[k] + SIGNS[k] * t) / (1.0 + (DT * RATES[k]) * local[5])
         delta_zero = start[k] - local[6 + k]
@@ -219,40 +299,59 @@
         pairs = head.reshape(4, 2, ROWS, LANES)
         scratch[9 + k] = (pairs[:, 0] + pairs[:, 1]).reshape(4 * ROWS, LANES)
         coarse = 0.25 * (scratch[9 + k, pl.ds(0, 32, stride=2)] + scratch[9 + k, pl.ds(1, 32, stride=2)])
-        out[k] = head + prolong(3 * k, start[k] - coarse)
-        out[3 + k] = new1[k] + prolong(3 * k + 1, 0.5 * (delta_zero + delta_one))
-        out[6 + k] = new2[k] + prolong(3 * k + 2, delta_one)
-
-
-def call(kernel, outs, scratch, *args):
+        parts = (
+            head + prolong(3 * k, start[k] - coarse),
+            new1[k] + prolong(3 * k + 1, 0.5 * (delta_zero + delta_one)),
+            new2[k] + prolong(3 * k + 2, delta_one),
+        )
+        for m in range(3):
+            out[3 * m + k] = parts[m]
+            copy = pltpu.make_async_copy(out.at[3 * m + k], far.at[3 * m + k], sems.at[3 * m + k])
+            copy.start()
+            copies.append(copy)
+    for copy in copies:
+        copy.wait()
+
+
+def call(kernel, outs, scratch, *args, near=True, near_out=True, cost=0, mib=32):
+    vmem, hbm = pl.BlockSpec(memory_space=pltpu.VMEM), pl.BlockSpec(memory_space=pltpu.HBM)
     return pl.pallas_call(
         kernel,
         out_shape=[jax.ShapeDtypeStruct(s, jnp.float32) for s in outs],
-        in_specs=[pl.BlockSpec(memory_space=pltpu.VMEM)] * len(args),
-        out_specs=[pl.BlockSpec(memory_space=pltpu.VMEM)] * len(outs),
-        scratch_shapes=[pltpu.VMEM(s, jnp.float32) for s in scratch],
-        compiler_params=pltpu.CompilerParams(vmem_limit_bytes=32 * 1024 * 1024),
+        in_specs=[vmem if near else hbm] * len(args),
+        out_specs=[vmem if near_out else hbm] * len(outs),
+        scratch_shapes=scratch,
+        compiler_params=pltpu.CompilerParams(vmem_limit_bytes=mib * 1024 * 1024),
+        cost_estimate=pl.CostEstimate(flops=cost, bytes_accessed=cost, transcendentals=0),
     )(*args)
+
+
+def f32(*shape):
+    return pltpu.VMEM(shape, jnp.float32)
 
 
 def on_device(fine_nodes, regions, activity, dirichlet):
     u = fine_nodes.reshape(9, 128, LANES)
     tables = [v.reshape(128, LANES) for v in (regions, activity, dirichlet)]
     edge = (EDGE, ROWS, LANES)
-    to_low, to_high = call(edge_kernel, [edge, edge], [], u, *tables)
+    buffers = [f32(2, 9, 48, LANES), pltpu.VMEM((2, 2, 32, LANES), jnp.int32), f32(2, 32, LANES), pltpu.SemaphoreType.DMA((8,))]
+    pinned = [pltpu.with_memory_space_constraint(v, pltpu.HBM) for v in (u, *tables)]
+    to_low, to_high = call(edge_kernel, [edge, edge], buffers, *pinned, near=False, cost=1000000, mib=32)
     count = lax.axis_size("space")
     low = lax.ppermute(to_high, "space", [(i, i + 1) for i in range(count - 1)])
     high = lax.ppermute(to_low, "space", [(i + 1, i) for i in range(count - 1)])
+    fine, coarse = call(inner_kernel, [(13, 128, LANES), (8, 32, LANES)], [f32(5, 64, LANES)], u, *tables, cost=3000000)
     brick = (3, 128, LANES)
     new1, new2, payload, local = call(
-        main_kernel, [brick, brick, (256, LANES), (12, 32, LANES)], [(11, 64, LANES)], u, *tables, low, high
+        main_kernel, [brick, brick, (256, LANES), (12, 32, LANES)], [f32(6, 64, LANES)], u, *tables, fine, coarse, low, high, cost=3000000
     )
     slices = lax.axis_size("tm")
     behind = lax.ppermute(new2, "tm", [(i, i + 1) for i in range(slices - 1)])
     arrived = lax.all_to_all(payload, "tm", 0, 0, tiled=True)
-    (starts,) = call(scan_kernel, [(128, LANES)], [(256, LANES), (3, 64, LANES)], arrived, local)
+    (starts,) = call(scan_kernel, [(128, LANES)], [f32(256, LANES), f32(3, 64, LANES)], arrived, local, cost=1000000)
     starts = lax.all_to_all(starts, "tm", 0, 0, tiled=True)
-    (out,) = call(finish_kernel, [(9, 128, LANES)], [(12, 64, LANES)], u, new1, new2, behind, local, starts)
+    outs, scratch = (9, 128, LANES), [f32(9, 128, LANES), f32(12, 64, LANES), pltpu.SemaphoreType.DMA((9,))]
+    (out,) = call(finish_kernel, [outs], scratch, u, new1, new2, behind, local, starts, near_out=False, cost=1000000)
     return out.reshape(fine_nodes.shape)
 
 

time: 68.1 us -> 65.1 us (0.956)
  local copies, waits for them, and re-layouts: 3.58 us -> 0.02 us
  Pallas kernels: 4.23 us -> 5.57 us
    unnamed x10 -> x8, local copies, waits for them, and re-layouts: 3.58 us -> 0.02 us
    pallas_call x4 -> x5, Pallas kernels: 4.23 us -> 5.57 us  [call(): pl.pallas_call(kernel, out_shape=[jax.ShapeDtypeStruct(s, jnp.float32) fo...]
  transfers between devices with their start and end apart: 5 -> 5, of which waited for: 4 -> 4; matrix products, arithmetic and copies ran while one was open for 0% -> 0% of each run, Pallas kernels for 2% -> 3%
where the time goes in v2:
time: 65.1 us; the launch traced here: 64.8 us
  starting transfers between devices  32.4 us (50%)
  waiting for transfers between devices  26.7 us (41%)
  Pallas kernels  5.57 us (9%)
    all_to_all x1, starting transfers between devices, on_device(): arrived = lax.all_to_all(payload, 'tm', 0, 0, tiled=True)  17.1 us
    all_to_all x1, waiting for transfers between devices, on_device(): starts = lax.all_to_all(starts, 'tm', 0, 0, tiled=True)  12.2 us
    all_to_all x1, waiting for transfers between devices, on_device(): arrived = lax.all_to_all(payload, 'tm', 0, 0, tiled=True)  8.78 us
    all_to_all x1, starting transfers between devices, on_device(): starts = lax.all_to_all(starts, 'tm', 0, 0, tiled=True)  5.59 us
    pallas_call x5, Pallas kernels, call(): pl.pallas_call(kernel, out_shape=[jax.ShapeDtypeStruct(s, jnp.float32) fo...  5.57 us
    ppermute x1, waiting for transfers between devices, on_device(): high = lax.ppermute(to_low, 'space', [(i + 1, i) for i in range(count - 1)])  4.92 us
    ppermute x1, starting transfers between devices, on_device(): behind = lax.ppermute(new2, 'tm', [(i, i + 1) for i in range(slices - 1)])  4.44 us
    ppermute x1, starting transfers between devices, on_device(): low = lax.ppermute(to_high, 'space', [(i, i + 1) for i in range(count - 1)])  3.12 us
  transfers between devices with their start and end apart: 5, of which 4 were waited for; matrix products, arithmetic and copies ran while one was open for 0% of the time, Pallas kernels for 3%

profile of v2, /device:TPU:7, one launch (start us, length us, event | category | flops | bytes accessed | tf_op | source)
XLA Modules:
  0.0 64.8 jit_solution(16102801352290326809)
XLA Ops:
  0.0 0.0 copy-start
  0.0 0.0 copy-start.1
  0.0 0.0 copy-start.2
  0.0 0.0 copy-start.3
  0.0 1.4 %shard_map.47 = (f32[18,16,128]{2,1,0:T(8,128)S(1)}, f32[18,16,128]{2,1,0:T(8,128)S(1)}) custom-call(f32[9,128,128]{2,1,0:T(8,128)} %bitcast.9, s32[128,128]{1,0:T(8,128)} %bitcast.13, f32[128,128]{1,0:T(8,128)} %bitcast.16, s32[128,128]{1,0:T(8,128)} %bitcast.19), custom_call_target="tpu_custom_call" | custom-call | flops 1000000 | bytes 1000000 | tf_op jit(solution)/shard_map/pallas_call | solution.py:318
  1.4 3.1 %collective-permute-start = (f32[18,16,128]{2,1,0:T(8,128)S(1)}, f32[18,16,128]{2,1,0:T(8,128)S(1)}, u32[]{:S(2)}, u32[]{:S(2)}) collective-permute-start(f32[18,16,128]{2,1,0:T(8,128)S(1)} %get-tuple-element.15), channel_id=1, source_target_pairs={{0,1},{1,2},{2,3},{3,4},{4,5},{5,6},{6,7},{8,9},{9,10},{10,11},{11... | collective-permute-start | bytes 442376 | tf_op jit(solution)/shard_map/ppermute | solution.py:341
  4.5 2.2 %collective-permute-start.1 = (f32[18,16,128]{2,1,0:T(8,128)S(1)}, f32[18,16,128]{2,1,0:T(8,128)S(1)}, u32[]{:S(2)}, u32[]{:S(2)}) collective-permute-start(f32[18,16,128]{2,1,0:T(8,128)S(1)} %get-tuple-element.16), channel_id=1, source_target_pairs={{1,0},{2,1},{3,2},{4,3},{5,4},{6,5},{7,6},{9,8},{10,9},{11,10},{12... | collective-permute-start | bytes 442376 | tf_op jit(solution)/shard_map/ppermute | solution.py:342
  6.7 0.0 copy-done
  6.7 0.0 copy-done.1
  6.7 0.0 copy-done.2
  6.7 0.0 copy-done.3
  6.7 0.5 shard_map.46
  7.2 0.8 %collective-permute-done.low = f32[18,16,128]{2,1,0:T(8,128)S(1)} collective-permute-done((f32[18,16,128]{2,1,0:T(8,128)S(1)}, f32[18,16,128]{2,1,0:T(8,128)S(1)}, u32[]{:S(2)}, u32[]{:S(2)}) %collective-permute-start) | collective-permute-done | bytes 147488 | tf_op jit(solution)/shard_map/ppermute | solution.py:341
  8.0 4.9 %collective-permute-done.1.high = f32[18,16,128]{2,1,0:T(8,128)S(1)} collective-permute-done((f32[18,16,128]{2,1,0:T(8,128)S(1)}, f32[18,16,128]{2,1,0:T(8,128)S(1)}, u32[]{:S(2)}, u32[]{:S(2)}) %collective-permute-start.1) | collective-permute-done | bytes 147488 | tf_op jit(solution)/shard_map/ppermute | solution.py:342
  12.9 1.4 %shard_map.48 = (f32[3,128,128]{2,1,0:T(8,128)S(1)}, f32[3,128,128]{2,1,0:T(8,128)S(1)}, f32[256,128]{1,0:T(8,128)}, f32[12,32,128]{2,1,0:T(8,128)S(1)}) custom-call(f32[9,128,128]{2,1,0:T(8,128)S(1)} %bitcast.11, s32[128,128]{1,0:T(8,128)S(1)} %bitcast.15, f32[128,128]{1,0:T(8,128)S(1)} %bitcast.18, s32[128,128]{1,0:T(8,128)S(1)} %bitcast.21, ...), custom_call_target="tpu_custom_call" | custom-call | flops 3000000 | bytes 3000000 | tf_op jit(solution)/shard_map/pallas_call | solution.py:318
  14.4 17.1 %all-to-all-start = ((f32[64,4,128]{2,1,0:T(4,128)}), f32[64,4,128]{2,1,0:T(4,128)S(1)}, u32[]{:S(2)}, u32[]{:S(2)}) async-start(f32[64,4,128]{2,1,0:T(4,128)} %bitcast.4), calls=%async_computation | async-start | bytes 262144 | tf_op jit(solution)/shard_map/all_to_all | solution.py:350
  31.5 4.4 %collective-permute-start.2 = (f32[3,128,128]{2,1,0:T(8,128)S(1)}, f32[3,128,128]{2,1,0:T(8,128)S(1)}, u32[]{:S(2)}, u32[]{:S(2)}) collective-permute-start(f32[3,128,128]{2,1,0:T(8,128)S(1)} %get-tuple-element.18.new2), channel_id=1, source_target_pairs={{0,8},{8,16},{16,24},{24,32},{32,40},{40,48},{48,56},{56,64},{64,7... | collective-permute-start | bytes 589832 | tf_op jit(solution)/shard_map/ppermute | solution.py:349
  35.9 8.8 %all-to-all-done = f32[64,4,128]{2,1,0:T(4,128)S(1)} async-done(((f32[64,4,128]{2,1,0:T(4,128)}), f32[64,4,128]{2,1,0:T(4,128)S(1)}, u32[]{:S(2)}, u32[]{:S(2)}) %all-to-all-start) | async-done | bytes 131104 | tf_op jit(solution)/shard_map/all_to_all | solution.py:350
  44.7 1.3 %shard_map.49 = f32[128,128]{1,0:T(8,128)} custom-call(f32[256,128]{1,0:T(8,128)S(1)} %bitcast.22, f32[12,32,128]{2,1,0:T(8,128)S(1)} %get-tuple-element.19.local), custom_call_target="tpu_custom_call" | custom-call | flops 1000000 | bytes 1000000 | tf_op jit(solution)/shard_map/pallas_call | solution.py:318
  46.0 5.6 %all-to-all-start.1 = ((f32[64,2,128]{2,1,0:T(2,128)}), f32[64,2,128]{2,1,0:T(2,128)S(1)}, u32[]{:S(2)}, u32[]{:S(2)}) async-start(f32[64,2,128]{2,1,0:T(2,128)} %bitcast.6), calls=%async_computation.1 | async-start | bytes 131072 | tf_op jit(solution)/shard_map/all_to_all | solution.py:352
  51.6 0.0 collective-permute-done.2.behind
  51.6 12.2 %all-to-all-done.1 = f32[64,2,128]{2,1,0:T(2,128)S(1)} async-done(((f32[64,2,128]{2,1,0:T(2,128)}), f32[64,2,128]{2,1,0:T(2,128)S(1)}, u32[]{:S(2)}, u32[]{:S(2)}) %all-to-all-start.1) | async-done | bytes 65568 | tf_op jit(solution)/shard_map/all_to_all | solution.py:352
  63.8 1.0 %shard_map.50 = f32[9,128,128]{2,1,0:T(8,128)} custom-call(f32[9,128,128]{2,1,0:T(8,128)S(1)} %bitcast.12, f32[3,128,128]{2,1,0:T(8,128)S(1)} %get-tuple-element.17.new1, f32[3,128,128]{2,1,0:T(8,128)S(1)} %get-tuple-element.18.new2, f32[3,128,128]{2,1,0:T(8,128)S(1)} %collective-permute-done.2.behind, f32[12,32,128]{2,1,0:T(8,128)S(1)} %get-tuple-element.19.local, ...), custom_call_target="tpu_custom_call" | custom-call | flops 1000000 | bytes 1000000 | tf_op jit(solution)/shard_map/pallas_call | solution.py:318
Async XLA Ops:
  0.0 6.7 %copy-start = (f32[1,3,3,8,16,128]{5,4,3,2,1,0:T(8,128)S(1)}, f32[1,3,3,8,16,128]{5,4,3,2,1,0:T(8,128)}, u32[]{:S(2)}) copy-start(f32[1,3,3,8,16,128]{5,4,3,2,1,0:T(8,128)} %param.4) | copy-start | bytes 1769476
  0.0 6.7 %copy-start.1 = (s32[8,16,128]{2,1,0:T(8,128)S(1)}, s32[8,16,128]{2,1,0:T(8,128)}, u32[]{:S(2)}) copy-start(s32[8,16,128]{2,1,0:T(8,128)} %param.5) | copy-start | bytes 196612
  0.0 6.7 %copy-start.2 = (f32[8,16,128]{2,1,0:T(8,128)S(1)}, f32[8,16,128]{2,1,0:T(8,128)}, u32[]{:S(2)}) copy-start(f32[8,16,128]{2,1,0:T(8,128)} %param.6) | copy-start | bytes 196612
  0.0 6.7 %copy-start.3 = (s32[8,16,128]{2,1,0:T(8,128)S(1)}, s32[8,16,128]{2,1,0:T(8,128)}, u32[]{:S(2)}) copy-start(s32[8,16,128]{2,1,0:T(8,128)} %param.7) | copy-start | bytes 196612
  1.4 6.6 %collective-permute-start = (f32[18,16,128]{2,1,0:T(8,128)S(1)}, f32[18,16,128]{2,1,0:T(8,128)S(1)}, u32[]{:S(2)}, u32[]{:S(2)}) collective-permute-start(f32[18,16,128]{2,1,0:T(8,128)S(1)} %get-tuple-element.15), channel_id=1, source_target_pairs={{0,1},{1,2},{2,3},{3,4},{4,5},{5,6},{6,7},{8,9},{9,10},{10,11},{11... | collective-permute-start | bytes 442376 | tf_op jit(solution)/shard_map/ppermute | solution.py:341
  4.5 8.4 %collective-permute-start.1 = (f32[18,16,128]{2,1,0:T(8,128)S(1)}, f32[18,16,128]{2,1,0:T(8,128)S(1)}, u32[]{:S(2)}, u32[]{:S(2)}) collective-permute-start(f32[18,16,128]{2,1,0:T(8,128)S(1)} %get-tuple-element.16), channel_id=1, source_target_pairs={{1,0},{2,1},{3,2},{4,3},{5,4},{6,5},{7,6},{9,8},{10,9},{11,10},{12... | collective-permute-start | bytes 442376 | tf_op jit(solution)/shard_map/ppermute | solution.py:342
  14.4 30.3 %all-to-all-start = ((f32[64,4,128]{2,1,0:T(4,128)}), f32[64,4,128]{2,1,0:T(4,128)S(1)}, u32[]{:S(2)}, u32[]{:S(2)}) async-start(f32[64,4,128]{2,1,0:T(4,128)} %bitcast.4), calls=%async_computation | async-start | bytes 262144 | tf_op jit(solution)/shard_map/all_to_all | solution.py:350
  31.5 20.1 %collective-permute-start.2 = (f32[3,128,128]{2,1,0:T(8,128)S(1)}, f32[3,128,128]{2,1,0:T(8,128)S(1)}, u32[]{:S(2)}, u32[]{:S(2)}) collective-permute-start(f32[3,128,128]{2,1,0:T(8,128)S(1)} %get-tuple-element.18.new2), channel_id=1, source_target_pairs={{0,8},{8,16},{16,24},{24,32},{32,40},{40,48},{48,56},{56,64},{64,7... | collective-permute-start | bytes 589832 | tf_op jit(solution)/shard_map/ppermute | solution.py:349
  46.0 17.8 %all-to-all-start.1 = ((f32[64,2,128]{2,1,0:T(2,128)}), f32[64,2,128]{2,1,0:T(2,128)S(1)}, u32[]{:S(2)}, u32[]{:S(2)}) async-start(f32[64,2,128]{2,1,0:T(2,128)} %bitcast.6), calls=%async_computation.1 | async-start | bytes 131072 | tf_op jit(solution)/shard_map/all_to_all | solution.py:352

commit v3 on v2

--- a/solution.py
+++ b/solution.py
@@ -178,7 +178,7 @@
     return rest, [w2_of(old, k) for k in range(3)]
 
 
-def main_kernel(u, regions, activity, dirichlet, fine, coarse, low, high, new1_out, new2_out, payload, local, scratch):
+def main_kernel(u, regions, activity, dirichlet, fine, coarse, low, high, new1_out, lower_out, upper_out, payload, local, scratch):
     def wrap(first, inside, last):
         return jnp.concatenate([first, inside, last], axis=0)
 
@@ -215,7 +215,8 @@
         v = (new1[k] + mobile * inner) * inverse(mobile, k)
         new2.append(v)
         own2.append(v[ROWS:-ROWS])
-        new2_out[k] = own2[k]
+        lower_out[k] = own2[k][: 4 * ROWS]
+        upper_out[k] = own2[k][4 * ROWS :]
     flow3 = Q3[0] * fine[12] + (Q3[1] / H) * flow1[ROWS:-ROWS] + Q3[2] * current(own2, own_film)
     integral, one = [], []
     for k in range(3):
@@ -247,10 +248,8 @@
     half = lane < 64
     for m in range(3):
         x, y = sent[2 * m], sent[2 * m + 1]
-        payload[pl.ds(m, 32, stride=8)] = jnp.where(half, x, pltpu.roll(y, 64, 1))
-        payload[pl.ds(4 + m, 32, stride=8)] = jnp.where(half, pltpu.roll(x, 64, 1), y)
-    payload[pl.ds(3, 32, stride=8)] = jnp.zeros_like(a)
-    payload[pl.ds(7, 32, stride=8)] = jnp.zeros_like(a)
+        payload[pl.ds(m, 32, stride=6)] = jnp.where(half, x, pltpu.roll(y, 64, 1))
+        payload[pl.ds(3 + m, 32, stride=6)] = jnp.where(half, pltpu.roll(x, 64, 1), y)
 
 
 def scan_kernel(arrived, local, out, rolled, states):
@@ -263,8 +262,8 @@
     for n in range(64):
         for k in range(3):
             states[k, pl.ds(n, 1)] = v[k]
-        term = [arrived[pl.ds(4 * n, 1)], rolled[pl.ds(4 * n, 1)], arrived[pl.ds(4 * n + 1, 1)]]
-        a, b = rolled[pl.ds(4 * n + 1, 1)], arrived[pl.ds(4 * n + 2, 1)]
+        term = [arrived[pl.ds(3 * n, 1)], rolled[pl.ds(3 * n, 1)], arrived[pl.ds(3 * n + 1, 1)]]
+        a, b = rolled[pl.ds(3 * n + 1, 1)], arrived[pl.ds(3 * n + 2, 1)]
         t = a * v[0] + b * (v[1] - 0.5 * v[2])
         v = [keep[k] * (v[k] + term[k] + SIGNS[k] * t) for k in range(3)]
     half = lax.broadcasted_iota(jnp.int32, (64, LANES), 1) < 64
@@ -272,7 +271,7 @@
     out[pl.ds(1, 64, stride=2)] = states[2]
 
 
-def finish_kernel(u, new1, new2, behind, local, starts, far, out, scratch, sems):
+def finish_kernel(u, new1, lower, upper, lower_behind, upper_behind, local, starts, far, out, scratch, sems):
     is_first = lax.axis_index("tm") == 0
     half = lax.broadcasted_iota(jnp.int32, (32, LANES), 1) < 64
     rows = [starts[pl.ds(i, 32, stride=4)] for i in range(4)]
@@ -295,14 +294,15 @@
         end = (start[k] + local[k] + SIGNS[k] * t) / (1.0 + (DT * RATES[k]) * local[5])
         delta_zero = start[k] - local[6 + k]
         delta_one = end - local[9 + k]
-        head = jnp.where(is_first, u[k], behind[k])
+        new2 = jnp.concatenate([lower[k], upper[k]], axis=0)
+        head = jnp.where(is_first, u[k], jnp.concatenate([lower_behind[k], upper_behind[k]], axis=0))
         pairs = head.reshape(4, 2, ROWS, LANES)
         scratch[9 + k] = (pairs[:, 0] + pairs[:, 1]).reshape(4 * ROWS, LANES)
         coarse = 0.25 * (scratch[9 + k, pl.ds(0, 32, stride=2)] + scratch[9 + k, pl.ds(1, 32, stride=2)])
         parts = (
             head + prolong(3 * k, start[k] - coarse),
             new1[k] + prolong(3 * k + 1, 0.5 * (delta_zero + delta_one)),
-            new2[k] + prolong(3 * k + 2, delta_one),
+            new2 + prolong(3 * k + 2, delta_one),
         )
         for m in range(3):
             out[3 * m + k] = parts[m]
@@ -341,17 +341,18 @@
     low = lax.ppermute(to_high, "space", [(i, i + 1) for i in range(count - 1)])
     high = lax.ppermute(to_low, "space", [(i + 1, i) for i in range(count - 1)])
     fine, coarse = call(inner_kernel, [(13, 128, LANES), (8, 32, LANES)], [f32(5, 64, LANES)], u, *tables, cost=3000000)
-    brick = (3, 128, LANES)
-    new1, new2, payload, local = call(
-        main_kernel, [brick, brick, (256, LANES), (12, 32, LANES)], [f32(6, 64, LANES)], u, *tables, fine, coarse, low, high, cost=3000000
+    half = (3, 64, LANES)
+    new1, lower, upper, payload, local = call(
+        main_kernel, [(3, 128, LANES), half, half, (192, LANES), (12, 32, LANES)], [f32(6, 64, LANES)], u, *tables, fine, coarse, low, high, cost=3000000
     )
-    slices = lax.axis_size("tm")
-    behind = lax.ppermute(new2, "tm", [(i, i + 1) for i in range(slices - 1)])
-    arrived = lax.all_to_all(payload, "tm", 0, 0, tiled=True)
-    (starts,) = call(scan_kernel, [(128, LANES)], [f32(256, LANES), f32(3, 64, LANES)], arrived, local, cost=1000000)
+    nexts = [(i, i + 1) for i in range(lax.axis_size("tm") - 1)]
+    lower_behind = lax.ppermute(lower, "tm", nexts)
+    upper_behind = lax.ppermute(upper, "tm", nexts)
+    arrived = lax.all_to_all(payload.reshape(64, 1, 3 * LANES), "tm", 0, 0, tiled=True).reshape(192, LANES)
+    (starts,) = call(scan_kernel, [(128, LANES)], [f32(192, LANES), f32(3, 64, LANES)], arrived, local, cost=1000000)
     starts = lax.all_to_all(starts, "tm", 0, 0, tiled=True)
     outs, scratch = (9, 128, LANES), [f32(9, 128, LANES), f32(12, 64, LANES), pltpu.SemaphoreType.DMA((9,))]
-    (out,) = call(finish_kernel, [outs], scratch, u, new1, new2, behind, local, starts, near_out=False, cost=1000000)
+    (out,) = call(finish_kernel, [outs], scratch, u, new1, lower, upper, lower_behind, upper_behind, local, starts, near_out=False, cost=1000000)
     return out.reshape(fine_nodes.shape)
 
 

time: 65.1 us -> 62.5 us (0.960)
  blocking collectives: 0 us -> 29.5 us
  starting transfers between devices: 32.4 us -> 16.2 us
  waiting for transfers between devices: 26.7 us -> 11.5 us
  Pallas kernels: 5.57 us -> 4.9 us
    all_to_all x0 -> x1, blocking collectives: none -> 29.5 us  [on_device(): lax.all_to_all(payload.reshape(64, 1, 3 * LANES), 'tm', 0, 0, tiled=True)]
    all_to_all x1 -> x0, starting transfers between devices: 17.1 us -> none  [on_device(): arrived = lax.all_to_all(payload, 'tm', 0, 0, tiled=True)]
    all_to_all x1 -> x0, waiting for transfers between devices: 8.78 us -> none  [on_device(): arrived = lax.all_to_all(payload, 'tm', 0, 0, tiled=True)]
    all_to_all x1, waiting for transfers between devices: 12.2 us -> 4.04 us  [on_device(): starts = lax.all_to_all(starts, 'tm', 0, 0, tiled=True)]
    ppermute x1 -> x2, starting transfers between devices: 4.44 us -> 6.5 us  [the longest x1 4.45 us: on_device(): lower_behind = lax.ppermute(lower, 'tm', nexts)]
    ppermute x1 -> x2, waiting for transfers between devices: 0.01 us -> 1.71 us  [the longest x1 1.05 us: on_device(): upper_behind = lax.ppermute(upper, 'tm', nexts)]
    all_to_all x1, starting transfers between devices: 5.59 us -> 4.44 us  [on_device(): starts = lax.all_to_all(starts, 'tm', 0, 0, tiled=True)]
    pallas_call x5, Pallas kernels: 5.57 us -> 4.9 us  [call(): pl.pallas_call(kernel, out_shape=[jax.ShapeDtypeStruct(s, jnp.float32) fo...]
  transfers between devices with their start and end apart: 5 -> 5, of which waited for: 4 -> 5; matrix products, arithmetic and copies ran while one was open for 0% -> 0% of each run, Pallas kernels for 3% -> 1%
where the time goes in v3:
time: 62.5 us; the launch traced here: 62.2 us
  blocking collectives  29.5 us (47%)
  starting transfers between devices  16.2 us (26%)
  waiting for transfers between devices  11.5 us (18%)
  Pallas kernels  4.9 us (8%)
    all_to_all x1, blocking collectives, on_device(): lax.all_to_all(payload.reshape(64, 1, 3 * LANES), 'tm', 0, 0, tiled=True)  29.5 us
    ppermute x1, waiting for transfers between devices, on_device(): high = lax.ppermute(to_low, 'space', [(i + 1, i) for i in range(count - 1)])  4.92 us
    pallas_call x5, Pallas kernels, call(): pl.pallas_call(kernel, out_shape=[jax.ShapeDtypeStruct(s, jnp.float32) fo...  4.9 us
    ppermute x1, starting transfers between devices, on_device(): lower_behind = lax.ppermute(lower, 'tm', nexts)  4.45 us
    all_to_all x1, starting transfers between devices, on_device(): starts = lax.all_to_all(starts, 'tm', 0, 0, tiled=True)  4.44 us
    all_to_all x1, waiting for transfers between devices, on_device(): starts = lax.all_to_all(starts, 'tm', 0, 0, tiled=True)  4.04 us
    ppermute x1, starting transfers between devices, on_device(): low = lax.ppermute(to_high, 'space', [(i, i + 1) for i in range(count - 1)])  3.12 us
    ppermute x1, starting transfers between devices, on_device(): high = lax.ppermute(to_low, 'space', [(i + 1, i) for i in range(count - 1)])  2.16 us
  transfers between devices with their start and end apart: 5, of which 5 were waited for; matrix products, arithmetic and copies ran while one was open for 0% of the time, Pallas kernels for 1%

profile of v3, /device:TPU:7, one launch (start us, length us, event | category | flops | bytes accessed | tf_op | source)
XLA Modules:
  0.0 62.2 jit_solution(10806778454781893799)
XLA Ops:
  0.0 0.0 copy-start
  0.0 0.0 copy-start.1
  0.0 0.0 copy-start.2
  0.0 0.0 copy-start.3
  0.0 1.4 %shard_map.47 = (f32[18,16,128]{2,1,0:T(8,128)S(1)}, f32[18,16,128]{2,1,0:T(8,128)S(1)}) custom-call(f32[9,128,128]{2,1,0:T(8,128)} %bitcast.9, s32[128,128]{1,0:T(8,128)} %bitcast.13, f32[128,128]{1,0:T(8,128)} %bitcast.16, s32[128,128]{1,0:T(8,128)} %bitcast.19), custom_call_target="tpu_custom_call" | custom-call | flops 1000000 | bytes 1000000 | tf_op jit(solution)/shard_map/pallas_call | solution.py:318
  1.4 3.1 %collective-permute-start = (f32[18,16,128]{2,1,0:T(8,128)S(1)}, f32[18,16,128]{2,1,0:T(8,128)S(1)}, u32[]{:S(2)}, u32[]{:S(2)}) collective-permute-start(f32[18,16,128]{2,1,0:T(8,128)S(1)} %get-tuple-element.16), channel_id=1, source_target_pairs={{0,1},{1,2},{2,3},{3,4},{4,5},{5,6},{6,7},{8,9},{9,10},{10,11},{11... | collective-permute-start | bytes 442376 | tf_op jit(solution)/shard_map/ppermute | solution.py:341
  4.5 2.2 %collective-permute-start.1 = (f32[18,16,128]{2,1,0:T(8,128)S(1)}, f32[18,16,128]{2,1,0:T(8,128)S(1)}, u32[]{:S(2)}, u32[]{:S(2)}) collective-permute-start(f32[18,16,128]{2,1,0:T(8,128)S(1)} %get-tuple-element.17), channel_id=1, source_target_pairs={{1,0},{2,1},{3,2},{4,3},{5,4},{6,5},{7,6},{9,8},{10,9},{11,10},{12... | collective-permute-start | bytes 442376 | tf_op jit(solution)/shard_map/ppermute | solution.py:342
  6.7 0.0 copy-done
  6.7 0.0 copy-done.1
  6.7 0.0 copy-done.2
  6.7 0.0 copy-done.3
  6.7 0.5 shard_map.46
  7.2 0.8 %collective-permute-done.low = f32[18,16,128]{2,1,0:T(8,128)S(1)} collective-permute-done((f32[18,16,128]{2,1,0:T(8,128)S(1)}, f32[18,16,128]{2,1,0:T(8,128)S(1)}, u32[]{:S(2)}, u32[]{:S(2)}) %collective-permute-start) | collective-permute-done | bytes 147488 | tf_op jit(solution)/shard_map/ppermute | solution.py:341
  8.0 4.9 %collective-permute-done.1.high = f32[18,16,128]{2,1,0:T(8,128)S(1)} collective-permute-done((f32[18,16,128]{2,1,0:T(8,128)S(1)}, f32[18,16,128]{2,1,0:T(8,128)S(1)}, u32[]{:S(2)}, u32[]{:S(2)}) %collective-permute-start.1) | collective-permute-done | bytes 147488 | tf_op jit(solution)/shard_map/ppermute | solution.py:342
  12.9 0.8 %shard_map.48 = (f32[3,128,128]{2,1,0:T(8,128)S(1)}, f32[3,64,128]{2,1,0:T(8,128)S(1)}, f32[3,64,128]{2,1,0:T(8,128)S(1)}, f32[192,128]{1,0:T(8,128)S(1)}, f32[12,32,128]{2,1,0:T(8,128)S(1)}) custom-call(f32[9,128,128]{2,1,0:T(8,128)S(1)} %bitcast.11, s32[128,128]{1,0:T(8,128)S(1)} %bitcast.15, f32[128,128]{1,0:T(8,128)S(1)} %bitcast.18, ...), custom_call_target="tpu_custom_call" | custom-call | flops 3000000 | bytes 3000000 | tf_op jit(solution)/shard_map/pallas_call | solution.py:318
  13.7 29.5 %all_to_all.16 = f32[64,1,384]{2,1,0:T(1,128)S(1)} all-to-all(f32[64,1,384]{2,1,0:T(1,128)S(1)} %bitcast.24), channel_id=1, replica_groups=mesh['tm'=64,'space'=8] {'tm'}, dimensions={0} | all-to-all | bytes 196608 | tf_op jit(solution)/shard_map/all_to_all | solution.py:351
  43.2 1.3 %shard_map.49 = f32[128,128]{1,0:T(8,128)} custom-call(f32[192,128]{1,0:T(8,128)S(1)} %bitcast.22, f32[12,32,128]{2,1,0:T(8,128)S(1)} %get-tuple-element.21.local), custom_call_target="tpu_custom_call" | custom-call | flops 1000000 | bytes 1000000 | tf_op jit(solution)/shard_map/pallas_call | solution.py:318
  44.5 4.4 %all-to-all-start.1 = ((f32[64,2,128]{2,1,0:T(2,128)}), f32[64,2,128]{2,1,0:T(2,128)S(1)}, u32[]{:S(2)}, u32[]{:S(2)}) async-start(f32[64,2,128]{2,1,0:T(2,128)} %bitcast.6), calls=%async_computation.1 | async-start | bytes 131072 | tf_op jit(solution)/shard_map/all_to_all | solution.py:353
  49.0 4.4 %collective-permute-start.2 = (f32[3,64,128]{2,1,0:T(8,128)S(1)}, f32[3,64,128]{2,1,0:T(8,128)S(1)}, u32[]{:S(2)}, u32[]{:S(2)}) collective-permute-start(f32[3,64,128]{2,1,0:T(8,128)S(1)} %get-tuple-element.19.lower), channel_id=1, source_target_pairs={{0,8},{8,16},{16,24},{24,32},{32,40},{40,48},{48,56},{56,64},{64,7... | collective-permute-start | bytes 294920 | tf_op jit(solution)/shard_map/ppermute | solution.py:349
  53.4 2.1 %collective-permute-start.3 = (f32[3,64,128]{2,1,0:T(8,128)S(1)}, f32[3,64,128]{2,1,0:T(8,128)S(1)}, u32[]{:S(2)}, u32[]{:S(2)}) collective-permute-start(f32[3,64,128]{2,1,0:T(8,128)S(1)} %get-tuple-element.20.upper), channel_id=1, source_target_pairs={{0,8},{8,16},{16,24},{24,32},{32,40},{40,48},{48,56},{56,64},{64,7... | collective-permute-start | bytes 294920 | tf_op jit(solution)/shard_map/ppermute | solution.py:350
  55.5 0.7 %collective-permute-done.2.lower_behind = f32[3,64,128]{2,1,0:T(8,128)S(1)} collective-permute-done((f32[3,64,128]{2,1,0:T(8,128)S(1)}, f32[3,64,128]{2,1,0:T(8,128)S(1)}, u32[]{:S(2)}, u32[]{:S(2)}) %collective-permute-start.2) | collective-permute-done | bytes 98336 | tf_op jit(solution)/shard_map/ppermute | solution.py:349
  56.1 1.1 %collective-permute-done.3.upper_behind = f32[3,64,128]{2,1,0:T(8,128)S(1)} collective-permute-done((f32[3,64,128]{2,1,0:T(8,128)S(1)}, f32[3,64,128]{2,1,0:T(8,128)S(1)}, u32[]{:S(2)}, u32[]{:S(2)}) %collective-permute-start.3) | collective-permute-done | bytes 98336 | tf_op jit(solution)/shard_map/ppermute | solution.py:350
  57.2 4.0 %all-to-all-done.1 = f32[64,2,128]{2,1,0:T(2,128)S(1)} async-done(((f32[64,2,128]{2,1,0:T(2,128)}), f32[64,2,128]{2,1,0:T(2,128)S(1)}, u32[]{:S(2)}, u32[]{:S(2)}) %all-to-all-start.1) | async-done | bytes 65568 | tf_op jit(solution)/shard_map/all_to_all | solution.py:353
  61.2 1.0 %shard_map.50 = f32[9,128,128]{2,1,0:T(8,128)} custom-call(f32[9,128,128]{2,1,0:T(8,128)S(1)} %bitcast.12, f32[3,128,128]{2,1,0:T(8,128)S(1)} %get-tuple-element.18.new1, f32[3,64,128]{2,1,0:T(8,128)S(1)} %get-tuple-element.19.lower, f32[3,64,128]{2,1,0:T(8,128)S(1)} %get-tuple-element.20.upper, f32[3,64,128]{2,1,0:T(8,128)S(1)} %collective-permute-done.2.lower_behind, ...), custom_call_target="tpu_custom_call" | custom-call | flops 1000000 | bytes 1000000 | tf_op jit(solution)/shard_map/pallas_call | solution.py:318
Async XLA Ops:
  0.0 6.7 %copy-start = (f32[1,3,3,8,16,128]{5,4,3,2,1,0:T(8,128)S(1)}, f32[1,3,3,8,16,128]{5,4,3,2,1,0:T(8,128)}, u32[]{:S(2)}) copy-start(f32[1,3,3,8,16,128]{5,4,3,2,1,0:T(8,128)} %param.4) | copy-start | bytes 1769476
  0.0 6.7 %copy-start.1 = (s32[8,16,128]{2,1,0:T(8,128)S(1)}, s32[8,16,128]{2,1,0:T(8,128)}, u32[]{:S(2)}) copy-start(s32[8,16,128]{2,1,0:T(8,128)} %param.5) | copy-start | bytes 196612
  0.0 6.7 %copy-start.2 = (f32[8,16,128]{2,1,0:T(8,128)S(1)}, f32[8,16,128]{2,1,0:T(8,128)}, u32[]{:S(2)}) copy-start(f32[8,16,128]{2,1,0:T(8,128)} %param.6) | copy-start | bytes 196612
  0.0 6.7 %copy-start.3 = (s32[8,16,128]{2,1,0:T(8,128)S(1)}, s32[8,16,128]{2,1,0:T(8,128)}, u32[]{:S(2)}) copy-start(s32[8,16,128]{2,1,0:T(8,128)} %param.7) | copy-start | bytes 196612
  1.4 6.6 %collective-permute-start = (f32[18,16,128]{2,1,0:T(8,128)S(1)}, f32[18,16,128]{2,1,0:T(8,128)S(1)}, u32[]{:S(2)}, u32[]{:S(2)}) collective-permute-start(f32[18,16,128]{2,1,0:T(8,128)S(1)} %get-tuple-element.16), channel_id=1, source_target_pairs={{0,1},{1,2},{2,3},{3,4},{4,5},{5,6},{6,7},{8,9},{9,10},{10,11},{11... | collective-permute-start | bytes 442376 | tf_op jit(solution)/shard_map/ppermute | solution.py:341
  4.5 8.4 %collective-permute-start.1 = (f32[18,16,128]{2,1,0:T(8,128)S(1)}, f32[18,16,128]{2,1,0:T(8,128)S(1)}, u32[]{:S(2)}, u32[]{:S(2)}) collective-permute-start(f32[18,16,128]{2,1,0:T(8,128)S(1)} %get-tuple-element.17), channel_id=1, source_target_pairs={{1,0},{2,1},{3,2},{4,3},{5,4},{6,5},{7,6},{9,8},{10,9},{11,10},{12... | collective-permute-start | bytes 442376 | tf_op jit(solution)/shard_map/ppermute | solution.py:342
  44.5 16.7 %all-to-all-start.1 = ((f32[64,2,128]{2,1,0:T(2,128)}), f32[64,2,128]{2,1,0:T(2,128)S(1)}, u32[]{:S(2)}, u32[]{:S(2)}) async-start(f32[64,2,128]{2,1,0:T(2,128)} %bitcast.6), calls=%async_computation.1 | async-start | bytes 131072 | tf_op jit(solution)/shard_map/all_to_all | solution.py:353
  49.0 7.2 %collective-permute-start.2 = (f32[3,64,128]{2,1,0:T(8,128)S(1)}, f32[3,64,128]{2,1,0:T(8,128)S(1)}, u32[]{:S(2)}, u32[]{:S(2)}) collective-permute-start(f32[3,64,128]{2,1,0:T(8,128)S(1)} %get-tuple-element.19.lower), channel_id=1, source_target_pairs={{0,8},{8,16},{16,24},{24,32},{32,40},{40,48},{48,56},{56,64},{64,7... | collective-permute-start | bytes 294920 | tf_op jit(solution)/shard_map/ppermute | solution.py:349
  53.4 3.8 %collective-permute-start.3 = (f32[3,64,128]{2,1,0:T(8,128)S(1)}, f32[3,64,128]{2,1,0:T(8,128)S(1)}, u32[]{:S(2)}, u32[]{:S(2)}) collective-permute-start(f32[3,64,128]{2,1,0:T(8,128)S(1)} %get-tuple-element.20.upper), channel_id=1, source_target_pairs={{0,8},{8,16},{16,24},{24,32},{32,40},{40,48},{48,56},{56,64},{64,7... | collective-permute-start | bytes 294920 | tf_op jit(solution)/shard_map/ppermute | solution.py:350

commit v4 on v3

--- a/solution.py
+++ b/solution.py
@@ -15,7 +15,7 @@
 Q3 = (DT / 6.0, DT * 2.0 / 3.0, DT / 6.0)
 ROWS = 16
 LANES = 128
-EDGE = 18
+EDGE = 15
 
 
 def combine(weights, states):
@@ -73,6 +73,15 @@
     return combine((Q2[0], Q2[1] - H, Q2[2]), [old[m][k] for m in range(3)])
 
 
+def rest_of(old, flows):
+    flow = combine((Q2[0], Q2[1] - H, Q2[2]), flows)
+    rest = []
+    for k in range(3):
+        decay = H * old[2][k] - combine(Q2, [old[m][k] for m in range(3)])
+        rest.append(SIGNS[k] * flow + RATES[k] * decay)
+    return rest
+
+
 def planes(lo, hi):
     return pl.ds(lo * ROWS, (hi - lo) * ROWS)
 
@@ -104,19 +113,27 @@
     mid = planes(1, 2)
     for side, out, edge in ((0, low_out, 0), (1, high_out, 2)):
         old = [[u[side, m * 3 + k, mid] for k in range(3)] for m in range(3)]
-        lap = []
+        w1 = [combine(Q1, [u[side, m * 3 + k] for m in range(3)]) for k in range(3)]
+        news = first_new(old, [laplace(v) for v in w1], *tables(side, 1 - side))
+        v2 = [H * news[k] + w2_of(old, k) for k in range(3)]
+        end = planes(edge, edge + 1)
+        old = [[u[side, m * 3 + k, end] for k in range(3)] for m in range(3)]
+        region, film, mobile = tables(side, side)
+        flows = [current(old[m], film) for m in range(3)]
+        w1_end = [combine(Q1, [old[m][k] for m in range(3)]) for k in range(3)]
+        lap = [w1[k][ROWS : 2 * ROWS] + shifted(w1_end[k]) - 6.0 * w1_end[k] for k in range(3)]
+        partial = first_new(old, lap, region, film, mobile)
+        rest = rest_of(old, flows)
         for k in range(3):
-            w1 = combine(Q1, [u[side, m * 3 + k] for m in range(3)])
-            out[9 + k] = w1[ROWS : 2 * ROWS]
-            lap.append(laplace(w1))
-        news = first_new(old, lap, *tables(side, 1 - side))
-        for k in range(3):
-            out[12 + k] = H * news[k] + w2_of(old, k)
-        end = planes(edge, edge + 1)
-        for i in range(9):
-            out[i] = u[side, i, end]
-        for i, table in enumerate(tables(side, side)):
-            out[15 + i] = table
+            w2 = w2_of(old, k)
+            inner = conduct(region, k) * (v2[k] + shifted(w2) - 6.0 * w2) + rest[k]
+            out[k] = w1_end[k]
+            out[3 + k] = w2
+            out[6 + k] = partial[k]
+            out[9 + k] = old[0][k] + mobile * inner * inverse(mobile, k)
+        out[12] = region
+        out[13] = film
+        out[14] = mobile
 
 
 def restrict(scratch, i, v):
@@ -138,13 +155,12 @@
         lap1.append(laplace(jnp.concatenate([zeros, w1, zeros], axis=0)))
     new1 = first_new(old, lap1, region, film, mobile)
     flows = [current(old[m], film) for m in range(3)]
-    flow2 = combine((Q2[0], Q2[1] - H, Q2[2]), flows)
+    rest = rest_of(old, flows)
     fine[12] = flows[0]
     for k in range(3):
         fine[k] = new1[k]
         fine[3 + k] = w2_of(old, k)
-        decay = H * old[2][k] - combine(Q2, [old[m][k] for m in range(3)])
-        fine[6 + k] = SIGNS[k] * flow2 + RATES[k] * decay
+        fine[6 + k] = rest[k]
     zero = [restrict(scratch, k, old[0][k]) for k in range(3)]
     cfilm = restrict(scratch, 3, film)
     cmobile = restrict(scratch, 4, mobile)
@@ -159,73 +175,62 @@
         coarse[5 + k] = zero[k]
 
 
-def outer_new1(near, side):
-    old = [[side[m * 3 + k] for k in range(3)] for m in range(3)]
-    lap = []
-    for k in range(3):
-        w1 = combine(Q1, [old[m][k] for m in range(3)])
-        lap.append(side[9 + k] + near[k] + shifted(w1) - 6.0 * w1)
-    return first_new(old, lap, side[15], side[16], side[17])
-
-
-def outer_rest(side):
-    old = [[side[m * 3 + k] for k in range(3)] for m in range(3)]
-    flow2 = combine((Q2[0], Q2[1] - H, Q2[2]), [current(old[m], side[16]) for m in range(3)])
-    rest = []
-    for k in range(3):
-        decay = H * old[2][k] - combine(Q2, [old[m][k] for m in range(3)])
-        rest.append(SIGNS[k] * flow2 + RATES[k] * decay)
-    return rest, [w2_of(old, k) for k in range(3)]
+def outer_plane(side, w1):
+    region, film, mobile = side[12], side[13], side[14]
+    gain = [mobile * inverse(mobile, k) for k in range(3)]
+    flow = [gain[k] * conduct(region, k) for k in range(3)]
+    new1 = [side[6 + k] + flow[k] * w1[k] for k in range(3)]
+    v2 = [H * new1[k] + side[3 + k] for k in range(3)]
+    return new1, v2, flow, gain, H * current(new1, film), mobile
+
+
+def outer_v3(side, outer, v2):
+    new1, _, flow, gain, cur, mobile = outer
+    v3 = []
+    for k in range(3):
+        spread = v2[k] + H * (shifted(new1[k]) - 6.0 * new1[k])
+        total = side[9 + k] + new1[k] * inverse(mobile, k) + flow[k] * spread + gain[k] * (SIGNS[k] * cur)
+        v3.append(Q3[0] * total + Q3[1] * new1[k])
+    return v3
 
 
 def main_kernel(u, regions, activity, dirichlet, fine, coarse, low, high, new1_out, lower_out, upper_out, payload, local, scratch):
-    def wrap(first, inside, last):
-        return jnp.concatenate([first, inside, last], axis=0)
-
-    own_region = regions[...].astype(jnp.float32)
-    own_mobile = 1.0 - dirichlet[...].astype(jnp.float32)
-    own_film = jnp.where(regions[...] == 0, activity[...], 0.0)
-    region = wrap(low[15], own_region, high[15])
-    film = wrap(low[16], own_film, high[16])
-    mobile = wrap(low[17], own_mobile, high[17])
+    region = regions[...].astype(jnp.float32)
+    mobile = 1.0 - dirichlet[...].astype(jnp.float32)
+    film = jnp.where(regions[...] == 0, activity[...], 0.0)
     first, last, between = slice(0, ROWS), slice(7 * ROWS, 8 * ROWS), slice(ROWS, 7 * ROWS)
-    below = outer_new1([fine[9 + k, planes(0, 1)] for k in range(3)], low)
-    above = outer_new1([fine[9 + k, planes(7, 8)] for k in range(3)], high)
-    low_rest, low_w2 = outer_rest(low)
-    high_rest, high_w2 = outer_rest(high)
-    new1, own1 = [], []
+    below = outer_plane(low, [fine[9 + k, planes(0, 1)] for k in range(3)])
+    above = outer_plane(high, [fine[9 + k, planes(7, 8)] for k in range(3)])
+    new1, v2 = [], []
     for k in range(3):
         v = fine[k]
         ends = []
         for at, side in ((first, low), (last, high)):
-            factor = own_mobile[at] * inverse(own_mobile[at], k) * conduct(own_region[at], k)
-            ends.append(v[at] + factor * combine(Q1, [side[m * 3 + k] for m in range(3)]))
+            factor = mobile[at] * inverse(mobile[at], k) * conduct(region[at], k)
+            ends.append(v[at] + factor * side[k])
         v = jnp.concatenate([ends[0], v[between], ends[1]], axis=0)
-        own1.append(v)
+        new1.append(v)
         new1_out[k] = v
-        new1.append(wrap(below[k], v, above[k]))
+        v2.append(H * v + fine[3 + k])
     flow1 = H * current(new1, film)
-    new2, own2 = [], []
-    for k in range(3):
-        w2 = wrap(low_w2[k], fine[3 + k], high_w2[k])
-        v2 = H * new1[k] + w2
-        lap2 = laplace(jnp.concatenate([low[12 + k], v2, high[12 + k]], axis=0))
-        rest = wrap(low_rest[k], fine[6 + k], high_rest[k])
-        inner = conduct(region, k) * lap2 + SIGNS[k] * flow1 + rest
+    new2 = []
+    for k in range(3):
+        lap2 = laplace(jnp.concatenate([below[1][k], v2[k], above[1][k]], axis=0))
+        inner = conduct(region, k) * lap2 + SIGNS[k] * flow1 + fine[6 + k]
         v = (new1[k] + mobile * inner) * inverse(mobile, k)
         new2.append(v)
-        own2.append(v[ROWS:-ROWS])
-        lower_out[k] = own2[k][: 4 * ROWS]
-        upper_out[k] = own2[k][4 * ROWS :]
-    flow3 = Q3[0] * fine[12] + (Q3[1] / H) * flow1[ROWS:-ROWS] + Q3[2] * current(own2, own_film)
+        lower_out[k] = v[: 4 * ROWS]
+        upper_out[k] = v[4 * ROWS :]
+    flow3 = Q3[0] * fine[12] + (Q3[1] / H) * flow1 + Q3[2] * current(new2, film)
+    v3_low = outer_v3(low, below, [v[first] for v in v2])
+    v3_high = outer_v3(high, above, [v[last] for v in v2])
     integral, one = [], []
     for k in range(3):
-        ends = [combine(Q3, [side[k], new1[k][at], new2[k][at]]) for side, at in ((low, slice(0, ROWS)), (high, slice(9 * ROWS, 10 * ROWS)))]
-        v3 = combine(Q3, [u[k], own1[k], own2[k]])
-        lap3 = laplace(wrap(ends[0], v3, ends[1]))
-        force = own_mobile * (conduct(own_region, k) * lap3 + SIGNS[k] * flow3 - RATES[k] * v3)
+        v3 = combine(Q3, [u[k], new1[k], new2[k]])
+        lap3 = laplace(jnp.concatenate([v3_low[k], v3, v3_high[k]], axis=0))
+        force = mobile * (conduct(region, k) * lap3 + SIGNS[k] * flow3 - RATES[k] * v3)
         integral.append(restrict(scratch, k, force))
-        one.append(restrict(scratch, 3 + k, own2[k]))
+        one.append(restrict(scratch, 3 + k, new2[k]))
     a, b, cmobile, cfilm = (coarse[i] for i in range(4))
     zero = [coarse[5 + k] for k in range(3)]
     slope = a * zero[0] + b * (zero[1] - 0.5 * zero[2])
@@ -252,26 +257,80 @@
         payload[pl.ds(3 + m, 32, stride=6)] = jnp.where(half, pltpu.roll(x, 64, 1), y)
 
 
-def scan_kernel(arrived, local, out, rolled, states):
+def scan_kernel(arrived, local, out, rolled, states, segments):
     me = lax.axis_index("tm")
     row = local[5, pl.ds(me // 2, 1)]
     cmobile = jnp.where(lax.rem(me, 2) == 0, row, pltpu.roll(row, 64, 1))
     keep = [1.0 / (1.0 + (DT * RATES[k]) * cmobile) for k in range(3)]
+    push = [keep[k] * SIGNS[k] for k in range(3)]
     rolled[...] = pltpu.roll(arrived[...], 64, 1)
-    v = [jnp.zeros((1, LANES), jnp.float32) for _ in range(3)]
-    for n in range(64):
+
+    def rows(ref, t, m):
+        return ref[pl.ds(3 * t + m, 8, stride=24)]
+
+    terms = [[rows(arrived, t, 0), rows(rolled, t, 0), rows(arrived, t, 1)] for t in range(8)]
+    terms = [[keep[k] * term[k] for k in range(3)] for term in terms]
+    slopes = [(rows(rolled, t, 1), rows(arrived, t, 2)) for t in range(8)]
+
+    def advance(t, v):
+        a, b = slopes[t]
+        slope = a * v[0] + b * (v[1] - 0.5 * v[2])
+        return [keep[k] * v[k] + push[k] * slope for k in range(3)]
+
+    a, b = slopes[0]
+    columns = [[push[k] * f for k in range(3)] for f in (a, b, -0.5 * b)]
+    for k in range(3):
+        columns[k][k] = columns[k][k] + keep[k]
+    part = terms[0]
+    for t in range(1, 8):
+        columns = [advance(t, column) for column in columns]
+        part = [x + y for x, y in zip(advance(t, part), terms[t])]
+    for k in range(3):
+        for m, column in enumerate((*columns, part)):
+            segments[4 * k + m] = column[k]
+    v = [segments[4 * k + 3, 0:1] for k in range(3)]
+    for k in range(3):
+        segments[12 + k, 0:1] = jnp.zeros_like(v[k])
+    for g in range(1, 8):
+        at = slice(g, g + 1)
         for k in range(3):
-            states[k, pl.ds(n, 1)] = v[k]
-        term = [arrived[pl.ds(3 * n, 1)], rolled[pl.ds(3 * n, 1)], arrived[pl.ds(3 * n + 1, 1)]]
-        a, b = rolled[pl.ds(3 * n + 1, 1)], arrived[pl.ds(3 * n + 2, 1)]
-        t = a * v[0] + b * (v[1] - 0.5 * v[2])
-        v = [keep[k] * (v[k] + term[k] + SIGNS[k] * t) for k in range(3)]
+            segments[12 + k, at] = v[k]
+        if g < 7:
+            moved = []
+            for k in range(3):
+                left = segments[4 * k, at] * v[0] + segments[4 * k + 1, at] * v[1]
+                moved.append(left + (segments[4 * k + 2, at] * v[2] + segments[4 * k + 3, at]))
+            v = moved
+    v = [segments[12 + k] for k in range(3)]
+    for t in range(8):
+        for k in range(3):
+            states[k, pl.ds(t, 8, stride=8)] = v[k]
+        if t < 7:
+            v = [x + y for x, y in zip(advance(t, v), terms[t])]
     half = lax.broadcasted_iota(jnp.int32, (64, LANES), 1) < 64
     out[pl.ds(0, 64, stride=2)] = jnp.where(half, states[0], pltpu.roll(states[1], 64, 1))
     out[pl.ds(1, 64, stride=2)] = states[2]
 
 
-def finish_kernel(u, new1, lower, upper, lower_behind, upper_behind, local, starts, far, out, scratch, sems):
+def prolong(scratch, i, v):
+    scratch[i, pl.ds(0, 32, stride=2)] = v
+    scratch[i, pl.ds(1, 32, stride=2)] = v
+    wide = scratch[i].reshape(4, 1, ROWS, LANES)
+    return jnp.broadcast_to(wide, (4, 2, ROWS, LANES)).reshape(8 * ROWS, LANES)
+
+
+def base_kernel(u, new1, lower, upper, lower_behind, upper_behind, local, out, scratch):
+    is_first = lax.axis_index("tm") == 0
+    for k in range(3):
+        new2 = jnp.concatenate([lower[k], upper[k]], axis=0)
+        head = jnp.where(is_first, u[k], jnp.concatenate([lower_behind[k], upper_behind[k]], axis=0))
+        zero, one = local[6 + k], local[9 + k]
+        out[k] = head - prolong(scratch, 3 * k, restrict(scratch, 9 + k, head))
+        out[3 + k] = new1[k] - prolong(scratch, 3 * k + 1, 0.5 * (zero + one))
+        out[6 + k] = new2 - prolong(scratch, 3 * k + 2, one)
+
+
+def finish_kernel(base, local, starts, far, out, scratch, sems):
     is_first = lax.axis_index("tm") == 0
     half = lax.broadcasted_iota(jnp.int32, (32, LANES), 1) < 64
     rows = [starts[pl.ds(i, 32, stride=4)] for i in range(4)]
@@ -282,31 +341,13 @@
     ]
     start = [jnp.where(is_first, local[6 + k], start[k]) for k in range(3)]
     t = local[3] * start[0] + local[4] * (start[1] - 0.5 * start[2])
-
-    def prolong(i, v):
-        scratch[i, pl.ds(0, 32, stride=2)] = v
-        scratch[i, pl.ds(1, 32, stride=2)] = v
-        wide = scratch[i].reshape(4, 1, ROWS, LANES)
-        return jnp.broadcast_to(wide, (4, 2, ROWS, LANES)).reshape(8 * ROWS, LANES)
-
     copies = []
     for k in range(3):
         end = (start[k] + local[k] + SIGNS[k] * t) / (1.0 + (DT * RATES[k]) * local[5])
-        delta_zero = start[k] - local[6 + k]
-        delta_one = end - local[9 + k]
-        new2 = jnp.concatenate([lower[k], upper[k]], axis=0)
-        head = jnp.where(is_first, u[k], jnp.concatenate([lower_behind[k], upper_behind[k]], axis=0))
-        pairs = head.reshape(4, 2, ROWS, LANES)
-        scratch[9 + k] = (pairs[:, 0] + pairs[:, 1]).reshape(4 * ROWS, LANES)
-        coarse = 0.25 * (scratch[9 + k, pl.ds(0, 32, stride=2)] + scratch[9 + k, pl.ds(1, 32, stride=2)])
-        parts = (
-            head + prolong(3 * k, start[k] - coarse),
-            new1[k] + prolong(3 * k + 1, 0.5 * (delta_zero + delta_one)),
-            new2 + prolong(3 * k + 2, delta_one),
-        )
-        for m in range(3):
-            out[3 * m + k] = parts[m]
-            copy = pltpu.make_async_copy(out.at[3 * m + k], far.at[3 * m + k], sems.at[3 * m + k])
+        for m, v in enumerate((start[k], 0.5 * (start[k] + end), end)):
+            i = 3 * m + k
+            out[i] = base[i] + prolong(scratch, i, v)
+            copy = pltpu.make_async_copy(out.at[i], far.at[i], sems.at[i])
             copy.start()
             copies.append(copy)
     for copy in copies:
@@ -349,10 +390,14 @@
     lower_behind = lax.ppermute(lower, "tm", nexts)
     upper_behind = lax.ppermute(upper, "tm", nexts)
     arrived = lax.all_to_all(payload.reshape(64, 1, 3 * LANES), "tm", 0, 0, tiled=True).reshape(192, LANES)
-    (starts,) = call(scan_kernel, [(128, LANES)], [f32(192, LANES), f32(3, 64, LANES)], arrived, local, cost=1000000)
+    scratch = [f32(192, LANES), f32(3, 64, LANES), f32(15, 8, LANES)]
+    (starts,) = call(scan_kernel, [(128, LANES)], scratch, arrived, local, cost=1000000)
+    whole, scratch = (9, 128, LANES), f32(12, 64, LANES)
+    fine_parts = (u, new1, lower, upper, lower_behind, upper_behind)
+    (base,) = call(base_kernel, [whole], [scratch], *fine_parts, local, cost=1000000)
     starts = lax.all_to_all(starts, "tm", 0, 0, tiled=True)
-    outs, scratch = (9, 128, LANES), [f32(9, 128, LANES), f32(12, 64, LANES), pltpu.SemaphoreType.DMA((9,))]
-    (out,) = call(finish_kernel, [outs], scratch, u, new1, lower, upper, lower_behind, upper_behind, local, starts, near_out=False, cost=1000000)
+    scratch = [f32(*whole), scratch, pltpu.SemaphoreType.DMA((9,))]
+    (out,) = call(finish_kernel, [whole], scratch, base, local, starts, near_out=False, cost=1000000)
     return out.reshape(fine_nodes.shape)
 
 

time: 62.5 us -> 61.8 us (0.989)
  waiting for transfers between devices: 11.5 us -> 10.7 us
    pallas_call x5 -> x6, Pallas kernels: 4.9 us -> 4.7 us  [call(): pl.pallas_call(kernel, out_shape=[jax.ShapeDtypeStruct(s, jnp.float32) fo...]
where the time goes in v4:
time: 61.8 us; the launch traced here: 61.5 us
  blocking collectives  29.8 us (48%)
  starting transfers between devices  16.2 us (26%)
  waiting for transfers between devices  10.7 us (17%)
  Pallas kernels  4.7 us (8%)
    all_to_all x1, blocking collectives, on_device(): lax.all_to_all(payload.reshape(64, 1, 3 * LANES), 'tm', 0, 0, tiled=True)  29.8 us
    ppermute x1, waiting for transfers between devices, on_device(): high = lax.ppermute(to_low, 'space', [(i + 1, i) for i in range(count - 1)])  4.78 us
    pallas_call x6, Pallas kernels, call(): pl.pallas_call(kernel, out_shape=[jax.ShapeDtypeStruct(s, jnp.float32) fo...  4.7 us
    ppermute x1, starting transfers between devices, on_device(): lower_behind = lax.ppermute(lower, 'tm', nexts)  4.45 us
    all_to_all x1, starting transfers between devices, on_device(): starts = lax.all_to_all(starts, 'tm', 0, 0, tiled=True)  4.44 us
    all_to_all x1, waiting for transfers between devices, on_device(): starts = lax.all_to_all(starts, 'tm', 0, 0, tiled=True)  3.95 us
    ppermute x1, starting transfers between devices, on_device(): low = lax.ppermute(to_high, 'space', [(i, i + 1) for i in range(count - 1)])  3.12 us
    ppermute x1, starting transfers between devices, on_device(): high = lax.ppermute(to_low, 'space', [(i + 1, i) for i in range(count - 1)])  2.16 us
  transfers between devices with their start and end apart: 5, of which 5 were waited for; matrix products, arithmetic and copies ran while one was open for 0% of the time, Pallas kernels for 1%

profile of v4, /device:TPU:7, one launch (start us, length us, event | category | flops | bytes accessed | tf_op | source)
XLA Modules:
  0.0 61.5 jit_solution(10355236173385647769)
XLA Ops:
  0.0 0.0 copy-start
  0.0 0.0 copy-start.1
  0.0 0.0 copy-start.2
  0.0 0.0 copy-start.3
  0.0 1.5 %shard_map.47 = (f32[15,16,128]{2,1,0:T(8,128)S(1)}, f32[15,16,128]{2,1,0:T(8,128)S(1)}) custom-call(f32[9,128,128]{2,1,0:T(8,128)} %bitcast.9, s32[128,128]{1,0:T(8,128)} %bitcast.13, f32[128,128]{1,0:T(8,128)} %bitcast.16, s32[128,128]{1,0:T(8,128)} %bitcast.19), custom_call_target="tpu_custom_call" | custom-call | flops 1000000 | bytes 1000000 | tf_op jit(solution)/shard_map/pallas_call | solution.py:359
  1.5 3.1 %collective-permute-start = (f32[15,16,128]{2,1,0:T(8,128)S(1)}, f32[15,16,128]{2,1,0:T(8,128)S(1)}, u32[]{:S(2)}, u32[]{:S(2)}) collective-permute-start(f32[15,16,128]{2,1,0:T(8,128)S(1)} %get-tuple-element.16), channel_id=1, source_target_pairs={{0,1},{1,2},{2,3},{3,4},{4,5},{5,6},{6,7},{8,9},{9,10},{10,11},{11... | collective-permute-start | bytes 368648 | tf_op jit(solution)/shard_map/ppermute | solution.py:382
  4.6 2.2 %collective-permute-start.1 = (f32[15,16,128]{2,1,0:T(8,128)S(1)}, f32[15,16,128]{2,1,0:T(8,128)S(1)}, u32[]{:S(2)}, u32[]{:S(2)}) collective-permute-start(f32[15,16,128]{2,1,0:T(8,128)S(1)} %get-tuple-element.17), channel_id=1, source_target_pairs={{1,0},{2,1},{3,2},{4,3},{5,4},{6,5},{7,6},{9,8},{10,9},{11,10},{12... | collective-permute-start | bytes 368648 | tf_op jit(solution)/shard_map/ppermute | solution.py:383
  6.8 0.0 copy-done
  6.8 0.0 copy-done.1
  6.8 0.0 copy-done.2
  6.8 0.0 copy-done.3
  6.9 0.5 shard_map.46
  7.3 0.3 collective-permute-done.low
  7.6 4.8 %collective-permute-done.1.high = f32[15,16,128]{2,1,0:T(8,128)S(1)} collective-permute-done((f32[15,16,128]{2,1,0:T(8,128)S(1)}, f32[15,16,128]{2,1,0:T(8,128)S(1)}, u32[]{:S(2)}, u32[]{:S(2)}) %collective-permute-start.1) | collective-permute-done | bytes 122912 | tf_op jit(solution)/shard_map/ppermute | solution.py:383
  12.4 0.7 %shard_map.48 = (f32[3,128,128]{2,1,0:T(8,128)S(1)}, f32[3,64,128]{2,1,0:T(8,128)S(1)}, f32[3,64,128]{2,1,0:T(8,128)S(1)}, f32[192,128]{1,0:T(8,128)S(1)}, f32[12,32,128]{2,1,0:T(8,128)S(1)}) custom-call(f32[9,128,128]{2,1,0:T(8,128)S(1)} %bitcast.11, s32[128,128]{1,0:T(8,128)S(1)} %bitcast.15, f32[128,128]{1,0:T(8,128)S(1)} %bitcast.18, ...), custom_call_target="tpu_custom_call" | custom-call | flops 3000000 | bytes 3000000 | tf_op jit(solution)/shard_map/pallas_call | solution.py:359
  13.1 29.8 %all_to_all.16 = f32[64,1,384]{2,1,0:T(1,128)S(1)} all-to-all(f32[64,1,384]{2,1,0:T(1,128)S(1)} %bitcast.24), channel_id=1, replica_groups=mesh['tm'=64,'space'=8] {'tm'}, dimensions={0} | all-to-all | bytes 196608 | tf_op jit(solution)/shard_map/all_to_all | solution.py:392
  42.8 1.0 %shard_map.50 = f32[128,128]{1,0:T(8,128)} custom-call(f32[192,128]{1,0:T(8,128)S(1)} %bitcast.22, f32[12,32,128]{2,1,0:T(8,128)S(1)} %get-tuple-element.21.local), custom_call_target="tpu_custom_call" | custom-call | flops 1000000 | bytes 1000000 | tf_op jit(solution)/shard_map/pallas_call | solution.py:359
  43.8 4.4 %all-to-all-start.1 = ((f32[64,2,128]{2,1,0:T(2,128)}), f32[64,2,128]{2,1,0:T(2,128)S(1)}, u32[]{:S(2)}, u32[]{:S(2)}) async-start(f32[64,2,128]{2,1,0:T(2,128)} %bitcast.6), calls=%async_computation.1 | async-start | bytes 131072 | tf_op jit(solution)/shard_map/all_to_all | solution.py:398
  48.2 4.4 %collective-permute-start.2 = (f32[3,64,128]{2,1,0:T(8,128)S(1)}, f32[3,64,128]{2,1,0:T(8,128)S(1)}, u32[]{:S(2)}, u32[]{:S(2)}) collective-permute-start(f32[3,64,128]{2,1,0:T(8,128)S(1)} %get-tuple-element.19.lower), channel_id=1, source_target_pairs={{0,8},{8,16},{16,24},{24,32},{32,40},{40,48},{48,56},{56,64},{64,7... | collective-permute-start | bytes 294920 | tf_op jit(solution)/shard_map/ppermute | solution.py:390
  52.7 2.1 %collective-permute-start.3 = (f32[3,64,128]{2,1,0:T(8,128)S(1)}, f32[3,64,128]{2,1,0:T(8,128)S(1)}, u32[]{:S(2)}, u32[]{:S(2)}) collective-permute-start(f32[3,64,128]{2,1,0:T(8,128)S(1)} %get-tuple-element.20.upper), channel_id=1, source_target_pairs={{0,8},{8,16},{16,24},{24,32},{32,40},{40,48},{48,56},{56,64},{64,7... | collective-permute-start | bytes 294920 | tf_op jit(solution)/shard_map/ppermute | solution.py:391
  54.8 0.7 %collective-permute-done.2.lower_behind = f32[3,64,128]{2,1,0:T(8,128)S(1)} collective-permute-done((f32[3,64,128]{2,1,0:T(8,128)S(1)}, f32[3,64,128]{2,1,0:T(8,128)S(1)}, u32[]{:S(2)}, u32[]{:S(2)}) %collective-permute-start.2) | collective-permute-done | bytes 98336 | tf_op jit(solution)/shard_map/ppermute | solution.py:390
  55.4 1.1 %collective-permute-done.3.upper_behind = f32[3,64,128]{2,1,0:T(8,128)S(1)} collective-permute-done((f32[3,64,128]{2,1,0:T(8,128)S(1)}, f32[3,64,128]{2,1,0:T(8,128)S(1)}, u32[]{:S(2)}, u32[]{:S(2)}) %collective-permute-start.3) | collective-permute-done | bytes 98336 | tf_op jit(solution)/shard_map/ppermute | solution.py:391
  56.5 0.1 shard_map.49.base
  56.6 3.9 %all-to-all-done.1 = f32[64,2,128]{2,1,0:T(2,128)S(1)} async-done(((f32[64,2,128]{2,1,0:T(2,128)}), f32[64,2,128]{2,1,0:T(2,128)S(1)}, u32[]{:S(2)}, u32[]{:S(2)}) %all-to-all-start.1) | async-done | bytes 65568 | tf_op jit(solution)/shard_map/all_to_all | solution.py:398
  60.5 1.0 %shard_map.51 = f32[9,128,128]{2,1,0:T(8,128)} custom-call(f32[9,128,128]{2,1,0:T(8,128)S(1)} %shard_map.49.base, f32[12,32,128]{2,1,0:T(8,128)S(1)} %get-tuple-element.21.local, f32[128,128]{1,0:T(8,128)S(1)} %bitcast.23), custom_call_target="tpu_custom_call" | custom-call | flops 1000000 | bytes 1000000 | tf_op jit(solution)/shard_map/pallas_call | solution.py:359
Async XLA Ops:
  0.0 6.8 %copy-start = (f32[1,3,3,8,16,128]{5,4,3,2,1,0:T(8,128)S(1)}, f32[1,3,3,8,16,128]{5,4,3,2,1,0:T(8,128)}, u32[]{:S(2)}) copy-start(f32[1,3,3,8,16,128]{5,4,3,2,1,0:T(8,128)} %param.4) | copy-start | bytes 1769476
  0.0 6.8 %copy-start.1 = (s32[8,16,128]{2,1,0:T(8,128)S(1)}, s32[8,16,128]{2,1,0:T(8,128)}, u32[]{:S(2)}) copy-start(s32[8,16,128]{2,1,0:T(8,128)} %param.5) | copy-start | bytes 196612
  0.0 6.8 %copy-start.2 = (f32[8,16,128]{2,1,0:T(8,128)S(1)}, f32[8,16,128]{2,1,0:T(8,128)}, u32[]{:S(2)}) copy-start(f32[8,16,128]{2,1,0:T(8,128)} %param.6) | copy-start | bytes 196612
  0.0 6.8 %copy-start.3 = (s32[8,16,128]{2,1,0:T(8,128)S(1)}, s32[8,16,128]{2,1,0:T(8,128)}, u32[]{:S(2)}) copy-start(s32[8,16,128]{2,1,0:T(8,128)} %param.7) | copy-start | bytes 196612
  1.5 6.1 %collective-permute-start = (f32[15,16,128]{2,1,0:T(8,128)S(1)}, f32[15,16,128]{2,1,0:T(8,128)S(1)}, u32[]{:S(2)}, u32[]{:S(2)}) collective-permute-start(f32[15,16,128]{2,1,0:T(8,128)S(1)} %get-tuple-element.16), channel_id=1, source_target_pairs={{0,1},{1,2},{2,3},{3,4},{4,5},{5,6},{6,7},{8,9},{9,10},{10,11},{11... | collective-permute-start | bytes 368648 | tf_op jit(solution)/shard_map/ppermute | solution.py:382
  4.6 7.7 %collective-permute-start.1 = (f32[15,16,128]{2,1,0:T(8,128)S(1)}, f32[15,16,128]{2,1,0:T(8,128)S(1)}, u32[]{:S(2)}, u32[]{:S(2)}) collective-permute-start(f32[15,16,128]{2,1,0:T(8,128)S(1)} %get-tuple-element.17), channel_id=1, source_target_pairs={{1,0},{2,1},{3,2},{4,3},{5,4},{6,5},{7,6},{9,8},{10,9},{11,10},{12... | collective-permute-start | bytes 368648 | tf_op jit(solution)/shard_map/ppermute | solution.py:383
  43.8 16.7 %all-to-all-start.1 = ((f32[64,2,128]{2,1,0:T(2,128)}), f32[64,2,128]{2,1,0:T(2,128)S(1)}, u32[]{:S(2)}, u32[]{:S(2)}) async-start(f32[64,2,128]{2,1,0:T(2,128)} %bitcast.6), calls=%async_computation.1 | async-start | bytes 131072 | tf_op jit(solution)/shard_map/all_to_all | solution.py:398
  48.2 7.2 %collective-permute-start.2 = (f32[3,64,128]{2,1,0:T(8,128)S(1)}, f32[3,64,128]{2,1,0:T(8,128)S(1)}, u32[]{:S(2)}, u32[]{:S(2)}) collective-permute-start(f32[3,64,128]{2,1,0:T(8,128)S(1)} %get-tuple-element.19.lower), channel_id=1, source_target_pairs={{0,8},{8,16},{16,24},{24,32},{32,40},{40,48},{48,56},{56,64},{64,7... | collective-permute-start | bytes 294920 | tf_op jit(solution)/shard_map/ppermute | solution.py:390
  52.7 3.8 %collective-permute-start.3 = (f32[3,64,128]{2,1,0:T(8,128)S(1)}, f32[3,64,128]{2,1,0:T(8,128)S(1)}, u32[]{:S(2)}, u32[]{:S(2)}) collective-permute-start(f32[3,64,128]{2,1,0:T(8,128)S(1)} %get-tuple-element.20.upper), channel_id=1, source_target_pairs={{0,8},{8,16},{16,24},{24,32},{32,40},{40,48},{48,56},{56,64},{64,7... | collective-permute-start | bytes 294920 | tf_op jit(solution)/shard_map/ppermute | solution.py:391

commit v5 on v4

--- a/solution.py
+++ b/solution.py
@@ -142,10 +142,14 @@
     return 0.25 * (scratch[i, pl.ds(0, 32, stride=2)] + scratch[i, pl.ds(1, 32, stride=2)])
 
 
-def inner_kernel(u, regions, activity, dirichlet, fine, coarse, scratch):
-    region = regions[...].astype(jnp.float32)
-    film = jnp.where(regions[...] == 0, activity[...], 0.0)
-    mobile = 1.0 - dirichlet[...].astype(jnp.float32)
+def inner_kernel(u_far, regions_far, activity_far, dirichlet_far, fine, coarse, scratch, u, ints, acts, sems):
+    copy_all([(u_far, u), (regions_far, ints.at[0]), (dirichlet_far, ints.at[1]), (activity_far, acts)], sems)
+    region = ints[0].astype(jnp.float32)
+    film = jnp.where(region == 0.0, acts[...], 0.0)
+    mobile = 1.0 - ints[1].astype(jnp.float32)
+    fine[13] = region
+    fine[14] = film
+    fine[15] = mobile
     old = [[u[m * 3 + k] for k in range(3)] for m in range(3)]
     zeros = jnp.zeros((ROWS, LANES), jnp.float32)
     lap1 = []
@@ -159,6 +163,7 @@
     fine[12] = flows[0]
     for k in range(3):
         fine[k] = new1[k]
+        fine[16 + k] = old[0][k]
         fine[3 + k] = w2_of(old, k)
         fine[6 + k] = rest[k]
     zero = [restrict(scratch, k, old[0][k]) for k in range(3)]
@@ -194,10 +199,8 @@
     return v3
 
 
-def main_kernel(u, regions, activity, dirichlet, fine, coarse, low, high, new1_out, lower_out, upper_out, payload, local, scratch):
-    region = regions[...].astype(jnp.float32)
-    mobile = 1.0 - dirichlet[...].astype(jnp.float32)
-    film = jnp.where(regions[...] == 0, activity[...], 0.0)
+def main_kernel(fine, coarse, low, high, new1_out, lower_out, upper_out, payload, local, scratch):
+    region, film, mobile = fine[13], fine[14], fine[15]
     first, last, between = slice(0, ROWS), slice(7 * ROWS, 8 * ROWS), slice(ROWS, 7 * ROWS)
     below = outer_plane(low, [fine[9 + k, planes(0, 1)] for k in range(3)])
     above = outer_plane(high, [fine[9 + k, planes(7, 8)] for k in range(3)])
@@ -226,7 +229,7 @@
     v3_high = outer_v3(high, above, [v[last] for v in v2])
     integral, one = [], []
     for k in range(3):
-        v3 = combine(Q3, [u[k], new1[k], new2[k]])
+        v3 = combine(Q3, [fine[16 + k], new1[k], new2[k]])
         lap3 = laplace(jnp.concatenate([v3_low[k], v3, v3_high[k]], axis=0))
         force = mobile * (conduct(region, k) * lap3 + SIGNS[k] * flow3 - RATES[k] * v3)
         integral.append(restrict(scratch, k, force))
@@ -319,11 +322,11 @@
     return jnp.broadcast_to(wide, (4, 2, ROWS, LANES)).reshape(8 * ROWS, LANES)
 
 
-def base_kernel(u, new1, lower, upper, lower_behind, upper_behind, local, out, scratch):
+def base_kernel(fine, new1, lower, upper, lower_behind, upper_behind, local, out, scratch):
     is_first = lax.axis_index("tm") == 0
     for k in range(3):
         new2 = jnp.concatenate([lower[k], upper[k]], axis=0)
-        head = jnp.where(is_first, u[k], jnp.concatenate([lower_behind[k], upper_behind[k]], axis=0))
+        head = jnp.where(is_first, fine[16 + k], jnp.concatenate([lower_behind[k], upper_behind[k]], axis=0))
         zero, one = local[6 + k], local[9 + k]
         out[k] = head - prolong(scratch, 3 * k, restrict(scratch, 9 + k, head))
         out[3 + k] = new1[k] - prolong(scratch, 3 * k + 1, 0.5 * (zero + one))
@@ -381,10 +384,11 @@
     count = lax.axis_size("space")
     low = lax.ppermute(to_high, "space", [(i, i + 1) for i in range(count - 1)])
     high = lax.ppermute(to_low, "space", [(i + 1, i) for i in range(count - 1)])
-    fine, coarse = call(inner_kernel, [(13, 128, LANES), (8, 32, LANES)], [f32(5, 64, LANES)], u, *tables, cost=3000000)
+    buffers = [f32(5, 64, LANES), f32(9, 128, LANES), pltpu.VMEM((2, 128, LANES), jnp.int32), f32(128, LANES), pltpu.SemaphoreType.DMA((4,))]
+    fine, coarse = call(inner_kernel, [(19, 128, LANES), (8, 32, LANES)], buffers, *pinned, near=False, cost=3000000)
     half = (3, 64, LANES)
     new1, lower, upper, payload, local = call(
-        main_kernel, [(3, 128, LANES), half, half, (192, LANES), (12, 32, LANES)], [f32(6, 64, LANES)], u, *tables, fine, coarse, low, high, cost=3000000
+        main_kernel, [(3, 128, LANES), half, half, (192, LANES), (12, 32, LANES)], [f32(6, 64, LANES)], fine, coarse, low, high, cost=3000000
     )
     nexts = [(i, i + 1) for i in range(lax.axis_size("tm") - 1)]
     lower_behind = lax.ppermute(lower, "tm", nexts)
@@ -393,7 +397,7 @@
     scratch = [f32(192, LANES), f32(3, 64, LANES), f32(15, 8, LANES)]
     (starts,) = call(scan_kernel, [(128, LANES)], scratch, arrived, local, cost=1000000)
     whole, scratch = (9, 128, LANES), f32(12, 64, LANES)
-    fine_parts = (u, new1, lower, upper, lower_behind, upper_behind)
+    fine_parts = (fine, new1, lower, upper, lower_behind, upper_behind)
     (base,) = call(base_kernel, [whole], [scratch], *fine_parts, local, cost=1000000)
     starts = lax.all_to_all(starts, "tm", 0, 0, tiled=True)
     scratch = [f32(*whole), scratch, pltpu.SemaphoreType.DMA((9,))]

time: 61.8 us -> 61.7 us (level)
  waiting for transfers between devices: 10.7 us -> 9.63 us
  Pallas kernels: 4.7 us -> 5.7 us
    pallas_call x6, Pallas kernels: 4.7 us -> 5.7 us  [call(): pl.pallas_call(kernel, out_shape=[jax.ShapeDtypeStruct(s, jnp.float32) fo...]
    ppermute x1, waiting for transfers between devices: 4.78 us -> 3.97 us  [on_device(): high = lax.ppermute(to_low, 'space', [(i + 1, i) for i in range(count - 1)])]
  transfers between devices with their start and end apart: 5 -> 5, of which waited for: 5 -> 4; matrix products, arithmetic and copies ran while one was open for 0% -> 0% of each run, Pallas kernels for 1% -> 3%
where the time goes in v5:
time: 61.7 us; the launch traced here: 61.4 us
  blocking collectives  29.8 us (48%)
  starting transfers between devices  16.2 us (26%)
  waiting for transfers between devices  9.63 us (16%)
  Pallas kernels  5.7 us (9%)
    all_to_all x1, blocking collectives, on_device(): lax.all_to_all(payload.reshape(64, 1, 3 * LANES), 'tm', 0, 0, tiled=True)  29.8 us
    pallas_call x6, Pallas kernels, call(): pl.pallas_call(kernel, out_shape=[jax.ShapeDtypeStruct(s, jnp.float32) fo...  5.7 us
    ppermute x1, starting transfers between devices, on_device(): lower_behind = lax.ppermute(lower, 'tm', nexts)  4.45 us
    all_to_all x1, starting transfers between devices, on_device(): starts = lax.all_to_all(starts, 'tm', 0, 0, tiled=True)  4.44 us
    ppermute x1, waiting for transfers between devices, on_device(): high = lax.ppermute(to_low, 'space', [(i + 1, i) for i in range(count - 1)])  3.97 us
    all_to_all x1, waiting for transfers between devices, on_device(): starts = lax.all_to_all(starts, 'tm', 0, 0, tiled=True)  3.95 us
    ppermute x1, starting transfers between devices, on_device(): low = lax.ppermute(to_high, 'space', [(i, i + 1) for i in range(count - 1)])  3.12 us
    ppermute x1, starting transfers between devices, on_device(): high = lax.ppermute(to_low, 'space', [(i + 1, i) for i in range(count - 1)])  2.16 us
  transfers between devices with their start and end apart: 5, of which 4 were waited for; matrix products, arithmetic and copies ran while one was open for 0% of the time, Pallas kernels for 3%

profile of v5, /device:TPU:7, one launch (start us, length us, event | category | flops | bytes accessed | tf_op | source)
XLA Modules:
  0.0 61.4 jit_solution(8161077323930178247)
XLA Ops:
  0.0 1.4 %shard_map.47 = (f32[15,16,128]{2,1,0:T(8,128)S(1)}, f32[15,16,128]{2,1,0:T(8,128)S(1)}) custom-call(f32[9,128,128]{2,1,0:T(8,128)} %bitcast.12, s32[128,128]{1,0:T(8,128)} %bitcast.14, f32[128,128]{1,0:T(8,128)} %bitcast.16, s32[128,128]{1,0:T(8,128)} %bitcast.18), custom_call_target="tpu_custom_call" | custom-call | flops 1000000 | bytes 1000000 | tf_op jit(solution)/shard_map/pallas_call | solution.py:362
  1.4 3.1 %collective-permute-start = (f32[15,16,128]{2,1,0:T(8,128)S(1)}, f32[15,16,128]{2,1,0:T(8,128)S(1)}, u32[]{:S(2)}, u32[]{:S(2)}) collective-permute-start(f32[15,16,128]{2,1,0:T(8,128)S(1)} %get-tuple-element.16), channel_id=1, source_target_pairs={{0,1},{1,2},{2,3},{3,4},{4,5},{5,6},{6,7},{8,9},{9,10},{10,11},{11... | collective-permute-start | bytes 368648 | tf_op jit(solution)/shard_map/ppermute | solution.py:385
  4.5 2.2 %collective-permute-start.1 = (f32[15,16,128]{2,1,0:T(8,128)S(1)}, f32[15,16,128]{2,1,0:T(8,128)S(1)}, u32[]{:S(2)}, u32[]{:S(2)}) collective-permute-start(f32[15,16,128]{2,1,0:T(8,128)S(1)} %get-tuple-element.17), channel_id=1, source_target_pairs={{1,0},{2,1},{3,2},{4,3},{5,4},{6,5},{7,6},{9,8},{10,9},{11,10},{12... | collective-permute-start | bytes 368648 | tf_op jit(solution)/shard_map/ppermute | solution.py:386
  6.7 1.6 %shard_map.46 = (f32[19,128,128]{2,1,0:T(8,128)S(1)}, f32[8,32,128]{2,1,0:T(8,128)S(1)}) custom-call(f32[9,128,128]{2,1,0:T(8,128)} %bitcast.13, s32[128,128]{1,0:T(8,128)} %bitcast.15, f32[128,128]{1,0:T(8,128)} %bitcast.17, s32[128,128]{1,0:T(8,128)} %bitcast.19), custom_call_target="tpu_custom_call" | custom-call | flops 3000000 | bytes 3000000 | tf_op jit(solution)/shard_map/pallas_call | solution.py:362
  8.3 0.0 collective-permute-done.low
  8.3 4.0 %collective-permute-done.1.high = f32[15,16,128]{2,1,0:T(8,128)S(1)} collective-permute-done((f32[15,16,128]{2,1,0:T(8,128)S(1)}, f32[15,16,128]{2,1,0:T(8,128)S(1)}, u32[]{:S(2)}, u32[]{:S(2)}) %collective-permute-start.1) | collective-permute-done | bytes 122912 | tf_op jit(solution)/shard_map/ppermute | solution.py:386
  12.3 0.7 %shard_map.48 = (f32[3,128,128]{2,1,0:T(8,128)S(1)}, f32[3,64,128]{2,1,0:T(8,128)S(1)}, f32[3,64,128]{2,1,0:T(8,128)S(1)}, f32[192,128]{1,0:T(8,128)S(1)}, f32[12,32,128]{2,1,0:T(8,128)S(1)}) custom-call(f32[19,128,128]{2,1,0:T(8,128)S(1)} %get-tuple-element.14.fine, f32[8,32,128]{2,1,0:T(8,128)S(1)} %get-tuple-element.15.coarse, ...), custom_call_target="tpu_custom_call" | custom-call | flops 3000000 | bytes 3000000 | tf_op jit(solution)/shard_map/pallas_call | solution.py:362
  12.9 29.8 %all_to_all.16 = f32[64,1,384]{2,1,0:T(1,128)S(1)} all-to-all(f32[64,1,384]{2,1,0:T(1,128)S(1)} %bitcast.11), channel_id=1, replica_groups=mesh['tm'=64,'space'=8] {'tm'}, dimensions={0} | all-to-all | bytes 196608 | tf_op jit(solution)/shard_map/all_to_all | solution.py:396
  42.7 1.0 %shard_map.50 = f32[128,128]{1,0:T(8,128)} custom-call(f32[192,128]{1,0:T(8,128)S(1)} %bitcast.9, f32[12,32,128]{2,1,0:T(8,128)S(1)} %get-tuple-element.21.local), custom_call_target="tpu_custom_call" | custom-call | flops 1000000 | bytes 1000000 | tf_op jit(solution)/shard_map/pallas_call | solution.py:362
  43.7 4.4 %all-to-all-start.1 = ((f32[64,2,128]{2,1,0:T(2,128)}), f32[64,2,128]{2,1,0:T(2,128)S(1)}, u32[]{:S(2)}, u32[]{:S(2)}) async-start(f32[64,2,128]{2,1,0:T(2,128)} %bitcast.6), calls=%async_computation.1 | async-start | bytes 131072 | tf_op jit(solution)/shard_map/all_to_all | solution.py:402
  48.1 4.4 %collective-permute-start.2 = (f32[3,64,128]{2,1,0:T(8,128)S(1)}, f32[3,64,128]{2,1,0:T(8,128)S(1)}, u32[]{:S(2)}, u32[]{:S(2)}) collective-permute-start(f32[3,64,128]{2,1,0:T(8,128)S(1)} %get-tuple-element.19.lower), channel_id=1, source_target_pairs={{0,8},{8,16},{16,24},{24,32},{32,40},{40,48},{48,56},{56,64},{64,7... | collective-permute-start | bytes 294920 | tf_op jit(solution)/shard_map/ppermute | solution.py:394
  52.6 2.1 %collective-permute-start.3 = (f32[3,64,128]{2,1,0:T(8,128)S(1)}, f32[3,64,128]{2,1,0:T(8,128)S(1)}, u32[]{:S(2)}, u32[]{:S(2)}) collective-permute-start(f32[3,64,128]{2,1,0:T(8,128)S(1)} %get-tuple-element.20.upper), channel_id=1, source_target_pairs={{0,8},{8,16},{16,24},{24,32},{32,40},{40,48},{48,56},{56,64},{64,7... | collective-permute-start | bytes 294920 | tf_op jit(solution)/shard_map/ppermute | solution.py:395
  54.6 0.7 %collective-permute-done.2.lower_behind = f32[3,64,128]{2,1,0:T(8,128)S(1)} collective-permute-done((f32[3,64,128]{2,1,0:T(8,128)S(1)}, f32[3,64,128]{2,1,0:T(8,128)S(1)}, u32[]{:S(2)}, u32[]{:S(2)}) %collective-permute-start.2) | collective-permute-done | bytes 98336 | tf_op jit(solution)/shard_map/ppermute | solution.py:394
  55.3 1.1 %collective-permute-done.3.upper_behind = f32[3,64,128]{2,1,0:T(8,128)S(1)} collective-permute-done((f32[3,64,128]{2,1,0:T(8,128)S(1)}, f32[3,64,128]{2,1,0:T(8,128)S(1)}, u32[]{:S(2)}, u32[]{:S(2)}) %collective-permute-start.3) | collective-permute-done | bytes 98336 | tf_op jit(solution)/shard_map/ppermute | solution.py:395
  56.4 0.1 shard_map.49.base
  56.5 3.9 %all-to-all-done.1 = f32[64,2,128]{2,1,0:T(2,128)S(1)} async-done(((f32[64,2,128]{2,1,0:T(2,128)}), f32[64,2,128]{2,1,0:T(2,128)S(1)}, u32[]{:S(2)}, u32[]{:S(2)}) %all-to-all-start.1) | async-done | bytes 65568 | tf_op jit(solution)/shard_map/all_to_all | solution.py:402
  60.4 1.0 %shard_map.51 = f32[9,128,128]{2,1,0:T(8,128)} custom-call(f32[9,128,128]{2,1,0:T(8,128)S(1)} %shard_map.49.base, f32[12,32,128]{2,1,0:T(8,128)S(1)} %get-tuple-element.21.local, f32[128,128]{1,0:T(8,128)S(1)} %bitcast.10), custom_call_target="tpu_custom_call" | custom-call | flops 1000000 | bytes 1000000 | tf_op jit(solution)/shard_map/pallas_call | solution.py:362
Async XLA Ops:
  1.4 6.9 %collective-permute-start = (f32[15,16,128]{2,1,0:T(8,128)S(1)}, f32[15,16,128]{2,1,0:T(8,128)S(1)}, u32[]{:S(2)}, u32[]{:S(2)}) collective-permute-start(f32[15,16,128]{2,1,0:T(8,128)S(1)} %get-tuple-element.16), channel_id=1, source_target_pairs={{0,1},{1,2},{2,3},{3,4},{4,5},{5,6},{6,7},{8,9},{9,10},{10,11},{11... | collective-permute-start | bytes 368648 | tf_op jit(solution)/shard_map/ppermute | solution.py:385
  4.5 7.7 %collective-permute-start.1 = (f32[15,16,128]{2,1,0:T(8,128)S(1)}, f32[15,16,128]{2,1,0:T(8,128)S(1)}, u32[]{:S(2)}, u32[]{:S(2)}) collective-permute-start(f32[15,16,128]{2,1,0:T(8,128)S(1)} %get-tuple-element.17), channel_id=1, source_target_pairs={{1,0},{2,1},{3,2},{4,3},{5,4},{6,5},{7,6},{9,8},{10,9},{11,10},{12... | collective-permute-start | bytes 368648 | tf_op jit(solution)/shard_map/ppermute | solution.py:386
  43.7 16.7 %all-to-all-start.1 = ((f32[64,2,128]{2,1,0:T(2,128)}), f32[64,2,128]{2,1,0:T(2,128)S(1)}, u32[]{:S(2)}, u32[]{:S(2)}) async-start(f32[64,2,128]{2,1,0:T(2,128)} %bitcast.6), calls=%async_computation.1 | async-start | bytes 131072 | tf_op jit(solution)/shard_map/all_to_all | solution.py:402
  48.1 7.2 %collective-permute-start.2 = (f32[3,64,128]{2,1,0:T(8,128)S(1)}, f32[3,64,128]{2,1,0:T(8,128)S(1)}, u32[]{:S(2)}, u32[]{:S(2)}) collective-permute-start(f32[3,64,128]{2,1,0:T(8,128)S(1)} %get-tuple-element.19.lower), channel_id=1, source_target_pairs={{0,8},{8,16},{16,24},{24,32},{32,40},{40,48},{48,56},{56,64},{64,7... | collective-permute-start | bytes 294920 | tf_op jit(solution)/shard_map/ppermute | solution.py:394
  52.6 3.8 %collective-permute-start.3 = (f32[3,64,128]{2,1,0:T(8,128)S(1)}, f32[3,64,128]{2,1,0:T(8,128)S(1)}, u32[]{:S(2)}, u32[]{:S(2)}) collective-permute-start(f32[3,64,128]{2,1,0:T(8,128)S(1)} %get-tuple-element.20.upper), channel_id=1, source_target_pairs={{0,8},{8,16},{16,24},{24,32},{32,40},{40,48},{48,56},{56,64},{64,7... | collective-permute-start | bytes 294920 | tf_op jit(solution)/shard_map/ppermute | solution.py:395
